TPU v7x, 512 devices: a whole 4x4x16 slice. The times are simulated.
512 devices in a mesh: probe: 16 (over y_hi, x, core), gx: 32 (over z, y_lo).
Axes of the slice: x: 4, y: 4 (y_hi: 2, y_lo: 2; y = y_hi * 2 + y_lo), z: 16, core: 2. Of those that a mesh axis runs over, the one named last changes fastest.
Arguments:
- wavefields: float32 [16, 2, 2, 768, 32, 128], P('probe', None, None, 'gx'), may hold values from -6 to 6
- stiffness: float32 [768, 32, 128], P('gx'), may hold values from 0.05 to 0.2
- buoyancy: float32 [768, 32, 128], P('gx'), may hold values from 0.5 to 1.5
- pert_stiffness: float32 [15, 8, 8, 8], replicated, may hold values from -0.3 to 0.3
- pert_buoyancy: float32 [15, 8, 8, 8], replicated, may hold values from -1.5 to 1.5
- xblock_index: int32 [15], replicated, may hold values from 0 to 95
- zblock_index: int32 [15], replicated, may hold values from 0 to 3
- yblock_index: int32 [15], replicated, may hold values from 0 to 15
- source_xcell: int32 [2], replicated, may hold values from 0 to 767
- source_zcell: int32 [2], replicated, may hold values from 0 to 31
- source_ycell: int32 [2], replicated, may hold values from 0 to 127
- wavelet: float32 [2, 2], replicated, may hold values from -4 to 4
Outputs:
- advanced: float32 [16, 2, 2, 768, 32, 128], P('probe', None, None, 'gx')
All inputs are finite; a program needn't handle non-finite values.
Results may differ from a plain program's by a relative error of at most 0.0003.
Values sent between devices are 32-bit elements; how exact they have to be, the bound alone decides.
No kernel may reach another device: no remote copies, remote signals or barrier semaphores. Data moves between devices by JAX's collectives and lax.ppermute only.
A program may use at most 64 MiB of HBM per device.

v0:
```python
import jax
import jax.numpy as jnp
from jax import lax
from jax.sharding import PartitionSpec as P

ITERS = 2


def with_halo(block, sides, width):
    for axis, dim in sides:
        count = lax.axis_size(axis)
        forward = [(i, i + 1) for i in range(count - 1)]
        backward = [(target, source) for source, target in forward]
        low = lax.ppermute(
            lax.slice_in_dim(block, block.shape[dim] - width, None, axis=dim), axis, forward
        )
        high = lax.ppermute(lax.slice_in_dim(block, 0, width, axis=dim), axis, backward)
        block = jnp.concatenate([low, block, high], axis=dim)
    return block


def from_root(block, axis, owner):
    block = jnp.where(lax.axis_index(axis) == owner, block, jnp.zeros_like(block))
    return lax.psum(block, axis)


def shifted(values, dimension, offset):
    selector = [slice(None)] * values.ndim
    for inner in range(values.ndim - 3, values.ndim):
        selector[inner] = slice(1, values.shape[inner] - 1)
    selector[dimension] = slice(1 + offset, values.shape[dimension] - 1 + offset)
    return values[tuple(selector)]


def stencil(padded, coefficient):
    centre = shifted(padded, padded.ndim - 1, 0)
    centre_c = shifted(coefficient, coefficient.ndim - 1, 0)
    summed = None
    for which in range(3):
        for offset in (1, -1):
            neighbour = shifted(padded, padded.ndim - 3 + which, offset)
            neighbour_c = shifted(coefficient, coefficient.ndim - 3 + which, offset)
            termed = 0.5 * (centre_c + neighbour_c) * (neighbour - centre)
            summed = termed if summed is None else summed + termed
    return summed


def padside(values):
    return jnp.pad(values, [(0, 0)] * (values.ndim - 2) + [(1, 1)] * 2)


def place_local(values, xstart, zstart, ystart, first_x, width_x, depth, across):
    edge = values.shape[0]
    offset_x = first_x + jnp.arange(width_x, dtype=jnp.int32) - xstart * edge
    offset_z = jnp.arange(depth, dtype=jnp.int32) - zstart * edge
    offset_y = jnp.arange(across, dtype=jnp.int32) - ystart * edge
    picked = jnp.take(values, jnp.clip(offset_x, 0, edge - 1), axis=0)
    picked = jnp.take(picked, jnp.clip(offset_z, 0, edge - 1), axis=1)
    picked = jnp.take(picked, jnp.clip(offset_y, 0, edge - 1), axis=2)
    inside_x = (offset_x >= 0) & (offset_x < edge)
    inside_z = (offset_z >= 0) & (offset_z < edge)
    inside_y = (offset_y >= 0) & (offset_y < edge)
    inside = inside_x[:, None, None] & inside_z[None, :, None] & inside_y[None, None, :]
    return jnp.where(inside, picked, 0.0)


def source_mask(first_x, width_x, depth, across, source_xcell, source_zcell, source_ycell):
    cells_x = first_x + jnp.arange(width_x, dtype=jnp.int32)
    cells_z = jnp.arange(depth, dtype=jnp.int32)
    cells_y = jnp.arange(across, dtype=jnp.int32)
    return (
        (cells_x[None, :, None, None] == source_xcell[:, None, None, None])
        & (cells_z[None, None, :, None] == source_zcell[:, None, None, None])
        & (cells_y[None, None, None, :] == source_ycell[:, None, None, None])
    )


def on_device(
    wavefields,
    stiffness,
    buoyancy,
    pert_stiffness,
    pert_buoyancy,
    xblock_index,
    zblock_index,
    yblock_index,
    source_xcell,
    source_zcell,
    source_ycell,
    wavelet,
):
    shots = wavefields.shape[1]
    width = wavefields.shape[3]
    depth = wavefields.shape[4]
    across = wavefields.shape[5]
    group_index = lax.axis_index("probe")
    background_group = group_index == 0
    probe_row = jnp.maximum(group_index - 1, 0)
    first_x = lax.axis_index("gx") * width
    xstart = lax.dynamic_index_in_dim(xblock_index, probe_row, 0, keepdims=False)
    zstart = lax.dynamic_index_in_dim(zblock_index, probe_row, 0, keepdims=False)
    ystart = lax.dynamic_index_in_dim(yblock_index, probe_row, 0, keepdims=False)
    stiff_values = lax.dynamic_index_in_dim(pert_stiffness, probe_row, 0, keepdims=False)
    buoy_values = lax.dynamic_index_in_dim(pert_buoyancy, probe_row, 0, keepdims=False)
    coeff_ext = with_halo(jnp.stack([stiffness, buoyancy], 0), (("gx", 1),), ITERS)
    stiff_block = place_local(stiff_values, xstart, zstart, ystart, first_x, width, depth, across)
    buoy_block = place_local(
        buoy_values, xstart, zstart, ystart, first_x - 1, width + 2, depth, across
    )
    block_padded = padside(buoy_block)
    buoy_padded = padside(coeff_ext[1, ITERS - 1 : ITERS + 1 + width])
    source_hit = source_mask(
        first_x, width, depth, across, source_xcell, source_zcell, source_ycell
    )
    earlier = wavefields[0, :, 0]
    present = wavefields[0, :, 1]
    for instant in range(ITERS):
        back_present = from_root(present, "probe", 0)
        joined = jnp.concatenate([present, back_present], 0)
        extended = with_halo(joined, (("gx", 1),), 1)
        padded = padside(extended)
        laplace = stencil(padded, buoy_padded)
        laplace_own = laplace[:shots]
        laplace_back = laplace[shots:]
        born_term = stiff_block * laplace_back + stiffness * stencil(padded[shots:], block_padded)
        injected = jnp.where(source_hit, wavelet[:, instant][:, None, None, None], 0.0)
        forcing = jnp.where(background_group, injected, born_term)
        upcoming = 2.0 * present - earlier + stiffness * laplace_own + forcing
        earlier, present = (present, upcoming)
    return jnp.stack([earlier, present], 1)[None]


def solution(mesh):
    placed = (
        P("probe", None, None, "gx", None, None),
        P("gx", None, None),
        P("gx", None, None),
        P(),
        P(),
        P(),
        P(),
        P(),
        P(),
        P(),
        P(),
        P(),
    )
    return jax.shard_map(
        on_device,
        mesh=mesh,
        in_specs=placed,
        out_specs=P("probe", None, None, "gx", None, None),
        check_vma=False,
    )
```

profile of v0, /device:TPU:24, one launch (start us, length us, event | category | flops | bytes accessed | tf_op | source)
XLA Modules:
  0.0 369.8 jit_solution(13215306612799961780)
XLA Ops:
  6.6 2.2 broadcast_select_fusion.1
  9.5 2.6 collective-permute-start
  12.2 4.1 %collective-permute-start.2 = (f32[2,2,32,128]{3,2,1,0:T(8,128)}, f32[2,2,32,128]{3,2,1,0:T(8,128)}, u32[]{:S(2)}, u32[]{:S(2)}) collective-permute-start(f32[2,2,32,128]{3,2,1,0:T(8,128)} %get-tuple-element.23), channel_id=1, source_target_pairs={{0,1},{1,2},{2,3},{3,4},{4,5},{5,6},{6,7},{7,8},{8,9},{9,10},{10,1... | collective-permute-start | bytes 196616 | tf_op jit(solution)/shard_map/ppermute | solution.py:14
  24.1 1.8 copy.114
  29.3 1.2 copy.110
  31.4 1.2 bitcast_select_fusion.1
  33.5 1.7 fusion.76
  35.8 1.5 fusion.58
  37.3 131.7 %all-reduce.7.cloned.1.call-done = f32[2,24,32,128]{3,2,1,0:T(8,128)} async-done(((f32[2,24,32,128]{3,2,1,0:T(8,128)}), f32[2,24,32,128]{3,2,1,0:T(8,128)}) %all-reduce.7.cloned.1.call-update) | async-done | bytes 786448 | tf_op jit(solution)/shard_map/psum | solution.py:24
  169.9 2.7 collective-permute-start.1
  172.7 4.1 %collective-permute-start.3 = (f32[4,1,32,128]{3,2,1,0:T(8,128)S(1)}, f32[4,1,32,128]{3,2,1,0:T(8,128)S(1)}, u32[]{:S(2)}, u32[]{:S(2)}) collective-permute-start(f32[4,1,32,128]{3,2,1,0:T(8,128)S(1)} %get-tuple-element.15), channel_id=1, source_target_pairs={{0,1},{1,2},{2,3},{3,4},{4,5},{5,6},{6,7},{7,8},{8,9},{9,10},{10,1... | collective-permute-start | bytes 196616 | tf_op jit(solution)/shard_map/ppermute | solution.py:14
  176.8 1.1 fusion.82
  178.0 1.0 collective-permute-done.3
  179.4 3.0 select_maximum_fusion.3
  182.6 1.8 fusion.15
  184.4 2.8 broadcast_select_fusion
  187.2 157.3 %all-reduce.9.cloned.1.call-done = f32[2,24,32,128]{3,2,1,0:T(8,128)} async-done(((f32[2,24,32,128]{3,2,1,0:T(8,128)}), f32[2,24,32,128]{3,2,1,0:T(8,128)}) %all-reduce.9.cloned.1.call-update) | async-done | bytes 786448 | tf_op jit(solution)/shard_map/psum | solution.py:24
  345.4 2.7 collective-permute-start.4
  348.2 4.2 %collective-permute-start.5 = (f32[4,1,32,128]{3,2,1,0:T(8,128)S(1)}, f32[4,1,32,128]{3,2,1,0:T(8,128)S(1)}, u32[]{:S(2)}, u32[]{:S(2)}) collective-permute-start(f32[4,1,32,128]{3,2,1,0:T(8,128)S(1)} %get-tuple-element.11), channel_id=1, source_target_pairs={{0,1},{1,2},{2,3},{3,4},{4,5},{5,6},{6,7},{7,8},{8,9},{9,10},{10,1... | collective-permute-start | bytes 196616 | tf_op jit(solution)/shard_map/ppermute | solution.py:14
  352.5 1.8 collective-permute-done.5
  354.8 3.0 select_maximum_fusion
  357.9 1.8 fusion.4
  359.8 1.9 fusion.29
  361.7 1.3 maximum_bitcast_fusion
  (139 shorter events, 14.9 us)
Async XLA Ops:
  6.5 162.5 %all-reduce.7.cloned.1.call-start = ((), (), s32[]{:S(2)}) async-start(), calls=%async_computation | async-start | bytes 1572864 | tf_op jit(solution)/shard_map/psum | solution.py:24
  6.5 9.7 %copy-start.38 = (s32[15]{0:T(128)S(1)}, s32[15]{0:T(128)}, u32[]{:S(2)}) copy-start(s32[15]{0:T(128)} %param.17) | copy-start | bytes 184
  6.5 11.1 %copy-start.39 = (s32[15]{0:T(128)S(1)}, s32[15]{0:T(128)}, u32[]{:S(2)}) copy-start(s32[15]{0:T(128)} %param.18) | copy-start | bytes 184
  6.5 12.5 %copy-start.40 = (s32[15]{0:T(128)S(1)}, s32[15]{0:T(128)}, u32[]{:S(2)}) copy-start(s32[15]{0:T(128)} %param.19) | copy-start | bytes 184
  6.6 14.4 %copy-start.34 = (f32[15,8,8,8]{0,3,2,1:T(8,128)S(1)}, f32[15,8,8,8]{0,3,2,1:T(8,128)}, u32[]{:S(2)}) copy-start(f32[15,8,8,8]{0,3,2,1:T(8,128)} %param.16) | copy-start | bytes 92164
  6.6 14.4 %copy-start.35 = (f32[15,8,8,8]{0,3,2,1:T(8,128)S(1)}, f32[15,8,8,8]{0,3,2,1:T(8,128)}, u32[]{:S(2)}) copy-start(f32[15,8,8,8]{0,3,2,1:T(8,128)} %param.15) | copy-start | bytes 92164
  8.8 335.8 %all-reduce.9.cloned.1.call-start = ((), (), s32[]{:S(2)}) async-start(), calls=%async_computation.1 | async-start | bytes 1572864 | tf_op jit(solution)/shard_map/psum | solution.py:24
  9.5 26.3 %collective-permute-start = (f32[2,2,32,128]{3,2,1,0:T(8,128)}, f32[2,2,32,128]{3,2,1,0:T(8,128)}, u32[]{:S(2)}, u32[]{:S(2)}) collective-permute-start(f32[2,2,32,128]{3,2,1,0:T(8,128)} %get-tuple-element.24), channel_id=1, source_target_pairs={{1,0},{2,1},{3,2},{4,3},{5,4},{6,5},{7,6},{8,7},{9,8},{10,9},{11,1... | collective-permute-start | bytes 196616 | tf_op jit(solution)/shard_map/ppermute | solution.py:17
  12.2 23.6 %collective-permute-start.2 = (f32[2,2,32,128]{3,2,1,0:T(8,128)}, f32[2,2,32,128]{3,2,1,0:T(8,128)}, u32[]{:S(2)}, u32[]{:S(2)}) collective-permute-start(f32[2,2,32,128]{3,2,1,0:T(8,128)} %get-tuple-element.23), channel_id=1, source_target_pairs={{0,1},{1,2},{2,3},{3,4},{4,5},{5,6},{6,7},{7,8},{8,9},{9,10},{10,1... | collective-permute-start | bytes 196616 | tf_op jit(solution)/shard_map/ppermute | solution.py:14
  29.3 4.0 %copy-start.3 = (f32[1,2,2,24,32,128]{5,4,3,2,1,0:T(8,128)S(1)}, f32[1,2,2,24,32,128]{5,4,3,2,1,0:T(8,128)}, u32[]{:S(2)}) copy-start(f32[1,2,2,24,32,128]{5,4,3,2,1,0:T(8,128)} %param.12) | copy-start | bytes 4718596
  35.1 141.7 %copy-start.6 = (f32[24,32,128]{2,1,0:T(8,128)S(1)}, f32[24,32,128]{2,1,0:T(8,128)}, u32[]{:S(2)}) copy-start(f32[24,32,128]{2,1,0:T(8,128)} %param.14) | copy-start | bytes 1179652
  169.1 7.8 %copy-start.33 = (f32[26,32,128]{2,1,0:T(8,128)S(1)}, f32[26,32,128]{2,1,0:T(8,128)}, u32[]{:S(2)}) copy-start(f32[26,32,128]{2,1,0:T(8,128)} %fusion.58) | copy-start | bytes 1277956
  169.9 8.1 %collective-permute-start.1 = (f32[4,1,32,128]{3,2,1,0:T(8,128)S(1)}, f32[4,1,32,128]{3,2,1,0:T(8,128)S(1)}, u32[]{:S(2)}, u32[]{:S(2)}) collective-permute-start(f32[4,1,32,128]{3,2,1,0:T(8,128)S(1)} %get-tuple-element.16), channel_id=1, source_target_pairs={{1,0},{2,1},{3,2},{4,3},{5,4},{6,5},{7,6},{8,7},{9,8},{10,9},{11,1... | collective-permute-start | bytes 196616 | tf_op jit(solution)/shard_map/ppermute | solution.py:17
  172.7 6.3 %copy-start = (f32[2,24,32,128]{3,2,1,0:T(8,128)S(1)}, f32[2,24,32,128]{3,2,1,0:T(8,128)}, u32[]{:S(2)}) copy-start(f32[2,24,32,128]{3,2,1,0:T(8,128)} %all-reduce.7.cloned.1.call-done) | copy-start | bytes 2359300
  172.7 6.3 %collective-permute-start.3 = (f32[4,1,32,128]{3,2,1,0:T(8,128)S(1)}, f32[4,1,32,128]{3,2,1,0:T(8,128)S(1)}, u32[]{:S(2)}, u32[]{:S(2)}) collective-permute-start(f32[4,1,32,128]{3,2,1,0:T(8,128)S(1)} %get-tuple-element.15), channel_id=1, source_target_pairs={{0,1},{1,2},{2,3},{3,4},{4,5},{5,6},{6,7},{7,8},{8,9},{9,10},{10,1... | collective-permute-start | bytes 196616 | tf_op jit(solution)/shard_map/ppermute | solution.py:14
  177.9 4.5 %copy-start.21 = (f32[24,32,128]{2,1,0:T(8,128)}, f32[24,32,128]{2,1,0:T(8,128)S(1)}, u32[]{:S(2)}) copy-start(f32[24,32,128]{2,1,0:T(8,128)S(1)} %get-tuple-element.17) | copy-start | bytes 1179652
  177.9 4.5 %copy-start.23 = (f32[24,32,128]{2,1,0:T(8,128)}, f32[24,32,128]{2,1,0:T(8,128)S(1)}, u32[]{:S(2)}) copy-start(f32[24,32,128]{2,1,0:T(8,128)S(1)} %get-tuple-element.18) | copy-start | bytes 1179652
  177.9 4.5 %copy-start.25 = (f32[24,32,128]{2,1,0:T(8,128)}, f32[24,32,128]{2,1,0:T(8,128)S(1)}, u32[]{:S(2)}) copy-start(f32[24,32,128]{2,1,0:T(8,128)S(1)} %get-tuple-element.31) | copy-start | bytes 1179652
  177.9 4.5 %copy-start.27 = (f32[24,32,128]{2,1,0:T(8,128)}, f32[24,32,128]{2,1,0:T(8,128)S(1)}, u32[]{:S(2)}) copy-start(f32[24,32,128]{2,1,0:T(8,128)S(1)} %get-tuple-element.32) | copy-start | bytes 1179652
  178.0 4.5 %copy-start.29 = (f32[24,32,128]{2,1,0:T(8,128)}, f32[24,32,128]{2,1,0:T(8,128)S(1)}, u32[]{:S(2)}) copy-start(f32[24,32,128]{2,1,0:T(8,128)S(1)} %get-tuple-element.33) | copy-start | bytes 1179652
  178.0 4.5 %copy-start.31 = (f32[24,32,128]{2,1,0:T(8,128)}, f32[24,32,128]{2,1,0:T(8,128)S(1)}, u32[]{:S(2)}) copy-start(f32[24,32,128]{2,1,0:T(8,128)S(1)} %get-tuple-element.34) | copy-start | bytes 1179652
  344.5 9.8 %copy-start.1 = (f32[2,24,32,128]{3,2,1,0:T(8,128)S(1)}, f32[2,24,32,128]{3,2,1,0:T(8,128)}, u32[]{:S(2)}) copy-start(f32[2,24,32,128]{3,2,1,0:T(8,128)} %all-reduce.9.cloned.1.call-done) | copy-start | bytes 2359300
  345.4 7.1 %collective-permute-start.4 = (f32[4,1,32,128]{3,2,1,0:T(8,128)S(1)}, f32[4,1,32,128]{3,2,1,0:T(8,128)S(1)}, u32[]{:S(2)}, u32[]{:S(2)}) collective-permute-start(f32[4,1,32,128]{3,2,1,0:T(8,128)S(1)} %get-tuple-element.12), channel_id=1, source_target_pairs={{1,0},{2,1},{3,2},{4,3},{5,4},{6,5},{7,6},{8,7},{9,8},{10,9},{11,1... | collective-permute-start | bytes 196616 | tf_op jit(solution)/shard_map/ppermute | solution.py:17
  348.2 6.2 %collective-permute-start.5 = (f32[4,1,32,128]{3,2,1,0:T(8,128)S(1)}, f32[4,1,32,128]{3,2,1,0:T(8,128)S(1)}, u32[]{:S(2)}, u32[]{:S(2)}) collective-permute-start(f32[4,1,32,128]{3,2,1,0:T(8,128)S(1)} %get-tuple-element.11), channel_id=1, source_target_pairs={{0,1},{1,2},{2,3},{3,4},{4,5},{5,6},{6,7},{7,8},{8,9},{9,10},{10,1... | collective-permute-start | bytes 196616 | tf_op jit(solution)/shard_map/ppermute | solution.py:14
  (26 other events, 56.3 us)
Sparse Core Ops, SparseCore 0:
  10.3 158.7 all-reduce.6
  187.3 157.1 all-reduce.8
where the time goes:
time: 372 us; the launch traced here: 370 us
  waiting for transfers between devices  292 us (78%)
  other arithmetic  29.5 us (8%)
  starting transfers between devices  20.6 us (6%)
  between operations  16.3 us (4%)
  local copies, waits for them, and re-layouts  11.4 us (3%)
    psum x2, waiting for transfers between devices, from_root(): return lax.psum(block, axis)  289 us
    ppermute x3, starting transfers between devices, with_halo(): lax.ppermute(lax.slice_in_dim(block, block.shape[dim] - width, None, axis...  12.4 us
    ppermute x3, starting transfers between devices, with_halo(): lax.ppermute(lax.slice_in_dim(block, 0, width, axis=dim), axis, backward)  8.12 us
  transfers between devices with their start and end apart: 8, of which 5 were waited for; matrix products, arithmetic and copies ran while one was open for 6% of the time, Pallas kernels for 0%

commit v1 on v0

v1 whole, which is shorter than its diff:
```python
import functools

import jax
import jax.numpy as jnp
from jax import lax
from jax.experimental import pallas as pl
from jax.experimental.pallas import tpu as pltpu
from jax.sharding import PartitionSpec as P

EDGE = 8
SPAN = EDGE + 4
PER_ROW = 10
STRIPS = [(s, 1, i) for s in range(2) for i in range(SPAN)] + [
    (s, 0, i) for s in range(2) for i in range(1, SPAN - 1)
]
PIECE = (64, 128)

FIRST = (1, 2, 6)
NEXT = ((9, 3, 7, 5), (10, 4, 12), (14, 15))
DIRECT = (8, 11, 13)

ANY = pl.BlockSpec(memory_space=pl.ANY)
SMEM = pl.BlockSpec(memory_space=pltpu.SMEM)
PARAMS = pltpu.CompilerParams(vmem_limit_bytes=32 * 1024 * 1024)


def copy_all(pairs, sems):
    copies = [pltpu.make_async_copy(a, b, sems.at[n]) for n, (a, b) in enumerate(pairs)]
    for copy in copies:
        copy.start()
    return copies


def wait_all(copies):
    for copy in copies:
        copy.wait()


def wrapped(shift):
    return jnp.bitwise_and(shift + 128, 127)


def split_kernel(
    width, xb, zb, yb, wave, stiff, buoy, low, high, p0, p1, p2, d0, d1, d2, slab, packed, sem, sem_slab, sem_out
):
    first = lax.axis_index("gx") * width
    edges = []
    for out, outer, inner in ((low, 0, 0), (high, width - 1, width - 2)):
        for s in range(2):
            edges.append((wave.at[s, 1, pl.ds(inner, 2)], out.at[pl.ds(2 * s, 2)]))
            edges.append((wave.at[s, 0, outer], out.at[4 + s]))
        edges.append((buoy.at[pl.ds(inner, 2)], out.at[pl.ds(6, 2)]))
        edges.append((stiff.at[outer], out.at[8]))
    edges = copy_all(edges, sem)

    def start_of(g):
        return xb[g] * EDGE - 2 - first

    def touches(g):
        x0 = start_of(g)
        return (x0 < width) & (x0 + SPAN > 0)

    def some(g, found):
        return found | touches(g).astype(jnp.int32)

    needed = lax.fori_loop(0, 15, some, jnp.int32(0))

    @pl.when((lax.axis_index("probe") == 0) & (needed > 0))
    def _():
        load = pltpu.make_async_copy(wave, slab.at[:, :, :, pl.ds(8, 32)], sem_slab)
        load.start()
        load.wait()
        lane = lax.broadcasted_iota(jnp.int32, (16, 128), 1)

        def one(g, at):
            x0 = start_of(g)
            r0 = zb[g] * EDGE + 6
            y0 = yb[g] * EDGE - 2
            for k in range(0, len(STRIPS), PER_ROW):
                row = jnp.zeros((16, 128), jnp.float32)
                for q, (s, t, i) in enumerate(STRIPS[k : k + PER_ROW]):
                    plane = jnp.clip(x0 + i, 0, width - 1)
                    values = slab[s, t, plane, pl.ds(r0, 16), :]
                    values = pltpu.roll(values, wrapped(SPAN * q - y0), 1)
                    row = jnp.where((lane >= SPAN * q) & (lane < SPAN * (q + 1)), values, row)
                packed[at, pl.ds(k // PER_ROW * SPAN, 16), :] = row

        at = 0
        spots = []
        for head, rest in zip(FIRST, NEXT):
            spots += [head, *rest]
        spots += DIRECT
        for at, probe in enumerate(spots):

            @pl.when(touches(probe - 1))
            def _():
                one(probe - 1, at)

        outs, at = [], 0
        for out, rest in zip((p0, p1, p2), NEXT):
            outs.append((packed.at[pl.ds(at, 1 + len(rest))], out))
            at += 1 + len(rest)
        for out in (d0, d1, d2):
            outs.append((packed.at[at], out))
            at += 1
        wait_all(copy_all(outs, sem_out))

    wait_all(edges)


def pass_kernel(r0, r1, r2, q0, q1, q2, q3, sem):
    row = lax.axis_index("probe")
    for head, rest, got in zip(FIRST, NEXT, (r0, r1, r2)):

        @pl.when(row == head)
        def _():
            pairs = [(got.at[1 + n], out) for n, out in zip(range(len(rest)), (q0, q1, q2, q3))]
            wait_all(copy_all(pairs, sem))


def pick_kernel(r0, r1, r2, d0, d1, d2, q0, q1, q2, q3, out, sem):
    row = lax.axis_index("probe")

    def bring(where, source):
        @pl.when(where)
        def _():
            copy = pltpu.make_async_copy(source, out, sem)
            copy.start()
            copy.wait()

    for head, got in zip(FIRST, (r0, r1, r2)):
        bring(row == head, got.at[0])
    for target, got in zip(DIRECT, (d0, d1, d2)):
        bring(row == target, got)
    for n, got in enumerate((q0, q1, q2, q3)):
        where = row < 0
        for rest in NEXT:
            if n < len(rest):
                where = where | (row == rest[n])
        bring(where, got)


def march_kernel(
    width, sx, sz, sy, wavelet, wave, stiff, buoy, below, above, out, pres, prev, cext, kext, mid, o1, o2, sem, sem_out
):
    rows = pl.ds(8, 32)
    loads = []
    for s in range(2):
        loads.append((wave.at[s, 1], pres.at[s, pl.ds(2, width), rows]))
        loads.append((below.at[pl.ds(2 * s, 2)], pres.at[s, pl.ds(0, 2), rows]))
        loads.append((above.at[pl.ds(2 * s, 2)], pres.at[s, pl.ds(width + 2, 2), rows]))
        loads.append((wave.at[s, 0], prev.at[s, pl.ds(1, width)]))
        loads.append((below.at[4 + s], prev.at[s, 0]))
        loads.append((above.at[4 + s], prev.at[s, width + 1]))
    loads.append((buoy, cext.at[pl.ds(2, width), rows]))
    loads.append((below.at[pl.ds(6, 2)], cext.at[pl.ds(0, 2), rows]))
    loads.append((above.at[pl.ds(6, 2)], cext.at[pl.ds(width + 2, 2), rows]))
    loads.append((stiff, kext.at[pl.ds(1, width)]))
    loads.append((below.at[8], kext.at[0]))
    loads.append((above.at[8], kext.at[width + 1]))
    loads = copy_all(loads, sem)
    pad = jnp.zeros((8, 128), jnp.float32)
    for p in range(width + 4):
        for at in (0, 40):
            cext[p, pl.ds(at, 8), :] = pad
            for s in range(2):
                pres[s, p, pl.ds(at, 8), :] = pad
    for p in range(width + 2):
        for at in (0, 40):
            for s in range(2):
                mid[s, p, pl.ds(at, 8), :] = pad
    wait_all(loads)

    first = lax.axis_index("gx") * width
    background = lax.axis_index("probe") == 0
    lane = lax.broadcasted_iota(jnp.int32, (32, 128), 1)
    depth = lax.broadcasted_iota(jnp.int32, (32, 128), 0)

    def next_y(v):
        return jnp.where(lane == 127, 0.0, pltpu.roll(v, 127, 1))

    def last_y(v):
        return jnp.where(lane == 0, 0.0, pltpu.roll(v, 1, 1))

    def advance(p, src, shift, before):
        c = cext[p + shift, rows, :]
        cxp = c + cext[p + shift + 1, rows, :]
        cxm = c + cext[p + shift - 1, rows, :]
        czp = c + cext[p + shift, pl.ds(9, 32), :]
        czm = c + cext[p + shift, pl.ds(7, 32), :]
        cyp = c + next_y(c)
        cym = c + last_y(c)
        k = 0.5 * kext[p + shift - 1]
        got = []
        for s in range(2):
            v = src[s, p, rows, :]
            total = cxp * (src[s, p + 1, rows, :] - v) + cxm * (src[s, p - 1, rows, :] - v)
            total += czp * (src[s, p, pl.ds(9, 32), :] - v) + czm * (src[s, p, pl.ds(7, 32), :] - v)
            total += cyp * (next_y(v) - v) + cym * (last_y(v) - v)
            got.append(2.0 * v - before(s) + k * total)
        return got

    def inject(dst_of, planes, offset, step):
        for s in range(2):
            x = sx[s] - first + offset

            @pl.when(background & (x >= 0) & (x < planes))
            def _():
                hit = (lane == sy[s]) & (depth == sz[s])
                view = dst_of(s, x)
                view[...] = view[...] + jnp.where(hit, wavelet[s, step], 0.0)

    def step_one(p, carry):
        got = advance(p + 1, pres, 0, lambda s: prev[s, p])
        for s in range(2):
            mid[s, p, rows, :] = got[s]
        return carry

    lax.fori_loop(0, width + 2, step_one, 0)
    inject(lambda s, x: mid.at[s, x, rows], width + 2, 1, 0)
    outs = []
    for s in range(2):
        outs.append(pltpu.make_async_copy(mid.at[s, pl.ds(1, width), rows], out.at[s, 0], sem_out.at[s]))
        outs[-1].start()

    def step_two(p, carry):
        got = advance(p + 1, mid, 1, lambda s: pres[s, p + 2, rows, :])
        for s in range(2):
            o2[s, p] = got[s]
        return carry

    lax.fori_loop(0, width, step_two, 0)
    inject(lambda s, x: o2.at[s, x], width, 0, 1)
    for s in range(2):
        outs.append(pltpu.make_async_copy(o2.at[s], out.at[s, 1], sem_out.at[2 + s]))
        outs[-1].start()
    wait_all(outs)


def born_kernel(
    width, extent, xb, zb, yb, sx, sz, sy, wavelet, own, left, right, stiff, buoy, below, above, pstiff, pbuoy, fields,
    out, pieces, cext, kext, ps, pb, placed, planes, sem, sem_planes
):
    del fields
    row = lax.axis_index("probe")
    g = jnp.maximum(row - 1, 0)
    first = lax.axis_index("gx") * width
    x0 = xb[g] * EDGE - 2 - first
    rows = pl.ds(8, 32)

    @pl.when((row > 0) & (x0 < width) & (x0 + SPAN > 0))
    def _():
        loads = [(own, pieces.at[1]), (left, pieces.at[0]), (right, pieces.at[2])]
        loads.append((pstiff.at[g], ps))
        loads.append((pbuoy.at[g], pb))
        loads.append((buoy, cext.at[pl.ds(2, width), rows]))
        loads.append((below.at[pl.ds(6, 2)], cext.at[pl.ds(0, 2), rows]))
        loads.append((above.at[pl.ds(6, 2)], cext.at[pl.ds(width + 2, 2), rows]))
        loads.append((stiff, kext.at[pl.ds(2, width), rows]))
        loads.append((below.at[8], kext.at[1, rows]))
        loads.append((above.at[8], kext.at[width + 2, rows]))
        loads = copy_all(loads, sem)

        def each_plane(act):
            for i in range(SPAN):

                @pl.when((x0 + i >= 0) & (x0 + i < width))
                def _():
                    act(i)

        def fetch(i):
            return pltpu.make_async_copy(out.at[:, :, x0 + i], planes.at[i, :, :, rows], sem_planes.at[i])

        def store(i):
            return pltpu.make_async_copy(planes.at[i, :, :, rows], out.at[:, :, x0 + i], sem_planes.at[i])

        each_plane(lambda i: fetch(i).start())

        z0 = zb[g] * EDGE - 2
        y0 = yb[g] * EDGE - 2
        lane = lax.broadcasted_iota(jnp.int32, (16, 128), 1)
        depth = lax.broadcasted_iota(jnp.int32, (16, 128), 0)
        here = (lane < SPAN) & (depth < SPAN)
        here &= (lane + y0 >= 0) & (lane + y0 < 128) & (depth + z0 >= 0) & (depth + z0 < 32)
        placed[...] = jnp.zeros(placed.shape, jnp.float32)
        wait_all(loads)
        for n, values in enumerate((ps, pb)):
            placed[n, pl.ds(2, EDGE), pl.ds(2, EDGE), pl.ds(0, EDGE)] = values[...]

        def inside(i):
            x = first + x0 + i
            return (x >= 0) & (x < extent)

        def coefficient(ref, low, high):
            got = []
            for i in range(SPAN):
                at = x0 + i + 2
                ok = here & (at >= low) & (at < high)
                values = ref[jnp.clip(at, 0, width + 3), pl.ds(z0 + 8, 16), :]
                got.append(jnp.where(ok, pltpu.roll(values, wrapped(-y0), 1), 0.0))
            return jnp.stack(got)

        c = coefficient(cext, 0, width + 4)
        k = coefficient(kext, 1, width + 3)
        sb = pltpu.roll(placed[0], 2, 2)
        bb = pltpu.roll(placed[1], 2, 2)

        def piece(s, t):
            got = []
            for i in range(SPAN):
                if (s, t, i) not in STRIPS:
                    got.append(jnp.zeros((16, 128), jnp.float32))
                    continue
                n = STRIPS.index((s, t, i))
                k, q = divmod(n, PER_ROW)
                at = jnp.where(x0 + i < 0, 0, jnp.where(x0 + i < width, 1, 2))
                values = pieces[at, pl.ds(k * SPAN, 16), :]
                if q:
                    values = pltpu.roll(values, 128 - SPAN * q, 1)
                got.append(jnp.where(here & inside(i), values, 0.0))
            return jnp.stack(got)

        def up(v, axis):
            return pltpu.roll(v, v.shape[axis] - 1, axis)

        def faces(coef):
            return 0.5 * (coef[1:] + coef[:-1]), 0.5 * (coef + up(coef, 1)), 0.5 * (coef + up(coef, 2))

        def op(v, coef):
            cx, cz, cy = coef
            fx = cx * (v[1:] - v[:-1])
            fz = cz * (up(v, 1) - v)
            fy = cy * (up(v, 2) - v)
            zero = jnp.zeros((1, 16, 128), jnp.float32)
            total = jnp.concatenate([fx, zero], 0) - jnp.concatenate([zero, fx], 0)
            total += fz - pltpu.roll(fz, 1, 1)
            total += fy - pltpu.roll(fy, 1, 2)
            return total

        of_c = faces(c)
        of_b = faces(bb)
        gains = []
        for s in range(2):
            now = piece(s, 1)
            laplace = op(now, of_c)
            forcing = sb * laplace + k * op(now, of_b)
            hit = here & (lane + y0 == sy[s]) & (depth + z0 == sz[s])
            source = []
            for i in range(SPAN):
                on = hit & (first + x0 + i == sx[s])
                source.append(jnp.where(on, wavelet[s, 0], 0.0))
            later = 2.0 * now - piece(s, 0) + k * laplace + jnp.stack(source)
            second = sb * op(later, of_c) + k * op(later, of_b)
            gains.append((forcing, 2.0 * forcing + k * op(forcing, of_c) + second))
        each_plane(lambda i: fetch(i).wait())
        for s in range(2):
            for t in range(2):
                moved = pltpu.roll(gains[s][t], wrapped(y0), 2)
                for i in range(SPAN):
                    view = planes.at[i, s, t, pl.ds(z0 + 8, 16)]
                    view[...] = view[...] + moved[i]
        each_plane(lambda i: store(i).start())
        each_plane(lambda i: store(i).wait())


def on_device(
    wavefields, stiffness, buoyancy, pert_stiffness, pert_buoyancy, xblock_index, zblock_index, yblock_index,
    source_xcell, source_zcell, source_ycell, wavelet
):
    wave = wavefields[0]
    width = wave.shape[2]
    slabs = lax.axis_size("gx")
    blocks = (xblock_index, zblock_index, yblock_index)
    sources = (source_xcell, source_zcell, source_ycell, wavelet)
    f32 = functools.partial(jax.ShapeDtypeStruct, dtype=jnp.float32)
    vmem = lambda *shape: pltpu.VMEM(shape, jnp.float32)
    dma = lambda *shape: pltpu.SemaphoreType.DMA(shape)

    counts = [1 + len(rest) for rest in NEXT]
    edge = f32((9, 32, 128))
    low, high, p0, p1, p2, d0, d1, d2 = pl.pallas_call(
        functools.partial(split_kernel, width),
        out_shape=[edge, edge] + [f32((n, *PIECE)) for n in counts] + [f32(PIECE)] * 3,
        in_specs=[SMEM] * 3 + [ANY] * 3,
        out_specs=[ANY] * 8,
        scratch_shapes=[vmem(2, 2, width, 48, 128), vmem(15, *PIECE), dma(12), dma(), dma(6)],
        compiler_params=PARAMS,
        name="split",
    )(*blocks, wave, stiffness, buoyancy)

    def place(row, slab):
        return row * slabs + slab

    def along_rows(value, pairs):
        every = [(place(a, s), place(b, s)) for a, b in pairs for s in range(slabs)]
        return lax.ppermute(value, ("probe", "gx"), every)

    def along_x(value, step):
        pairs = [(s, s + step) for s in range(slabs) if 0 <= s + step < slabs]
        return lax.ppermute(value, "gx", pairs)

    firsts = [along_rows(p, [(0, row)]) for p, row in zip((p0, p1, p2), FIRST)]
    directs = [along_rows(d, [(0, row)]) for d, row in zip((d0, d1, d2), DIRECT)]
    below, above = along_x(high, 1), along_x(low, -1)
    passed = pl.pallas_call(
        pass_kernel,
        out_shape=[f32(PIECE)] * 4,
        in_specs=[ANY] * 3,
        out_specs=[ANY] * 4,
        scratch_shapes=[dma(4)],
        compiler_params=PARAMS,
        name="pass_on",
    )(*firsts)
    nexts = [
        along_rows(value, [(head, rest[n]) for head, rest in zip(FIRST, NEXT) if n < len(rest)])
        for n, value in enumerate(passed)
    ]
    advanced = pl.pallas_call(
        functools.partial(march_kernel, width),
        out_shape=f32(wave.shape),
        in_specs=[SMEM] * 4 + [ANY] * 5,
        out_specs=ANY,
        scratch_shapes=[
            vmem(2, width + 4, 48, 128),
            vmem(2, width + 2, 32, 128),
            vmem(width + 4, 48, 128),
            vmem(width + 2, 32, 128),
            vmem(2, width + 2, 48, 128),
            vmem(8, 128),
            vmem(2, width, 32, 128),
            dma(18),
            dma(4),
        ],
        compiler_params=PARAMS,
        name="march",
    )(*sources, wave, stiffness, buoyancy, below, above)
    own = pl.pallas_call(
        pick_kernel,
        out_shape=f32(PIECE),
        in_specs=[ANY] * 10,
        out_specs=ANY,
        scratch_shapes=[dma()],
        compiler_params=PARAMS,
        name="pick",
    )(*firsts, *directs, *nexts)
    left, right = along_x(own, 1), along_x(own, -1)
    result = pl.pallas_call(
        functools.partial(born_kernel, width, width * slabs),
        out_shape=f32(wave.shape),
        in_specs=[SMEM] * 7 + [ANY] * 10,
        out_specs=ANY,
        input_output_aliases={16: 0},
        scratch_shapes=[
            vmem(3, *PIECE),
            vmem(width + 4, 48, 128),
            vmem(width + 4, 48, 128),
            vmem(EDGE, EDGE, EDGE),
            vmem(EDGE, EDGE, EDGE),
            vmem(2, SPAN, 16, 128),
            vmem(SPAN, 2, 2, 48, 128),
            dma(11),
            dma(SPAN),
        ],
        compiler_params=PARAMS,
        name="born",
    )(*blocks, *sources, own, left, right, stiffness, buoyancy, below, above, pert_stiffness, pert_buoyancy, advanced)
    return result[None]


def solution(mesh):
    field = P("probe", None, None, "gx", None, None)
    return jax.shard_map(
        on_device,
        mesh=mesh,
        in_specs=(field, P("gx", None, None), P("gx", None, None)) + (P(),) * 9,
        out_specs=field,
        check_vma=False,
    )
```

time: 372 us -> 53.7 us (0.14)
  waiting for transfers between devices: 292 us -> 8.05 us
  other arithmetic: 29.5 us -> 0 us
  between operations: 16.3 us -> 0.36 us
  Pallas kernels: 0 us -> 14.2 us
    psum x2 -> x0, waiting for transfers between devices: 289 us -> none  [from_root(): return lax.psum(block, axis)]
    pallas_call x0 -> x5, Pallas kernels: none -> 14.2 us  [the longest x1 8.13 us: on_device(): pl.pallas_call(functools.partial(march_kernel, width), out_shape=f32(wave...]
    unnamed x86 -> x36, local copies, waits for them, and re-layouts: 1.05 us -> 10.3 us
    concatenate x6 -> x0, other arithmetic: 8.53 us -> none  [the longest x4 6.83 us: with_halo(): block = jnp.concatenate([low, block, high], axis=dim)]
    select_n x12 -> x0, other arithmetic: 6.89 us -> none  [the longest x2 4.94 us: from_root(): jnp.where(lax.axis_index(axis) == owner, block, jnp.zeros_like(block))]
    gather x7 -> x0, local copies, waits for them, and re-layouts: 5.79 us -> none  [the longest x3 3.43 us: place_local(): picked = jnp.take(picked, jnp.clip(offset_y, 0, edge - 1), axis=2)]
    ppermute x6 -> x14, waiting for transfers between devices: 2.96 us -> 8.05 us  [the longest x10 8.04 us: along_rows(): return lax.ppermute(value, ('probe', 'gx'), every)]
    add x3 -> x0, other arithmetic: 4.1 us -> none  [the longest x2 3.56 us: stencil(): summed = termed if summed is None else summed + termed]
  transfers between devices with their start and end apart: 8 -> 14, of which waited for: 5 -> 1; matrix products, arithmetic and copies ran while one was open for 6% -> 4% of each run, Pallas kernels for 0% -> 16%
where the time goes in v1:
time: 53.7 us; the launch traced here: 53 us
  starting transfers between devices  20.1 us (37%)
  Pallas kernels  14.2 us (26%)
  local copies, waits for them, and re-layouts  10.3 us (19%)
  waiting for transfers between devices  8.05 us (15%)
    ppermute x4, starting transfers between devices, along_x(): return lax.ppermute(value, 'gx', pairs)  12.7 us
    unnamed x36, local copies, waits for them, and re-layouts  10.3 us
    pallas_call x1, Pallas kernels, on_device(): pl.pallas_call(functools.partial(march_kernel, width), out_shape=f32(wave...  8.13 us
    ppermute x10, waiting for transfers between devices, along_rows(): return lax.ppermute(value, ('probe', 'gx'), every)  8.04 us
    ppermute x10, starting transfers between devices, along_rows(): return lax.ppermute(value, ('probe', 'gx'), every)  7.4 us
    pallas_call x1, Pallas kernels, on_device(): pl.pallas_call(functools.partial(born_kernel, width, width * slabs), out_...  4.46 us
    pallas_call x1, Pallas kernels, on_device(): pl.pallas_call(functools.partial(split_kernel, width), out_shape=[edge, e...  1.41 us
  transfers between devices with their start and end apart: 14, of which 1 were waited for; matrix products, arithmetic and copies ran while one was open for 4% of the time, Pallas kernels for 16%

profile of v1, /device:TPU:24, one launch (start us, length us, event | category | flops | bytes accessed | tf_op | source)
XLA Modules:
  0.0 53.0 jit_solution(12344733590905385152)
XLA Ops:
  0.0 1.4 %copy-done = f32[1,2,2,24,32,128]{5,4,3,2,1,0:T(8,128)S(1)} copy-done((f32[1,2,2,24,32,128]{5,4,3,2,1,0:T(8,128)S(1)}, f32[1,2,2,24,32,128]{5,4,3,2,1,0:T(8,128)}, u32[]{:S(2)}) %copy-start) | copy-done | bytes 1572888
  1.4 1.0 %copy-done.2 = f32[24,32,128]{2,1,0:T(8,128)S(1)} copy-done((f32[24,32,128]{2,1,0:T(8,128)S(1)}, f32[24,32,128]{2,1,0:T(8,128)}, u32[]{:S(2)}) %copy-start.2) | copy-done | bytes 393240
  2.4 1.0 %copy-done.4 = f32[24,32,128]{2,1,0:T(8,128)S(1)} copy-done((f32[24,32,128]{2,1,0:T(8,128)S(1)}, f32[24,32,128]{2,1,0:T(8,128)}, u32[]{:S(2)}) %copy-start.4) | copy-done | bytes 393240
  3.4 0.7 %copy-done.7 = s32[15]{0:T(128)S(1)} copy-done((s32[15]{0:T(128)S(1)}, s32[15]{0:T(128)}, u32[]{:S(2)}) %copy-start.7) | copy-done | bytes 84
  5.4 1.4 %split.1 = (f32[9,32,128]{2,1,0:T(8,128)}, f32[9,32,128]{2,1,0:T(8,128)}, f32[5,64,128]{2,1,0:T(8,128)S(1)}, f32[4,64,128]{2,1,0:T(8,128)S(1)}, f32[3,64,128]{2,...) custom-call(s32[15]{0:T(128)S(1)} %copy-done.7, s32[15]{0:T(128)S(1)} %copy-done.9, ...), custom_call_target="tpu_custom_call" | custom-call | tf_op jit(solution)/shard_map/split/pallas_call | solution.py:381
  6.8 0.8 %collective-permute-start = (f32[5,64,128]{2,1,0:T(8,128)S(1)}, f32[5,64,128]{2,1,0:T(8,128)S(1)}, u32[]{:S(2)}, u32[]{:S(2)}) collective-permute-start(f32[5,64,128]{2,1,0:T(8,128)S(1)} %get-tuple-element.17), channel_id=1, source_target_pairs={{0,32},{1,33},{2,34},{3,35},{4,36},{5,37},{6,38},{7,39},{8,40},{9,... | collective-permute-start | bytes 491528 | tf_op jit(solution)/shard_map/ppermute | solution.py:396
  7.6 0.7 %collective-permute-start.1 = (f32[4,64,128]{2,1,0:T(8,128)S(1)}, f32[4,64,128]{2,1,0:T(8,128)S(1)}, u32[]{:S(2)}, u32[]{:S(2)}) collective-permute-start(f32[4,64,128]{2,1,0:T(8,128)S(1)} %get-tuple-element.18), channel_id=1, source_target_pairs={{0,64},{1,65},{2,66},{3,67},{4,68},{5,69},{6,70},{7,71},{8,72},{9,... | collective-permute-start | bytes 393224 | tf_op jit(solution)/shard_map/ppermute | solution.py:396
  8.3 0.7 %collective-permute-start.2 = (f32[3,64,128]{2,1,0:T(8,128)S(1)}, f32[3,64,128]{2,1,0:T(8,128)S(1)}, u32[]{:S(2)}, u32[]{:S(2)}) collective-permute-start(f32[3,64,128]{2,1,0:T(8,128)S(1)} %get-tuple-element.19), channel_id=1, source_target_pairs={{0,192},{1,193},{2,194},{3,195},{4,196},{5,197},{6,198},{7,199},{8... | collective-permute-start | bytes 294920 | tf_op jit(solution)/shard_map/ppermute | solution.py:396
  9.0 4.0 %collective-permute-start.12 = (f32[9,32,128]{2,1,0:T(8,128)}, f32[9,32,128]{2,1,0:T(8,128)S(1)}, u32[]{:S(2)}, u32[]{:S(2)}) collective-permute-start(f32[9,32,128]{2,1,0:T(8,128)} %get-tuple-element.27), channel_id=1, source_target_pairs={{0,1},{1,2},{2,3},{3,4},{4,5},{5,6},{6,7},{7,8},{8,9},{9,10},{10,1... | collective-permute-start | bytes 442376 | tf_op jit(solution)/shard_map/ppermute | solution.py:400
  13.0 1.9 %collective-permute-start.13 = (f32[9,32,128]{2,1,0:T(8,128)}, f32[9,32,128]{2,1,0:T(8,128)}, u32[]{:S(2)}, u32[]{:S(2)}) collective-permute-start(f32[9,32,128]{2,1,0:T(8,128)} %get-tuple-element.28), channel_id=1, source_target_pairs={{1,0},{2,1},{3,2},{4,3},{5,4},{6,5},{7,6},{8,7},{9,8},{10,9},{11,1... | collective-permute-start | bytes 442376 | tf_op jit(solution)/shard_map/ppermute | solution.py:400
  14.9 1.3 %collective-permute-start.3 = (f32[64,128]{1,0:T(8,128)S(1)}, f32[64,128]{1,0:T(8,128)S(1)}, u32[]{:S(2)}, u32[]{:S(2)}) collective-permute-start(f32[64,128]{1,0:T(8,128)S(1)} %get-tuple-element.20), channel_id=1, source_target_pairs={{0,256},{1,257},{2,258},{3,259},{4,260},{5,261},{6,262},{7,263},{8... | collective-permute-start | bytes 98312 | tf_op jit(solution)/shard_map/ppermute | solution.py:396
  16.3 0.7 %collective-permute-start.4 = (f32[64,128]{1,0:T(8,128)S(1)}, f32[64,128]{1,0:T(8,128)S(1)}, u32[]{:S(2)}, u32[]{:S(2)}) collective-permute-start(f32[64,128]{1,0:T(8,128)S(1)} %get-tuple-element.21), channel_id=1, source_target_pairs={{0,352},{1,353},{2,354},{3,355},{4,356},{5,357},{6,358},{7,359},{8... | collective-permute-start | bytes 98312 | tf_op jit(solution)/shard_map/ppermute | solution.py:396
  16.9 0.7 %collective-permute-start.5 = (f32[64,128]{1,0:T(8,128)S(1)}, f32[64,128]{1,0:T(8,128)S(1)}, u32[]{:S(2)}, u32[]{:S(2)}) collective-permute-start(f32[64,128]{1,0:T(8,128)S(1)} %get-tuple-element.22), channel_id=1, source_target_pairs={{0,416},{1,417},{2,418},{3,419},{4,420},{5,421},{6,422},{7,423},{8... | collective-permute-start | bytes 98312 | tf_op jit(solution)/shard_map/ppermute | solution.py:396
  17.7 8.0 %collective-permute-done.3.d0 = f32[64,128]{1,0:T(8,128)S(1)} collective-permute-done((f32[64,128]{1,0:T(8,128)S(1)}, f32[64,128]{1,0:T(8,128)S(1)}, u32[]{:S(2)}, u32[]{:S(2)}) %collective-permute-start.3) | collective-permute-done | bytes 32800 | tf_op jit(solution)/shard_map/ppermute | solution.py:396
  26.4 0.7 %collective-permute-start.7 = (f32[64,128]{1,0:T(8,128)S(1)}, f32[64,128]{1,0:T(8,128)S(1)}, u32[]{:S(2)}, u32[]{:S(2)}) collective-permute-start(f32[64,128]{1,0:T(8,128)S(1)} %get-tuple-element.24), channel_id=1, source_target_pairs={{32,96},{33,97},{34,98},{35,99},{36,100},{37,101},{38,102},{39,103... | collective-permute-start | bytes 98312 | tf_op jit(solution)/shard_map/ppermute | solution.py:396
  27.0 0.7 %collective-permute-start.8 = (f32[64,128]{1,0:T(8,128)S(1)}, f32[64,128]{1,0:T(8,128)S(1)}, u32[]{:S(2)}, u32[]{:S(2)}) collective-permute-start(f32[64,128]{1,0:T(8,128)S(1)} %get-tuple-element.25), channel_id=1, source_target_pairs={{32,224},{33,225},{34,226},{35,227},{36,228},{37,229},{38,230},{39... | collective-permute-start | bytes 98312 | tf_op jit(solution)/shard_map/ppermute | solution.py:396
  27.7 0.7 %collective-permute-start.9 = (f32[64,128]{1,0:T(8,128)S(1)}, f32[64,128]{1,0:T(8,128)S(1)}, u32[]{:S(2)}, u32[]{:S(2)}) collective-permute-start(f32[64,128]{1,0:T(8,128)S(1)} %get-tuple-element.26), channel_id=1, source_target_pairs={{32,160},{33,161},{34,162},{35,163},{36,164},{37,165},{38,166},{39... | collective-permute-start | bytes 98312 | tf_op jit(solution)/shard_map/ppermute | solution.py:396
  28.6 1.9 %collective-permute-start.11 = (f32[64,128]{1,0:T(8,128)S(1)}, f32[64,128]{1,0:T(8,128)S(1)}, u32[]{:S(2)}, u32[]{:S(2)}) collective-permute-start(f32[64,128]{1,0:T(8,128)S(1)} %pick.1.own), channel_id=1, source_target_pairs={{1,0},{2,1},{3,2},{4,3},{5,4},{6,5},{7,6},{8,7},{9,8},{10,9},{11,1... | collective-permute-start | bytes 98312 | tf_op jit(solution)/shard_map/ppermute | solution.py:400
  30.5 4.8 %collective-permute-start.10 = (f32[64,128]{1,0:T(8,128)S(1)}, f32[64,128]{1,0:T(8,128)}, u32[]{:S(2)}, u32[]{:S(2)}) collective-permute-start(f32[64,128]{1,0:T(8,128)S(1)} %pick.1.own), channel_id=1, source_target_pairs={{0,1},{1,2},{2,3},{3,4},{4,5},{5,6},{6,7},{7,8},{8,9},{9,10},{10,1... | collective-permute-start | bytes 98312 | tf_op jit(solution)/shard_map/ppermute | solution.py:400
  35.3 0.7 %copy.14.pstiff = f32[15,8,8,8]{3,2,1,0:T(8,128)S(1)} copy(f32[15,8,8,8]{0,3,2,1:T(8,128)S(1)} %copy-done.16) | data formatting | bytes 61440 | tf_op args[3]
  36.0 1.6 %copy.15.pbuoy = f32[15,8,8,8]{3,2,1,0:T(8,128)S(1)} copy(f32[15,8,8,8]{0,3,2,1:T(8,128)} %param.16) | data formatting | bytes 61440 | tf_op args[4]
  37.7 0.7 %copy-done.6 = f32[2,2]{1,0:T(2,128)S(1)} copy-done((f32[2,2]{1,0:T(2,128)S(1)}, f32[2,2]{1,0:T(2,128)}, u32[]{:S(2)}) %copy-start.6) | copy-done | bytes 40
  40.3 8.1 %march.1.fields = f32[2,2,24,32,128]{4,3,2,1,0:T(8,128)} custom-call(s32[2]{0:T(128)S(1)} %copy-done.13, s32[2]{0:T(128)S(1)} %copy-done.14, s32[2]{0:T(128)S(1)} %copy-done.15, f32[2,2]{1,0:T(2,128)S(1)} %copy-done.6, f32[2,2,24,32,128]{4,3,2,1,0:T(8,128)S(1)} %bitcast.3, f32[24,32,128]{2,1,0:T(8,128)S(1)} %copy-done.3, f32[24,32,128]{2,1,0:T(8,128)S(1)} %copy-done.5, ...), custom_call_target="tpu_custom_call" | custom-call | tf_op jit(solution)/shard_map/march/pallas_call | solution.py:418
  48.5 4.5 %born.1 = f32[2,2,24,32,128]{4,3,2,1,0:T(8,128)} custom-call(s32[15]{0:T(128)S(1)} %copy-done.8, s32[15]{0:T(128)S(1)} %copy-done.10, s32[15]{0:T(128)S(1)} %copy-done.12, s32[2]{0:T(128)S(1)} %copy-done.13, s32[2]{0:T(128)S(1)} %copy-done.14, s32[2]{0:T(128)S(1)} %copy-done.15, f32[2,2]{1,0:T(2,128)S(1)} %copy-done.6, ...), custom_call_target="tpu_custom_call", output_to_operand_aliasing={{}: (16, {})} | custom-call | tf_op jit(solution)/shard_map/born/pallas_call | solution.py:447
  (45 shorter events, 4.2 us)
Async XLA Ops:
  0.0 1.4 %copy-start = (f32[1,2,2,24,32,128]{5,4,3,2,1,0:T(8,128)S(1)}, f32[1,2,2,24,32,128]{5,4,3,2,1,0:T(8,128)}, u32[]{:S(2)}) copy-start(f32[1,2,2,24,32,128]{5,4,3,2,1,0:T(8,128)} %param.12) | copy-start | bytes 4718596
  1.4 1.0 %copy-start.2 = (f32[24,32,128]{2,1,0:T(8,128)S(1)}, f32[24,32,128]{2,1,0:T(8,128)}, u32[]{:S(2)}) copy-start(f32[24,32,128]{2,1,0:T(8,128)} %stiff.5) | copy-start | bytes 1179652
  2.4 1.0 %copy-start.4 = (f32[24,32,128]{2,1,0:T(8,128)S(1)}, f32[24,32,128]{2,1,0:T(8,128)}, u32[]{:S(2)}) copy-start(f32[24,32,128]{2,1,0:T(8,128)} %buoy.5) | copy-start | bytes 1179652
  5.4 30.0 %copy-start.16 = (f32[15,8,8,8]{0,3,2,1:T(8,128)S(1)}, f32[15,8,8,8]{0,3,2,1:T(8,128)}, u32[]{:S(2)}) copy-start(f32[15,8,8,8]{0,3,2,1:T(8,128)} %param.15) | copy-start | bytes 92164
  6.8 30.9 %copy-start.1 = (f32[1,2,2,24,32,128]{5,4,3,2,1,0:T(8,128)S(1)}, f32[1,2,2,24,32,128]{5,4,3,2,1,0:T(8,128)}, u32[]{:S(2)}) copy-start(f32[1,2,2,24,32,128]{5,4,3,2,1,0:T(8,128)} %param.12) | copy-start | bytes 4718596
  6.8 30.9 %copy-start.3 = (f32[24,32,128]{2,1,0:T(8,128)S(1)}, f32[24,32,128]{2,1,0:T(8,128)}, u32[]{:S(2)}) copy-start(f32[24,32,128]{2,1,0:T(8,128)} %stiff.5) | copy-start | bytes 1179652
  6.8 30.8 %copy-start.5 = (f32[24,32,128]{2,1,0:T(8,128)S(1)}, f32[24,32,128]{2,1,0:T(8,128)}, u32[]{:S(2)}) copy-start(f32[24,32,128]{2,1,0:T(8,128)} %buoy.5) | copy-start | bytes 1179652
  6.8 10.1 %collective-permute-start = (f32[5,64,128]{2,1,0:T(8,128)S(1)}, f32[5,64,128]{2,1,0:T(8,128)S(1)}, u32[]{:S(2)}, u32[]{:S(2)}) collective-permute-start(f32[5,64,128]{2,1,0:T(8,128)S(1)} %get-tuple-element.17), channel_id=1, source_target_pairs={{0,32},{1,33},{2,34},{3,35},{4,36},{5,37},{6,38},{7,39},{8,40},{9,... | collective-permute-start | bytes 491528 | tf_op jit(solution)/shard_map/ppermute | solution.py:396
  7.6 8.6 %collective-permute-start.1 = (f32[4,64,128]{2,1,0:T(8,128)S(1)}, f32[4,64,128]{2,1,0:T(8,128)S(1)}, u32[]{:S(2)}, u32[]{:S(2)}) collective-permute-start(f32[4,64,128]{2,1,0:T(8,128)S(1)} %get-tuple-element.18), channel_id=1, source_target_pairs={{0,64},{1,65},{2,66},{3,67},{4,68},{5,69},{6,70},{7,71},{8,72},{9,... | collective-permute-start | bytes 393224 | tf_op jit(solution)/shard_map/ppermute | solution.py:396
  8.3 6.6 %collective-permute-start.2 = (f32[3,64,128]{2,1,0:T(8,128)S(1)}, f32[3,64,128]{2,1,0:T(8,128)S(1)}, u32[]{:S(2)}, u32[]{:S(2)}) collective-permute-start(f32[3,64,128]{2,1,0:T(8,128)S(1)} %get-tuple-element.19), channel_id=1, source_target_pairs={{0,192},{1,193},{2,194},{3,195},{4,196},{5,197},{6,198},{7,199},{8... | collective-permute-start | bytes 294920 | tf_op jit(solution)/shard_map/ppermute | solution.py:396
  9.0 28.6 %collective-permute-start.12 = (f32[9,32,128]{2,1,0:T(8,128)}, f32[9,32,128]{2,1,0:T(8,128)S(1)}, u32[]{:S(2)}, u32[]{:S(2)}) collective-permute-start(f32[9,32,128]{2,1,0:T(8,128)} %get-tuple-element.27), channel_id=1, source_target_pairs={{0,1},{1,2},{2,3},{3,4},{4,5},{5,6},{6,7},{7,8},{8,9},{9,10},{10,1... | collective-permute-start | bytes 442376 | tf_op jit(solution)/shard_map/ppermute | solution.py:400
  13.0 24.6 %collective-permute-start.13 = (f32[9,32,128]{2,1,0:T(8,128)}, f32[9,32,128]{2,1,0:T(8,128)}, u32[]{:S(2)}, u32[]{:S(2)}) collective-permute-start(f32[9,32,128]{2,1,0:T(8,128)} %get-tuple-element.28), channel_id=1, source_target_pairs={{1,0},{2,1},{3,2},{4,3},{5,4},{6,5},{7,6},{8,7},{9,8},{10,9},{11,1... | collective-permute-start | bytes 442376 | tf_op jit(solution)/shard_map/ppermute | solution.py:400
  14.9 10.8 %collective-permute-start.3 = (f32[64,128]{1,0:T(8,128)S(1)}, f32[64,128]{1,0:T(8,128)S(1)}, u32[]{:S(2)}, u32[]{:S(2)}) collective-permute-start(f32[64,128]{1,0:T(8,128)S(1)} %get-tuple-element.20), channel_id=1, source_target_pairs={{0,256},{1,257},{2,258},{3,259},{4,260},{5,261},{6,262},{7,263},{8... | collective-permute-start | bytes 98312 | tf_op jit(solution)/shard_map/ppermute | solution.py:396
  16.3 10.1 %collective-permute-start.4 = (f32[64,128]{1,0:T(8,128)S(1)}, f32[64,128]{1,0:T(8,128)S(1)}, u32[]{:S(2)}, u32[]{:S(2)}) collective-permute-start(f32[64,128]{1,0:T(8,128)S(1)} %get-tuple-element.21), channel_id=1, source_target_pairs={{0,352},{1,353},{2,354},{3,355},{4,356},{5,357},{6,358},{7,359},{8... | collective-permute-start | bytes 98312 | tf_op jit(solution)/shard_map/ppermute | solution.py:396
  16.9 10.1 %collective-permute-start.5 = (f32[64,128]{1,0:T(8,128)S(1)}, f32[64,128]{1,0:T(8,128)S(1)}, u32[]{:S(2)}, u32[]{:S(2)}) collective-permute-start(f32[64,128]{1,0:T(8,128)S(1)} %get-tuple-element.22), channel_id=1, source_target_pairs={{0,416},{1,417},{2,418},{3,419},{4,420},{5,421},{6,422},{7,423},{8... | collective-permute-start | bytes 98312 | tf_op jit(solution)/shard_map/ppermute | solution.py:396
  25.7 2.0 %collective-permute-start.6 = (f32[64,128]{1,0:T(8,128)S(1)}, f32[64,128]{1,0:T(8,128)S(1)}, u32[]{:S(2)}, u32[]{:S(2)}) collective-permute-start(f32[64,128]{1,0:T(8,128)S(1)} %get-tuple-element.23), channel_id=1, source_target_pairs={{32,288},{33,289},{34,290},{35,291},{36,292},{37,293},{38,294},{39... | collective-permute-start | bytes 98312 | tf_op jit(solution)/shard_map/ppermute | solution.py:396
  26.4 2.0 %collective-permute-start.7 = (f32[64,128]{1,0:T(8,128)S(1)}, f32[64,128]{1,0:T(8,128)S(1)}, u32[]{:S(2)}, u32[]{:S(2)}) collective-permute-start(f32[64,128]{1,0:T(8,128)S(1)} %get-tuple-element.24), channel_id=1, source_target_pairs={{32,96},{33,97},{34,98},{35,99},{36,100},{37,101},{38,102},{39,103... | collective-permute-start | bytes 98312 | tf_op jit(solution)/shard_map/ppermute | solution.py:396
  27.0 1.4 %collective-permute-start.8 = (f32[64,128]{1,0:T(8,128)S(1)}, f32[64,128]{1,0:T(8,128)S(1)}, u32[]{:S(2)}, u32[]{:S(2)}) collective-permute-start(f32[64,128]{1,0:T(8,128)S(1)} %get-tuple-element.25), channel_id=1, source_target_pairs={{32,224},{33,225},{34,226},{35,227},{36,228},{37,229},{38,230},{39... | collective-permute-start | bytes 98312 | tf_op jit(solution)/shard_map/ppermute | solution.py:396
  27.7 0.7 %collective-permute-start.9 = (f32[64,128]{1,0:T(8,128)S(1)}, f32[64,128]{1,0:T(8,128)S(1)}, u32[]{:S(2)}, u32[]{:S(2)}) collective-permute-start(f32[64,128]{1,0:T(8,128)S(1)} %get-tuple-element.26), channel_id=1, source_target_pairs={{32,160},{33,161},{34,162},{35,163},{36,164},{37,165},{38,166},{39... | collective-permute-start | bytes 98312 | tf_op jit(solution)/shard_map/ppermute | solution.py:396
  28.6 19.9 %collective-permute-start.11 = (f32[64,128]{1,0:T(8,128)S(1)}, f32[64,128]{1,0:T(8,128)S(1)}, u32[]{:S(2)}, u32[]{:S(2)}) collective-permute-start(f32[64,128]{1,0:T(8,128)S(1)} %pick.1.own), channel_id=1, source_target_pairs={{1,0},{2,1},{3,2},{4,3},{5,4},{6,5},{7,6},{8,7},{9,8},{10,9},{11,1... | collective-permute-start | bytes 98312 | tf_op jit(solution)/shard_map/ppermute | solution.py:400
  30.5 18.0 %collective-permute-start.10 = (f32[64,128]{1,0:T(8,128)S(1)}, f32[64,128]{1,0:T(8,128)}, u32[]{:S(2)}, u32[]{:S(2)}) collective-permute-start(f32[64,128]{1,0:T(8,128)S(1)} %pick.1.own), channel_id=1, source_target_pairs={{0,1},{1,2},{2,3},{3,4},{4,5},{5,6},{6,7},{7,8},{8,9},{9,10},{10,1... | collective-permute-start | bytes 98312 | tf_op jit(solution)/shard_map/ppermute | solution.py:400
  40.3 8.2 %copy-start.8 = (s32[15]{0:T(128)S(1)}, s32[15]{0:T(128)}, u32[]{:S(2)}) copy-start(s32[15]{0:T(128)} %xb.3) | copy-start | bytes 184
  40.3 8.2 %copy-start.10 = (s32[15]{0:T(128)S(1)}, s32[15]{0:T(128)}, u32[]{:S(2)}) copy-start(s32[15]{0:T(128)} %zb.3) | copy-start | bytes 184
  40.3 8.2 %copy-start.12 = (s32[15]{0:T(128)S(1)}, s32[15]{0:T(128)}, u32[]{:S(2)}) copy-start(s32[15]{0:T(128)} %yb.3) | copy-start | bytes 184
  (7 other events, 4.6 us)

commit v2 on v0

v2 whole, which is shorter than its diff:
```python
import functools

import jax
import jax.numpy as jnp
from jax import lax
from jax.experimental import pallas as pl
from jax.experimental.pallas import tpu as pltpu
from jax.sharding import PartitionSpec as P

EDGE = 8
SPAN = EDGE + 4
PER_ROW = 10
STRIPS = [(s, 1, i) for s in range(2) for i in range(SPAN)] + [
    (s, 0, i) for s in range(2) for i in range(1, SPAN - 1)
]
PIECE = (64, 128)

FIRST = (1, 2, 6)
NEXT = ((9, 3, 7, 5), (10, 4, 12), (14, 15))
DIRECT = (8, 11, 13)

ANY = pl.BlockSpec(memory_space=pl.ANY)
HBM = pl.BlockSpec(memory_space=pltpu.HBM)
PARAMS = pltpu.CompilerParams(vmem_limit_bytes=32 * 1024 * 1024)


def copy_all(pairs, sems, start=0):
    copies = [pltpu.make_async_copy(a, b, sems.at[start + n]) for n, (a, b) in enumerate(pairs)]
    for copy in copies:
        copy.start()
    return copies


def wait_all(copies):
    for copy in copies:
        copy.wait()


def wrapped(shift):
    return jnp.bitwise_and(shift + 128, 127)


def window(xb, zb, yb, g, first):
    return xb[g] * EDGE - 2 - first, jnp.clip(zb[g] * EDGE - 2, 0, 32 - SPAN), yb[g] * EDGE - 2


def met(x0, width):
    return (x0 < width) & (x0 + SPAN > 0)


def from_sides(swap_a, swap_b, act):
    even = lax.rem(lax.axis_index("gx"), 2) == 0

    @pl.when(even)
    def _():
        act(swap_b, swap_a)

    @pl.when(jnp.logical_not(even))
    def _():
        act(swap_a, swap_b)


def edge_kernel(width, wave, stiff, buoy, swap_a, swap_b, sem):
    def pack(low, high):
        pairs = []
        for out, outer, inner in ((low, 0, 0), (high, width - 1, width - 2)):
            for s in range(2):
                pairs.append((wave.at[s, 1, pl.ds(inner, 2)], out.at[pl.ds(2 * s, 2)]))
                pairs.append((wave.at[s, 0, outer], out.at[4 + s]))
            pairs.append((buoy.at[pl.ds(inner, 2)], out.at[pl.ds(6, 2)]))
            pairs.append((stiff.at[outer], out.at[8]))
        wait_all(copy_all(pairs, sem))

    from_sides(swap_a, swap_b, pack)


def split_kernel(
    width, xb, zb, yb, wave, swap_a, swap_b, p0, p1, p2, d0, d1, d2, sxb, szb, syb, slab, packed, sem, sem_out
):
    @pl.when(lax.axis_index("probe") == 0)
    def _():
        first = lax.axis_index("gx") * width
        index = copy_all([(xb, sxb), (zb, szb), (yb, syb)], sem)
        rows = pl.ds(0, 32)
        load = copy_all([(wave, slab.at[:, :, pl.ds(2, width), rows])], sem, 3)

        def fill(below, above):
            pairs = []
            for s in range(2):
                pairs.append((below.at[pl.ds(2 * s, 2)], slab.at[s, 1, pl.ds(0, 2), rows]))
                pairs.append((above.at[pl.ds(2 * s, 2)], slab.at[s, 1, pl.ds(width + 2, 2), rows]))
                pairs.append((below.at[4 + s], slab.at[s, 0, 1, rows]))
                pairs.append((above.at[4 + s], slab.at[s, 0, width + 2, rows]))
            wait_all(copy_all(pairs, sem, 4))

        from_sides(swap_a, swap_b, fill)
        wait_all(index)
        wait_all(load)
        lane = lax.broadcasted_iota(jnp.int32, (16, 128), 1)

        def one(g, at):
            x0, z0, y0 = window(sxb, szb, syb, g, first)

            @pl.when(met(x0, width))
            def _():
                for k in range(0, len(STRIPS), PER_ROW):
                    row = jnp.zeros((16, 128), jnp.float32)
                    for q, (s, t, i) in enumerate(STRIPS[k : k + PER_ROW]):
                        plane = jnp.clip(x0 + i + 2, 0, width + 3)
                        values = pltpu.roll(slab[s, t, plane, pl.ds(z0, 16), :], wrapped(SPAN * q - y0), 1)
                        row = jnp.where((lane >= SPAN * q) & (lane < SPAN * (q + 1)), values, row)
                    packed[at, pl.ds(k // PER_ROW * SPAN, 16), :] = row

        spots = []
        for head, rest in zip(FIRST, NEXT):
            spots += [head, *rest]
        spots += DIRECT
        for at, row in enumerate(spots):
            one(row - 1, at)

        outs, at = [], 0
        for out, rest in zip((p0, p1, p2), NEXT):
            outs.append((packed.at[pl.ds(at, 1 + len(rest))], out))
            at += 1 + len(rest)
        for out in (d0, d1, d2):
            outs.append((packed.at[at], out))
            at += 1
        wait_all(copy_all(outs, sem_out))


def pass_kernel(r0, r1, r2, after, q0, q1, q2, q3, sem):
    del after
    row = lax.axis_index("probe")
    for head, rest, got in zip(FIRST, NEXT, (r0, r1, r2)):

        @pl.when(row == head)
        def _():
            pairs = [(got.at[1 + n], out) for n, out in zip(range(len(rest)), (q0, q1, q2, q3))]
            wait_all(copy_all(pairs, sem))


def march_kernel(
    width, xb, zb, yb, sx, sz, sy, wavelet, wave, stiff, buoy, swap_a, swap_b, pstiff, pbuoy, out, prep,
    sxb, szb, syb, ssx, ssz, ssy, swavelet, pres, prev, cext, kext, mid, later, perts, placed, sem, sem_side, sem_out,
):
    rows = pl.ds(8, 32)
    scalars = [(xb, sxb), (zb, szb), (yb, syb), (sx, ssx), (sz, ssz), (sy, ssy), (wavelet, swavelet)]
    loads = copy_all(scalars, sem)
    bulk = [(buoy, cext.at[pl.ds(2, width), rows]), (stiff, kext.at[pl.ds(2, width), pl.ds(0, 32)])]
    for s in range(2):
        bulk.append((wave.at[s, 1], pres.at[s, pl.ds(2, width), rows]))
        bulk.append((wave.at[s, 0], prev.at[s, pl.ds(1, width)]))
    bulk += [(pstiff, perts.at[0]), (pbuoy, perts.at[1])]
    loads += copy_all(bulk, sem, len(scalars))
    pad = jnp.zeros((8, 128), jnp.float32)
    for p in range(width + 4):
        for at in (0, 40):
            cext[p, pl.ds(at, 8), :] = pad
            for s in range(2):
                pres[s, p, pl.ds(at, 8), :] = pad
    for p in range(width + 2):
        for at in (0, 40):
            for s in range(2):
                mid[s, p, pl.ds(at, 8), :] = pad

    def fill(below, above):
        pairs = []
        for s in range(2):
            pairs.append((below.at[pl.ds(2 * s, 2)], pres.at[s, pl.ds(0, 2), rows]))
            pairs.append((above.at[pl.ds(2 * s, 2)], pres.at[s, pl.ds(width + 2, 2), rows]))
            pairs.append((below.at[4 + s], prev.at[s, 0]))
            pairs.append((above.at[4 + s], prev.at[s, width + 1]))
        pairs.append((below.at[pl.ds(6, 2)], cext.at[pl.ds(0, 2), rows]))
        pairs.append((above.at[pl.ds(6, 2)], cext.at[pl.ds(width + 2, 2), rows]))
        pairs.append((below.at[8], kext.at[1, pl.ds(0, 32)]))
        pairs.append((above.at[8], kext.at[width + 2, pl.ds(0, 32)]))
        wait_all(copy_all(pairs, sem_side))

    from_sides(swap_a, swap_b, fill)
    wait_all(loads)

    first = lax.axis_index("gx") * width
    row = lax.axis_index("probe")
    lane = lax.broadcasted_iota(jnp.int32, (32, 128), 1)
    depth = lax.broadcasted_iota(jnp.int32, (32, 128), 0)

    def next_y(v):
        return jnp.where(lane == 127, 0.0, pltpu.roll(v, 127, 1))

    def last_y(v):
        return jnp.where(lane == 0, 0.0, pltpu.roll(v, 1, 1))

    def advance(p, src, shift, before):
        c = cext[p + shift, rows, :]
        cxp = c + cext[p + shift + 1, rows, :]
        cxm = c + cext[p + shift - 1, rows, :]
        czp = c + cext[p + shift, pl.ds(9, 32), :]
        czm = c + cext[p + shift, pl.ds(7, 32), :]
        cyp = c + next_y(c)
        cym = c + last_y(c)
        k = 0.5 * kext[p + shift, pl.ds(0, 32), :]
        got = []
        for s in range(2):
            v = src[s, p, rows, :]
            total = cxp * (src[s, p + 1, rows, :] - v) + cxm * (src[s, p - 1, rows, :] - v)
            total += czp * (src[s, p, pl.ds(9, 32), :] - v) + czm * (src[s, p, pl.ds(7, 32), :] - v)
            total += cyp * (next_y(v) - v) + cym * (last_y(v) - v)
            got.append(2.0 * v - before(s) + k * total)
        return got

    def inject(view_of, planes, offset, step):
        for s in range(2):
            x = ssx[s] - first + offset

            @pl.when((row == 0) & (x >= 0) & (x < planes))
            def _():
                hit = (lane == ssy[s]) & (depth == ssz[s])
                view = view_of(s, x)
                view[...] = view[...] + jnp.where(hit, swavelet[s, step], 0.0)

    def step_one(p, carry):
        got = advance(p + 1, pres, 0, lambda s: prev[s, p])
        for s in range(2):
            mid[s, p, rows, :] = got[s]
        return carry

    lax.fori_loop(0, width + 2, step_one, 0)
    inject(lambda s, x: mid.at[s, x, rows], width + 2, 1, 0)
    outs = copy_all([(mid.at[s, pl.ds(1, width), rows], out.at[s, 0]) for s in range(2)], sem_out)

    def step_two(p, carry):
        got = advance(p + 1, mid, 1, lambda s: pres[s, p + 2, rows, :])
        for s in range(2):
            later[s, p] = got[s]
        return carry

    lax.fori_loop(0, width, step_two, 0)
    inject(lambda s, x: later.at[s, x], width, 0, 1)
    outs += copy_all([(later.at[s], out.at[s, 1]) for s in range(2)], sem_out, 2)

    g = jnp.maximum(row - 1, 0)
    x0, z0, y0 = window(sxb, szb, syb, g, first)

    @pl.when((row > 0) & met(x0, width))
    def _():
        strip = lax.broadcasted_iota(jnp.int32, (16, 128), 1)
        here = (strip < SPAN) & (lax.broadcasted_iota(jnp.int32, (16, 128), 0) < SPAN)
        here &= (strip + y0 >= 0) & (strip + y0 < 128)
        placed[...] = jnp.zeros(placed.shape, jnp.float32)
        for n, (ref, top, low) in enumerate(((cext, 8, 0), (kext, 0, 1))):
            for i in range(SPAN):
                at = x0 + i + 2
                ok = here & (at >= low) & (at < width + 4 - low)
                values = ref[jnp.clip(at, 0, width + 3), pl.ds(z0 + top, 16), :]
                placed[n, i] = jnp.where(ok, pltpu.roll(values, wrapped(-y0), 1), 0.0)
        wide = lax.broadcasted_iota(jnp.int32, (EDGE, EDGE, perts.shape[-1]), 2)
        diagonal = lax.broadcasted_iota(jnp.int32, (EDGE, EDGE, 128), 2)
        diagonal = diagonal == lax.broadcasted_iota(jnp.int32, (EDGE, EDGE, 128), 1) + 2
        dz = szb[g] * EDGE - z0
        for n in range(2):
            for i in range(EDGE):
                column = jnp.sum(jnp.where(wide == g, perts[n, i], 0.0), axis=2, keepdims=True)
                block = jnp.sum(jnp.where(diagonal, column, 0.0), axis=1)
                placed[2 + n, 2 + i, pl.ds(dz, EDGE), :] = block
        wait_all(copy_all([(placed, prep)], sem_out, 4))

    wait_all(outs)


def born_kernel(
    width, extent, xb, zb, yb, sx, sz, sy, wavelet, r0, r1, r2, d0, d1, d2, q0, q1, q2, q3, prep, fields, out,
    sxb, szb, syb, ssx, ssz, ssy, swavelet, piece, placed, planes, sem, sem_planes,
):
    del fields
    row = lax.axis_index("probe")

    @pl.when(row > 0)
    def _():
        scalars = [(xb, sxb), (zb, szb), (yb, syb), (sx, ssx), (sz, ssz), (sy, ssy), (wavelet, swavelet)]
        wait_all(copy_all(scalars, sem))
        g = row - 1
        first = lax.axis_index("gx") * width
        x0, z0, y0 = window(sxb, szb, syb, g, first)

        @pl.when(met(x0, width))
        def _():
            load = copy_all([(prep, placed)], sem)

            def each_plane(act):
                for i in range(SPAN):

                    @pl.when((x0 + i >= 0) & (x0 + i < width))
                    def _():
                        act(i)

            def plane(i):
                return out.at[:, :, x0 + i], planes.at[i, :, :, pl.ds(0, 32)]

            def fetch(i):
                source, target = plane(i)
                return pltpu.make_async_copy(source, target, sem_planes.at[i])

            def store(i):
                target, source = plane(i)
                return pltpu.make_async_copy(source, target, sem_planes.at[i])

            each_plane(lambda i: fetch(i).start())

            def bring(where, source):
                @pl.when(where)
                def _():
                    wait_all(copy_all([(source, piece)], sem, 1))

            for head, got in zip(FIRST, (r0, r1, r2)):
                bring(row == head, got.at[0])
            for target, got in zip(DIRECT, (d0, d1, d2)):
                bring(row == target, got)
            for n, got in enumerate((q0, q1, q2, q3)):
                where = row < 0
                for rest in NEXT:
                    if n < len(rest):
                        where = where | (row == rest[n])
                bring(where, got)
            wait_all(load)

            lane = lax.broadcasted_iota(jnp.int32, (16, 128), 1)
            depth = lax.broadcasted_iota(jnp.int32, (16, 128), 0)
            here = (lane < SPAN) & (depth < SPAN) & (lane + y0 >= 0) & (lane + y0 < 128)
            c, k, sb, bb = (placed[n] for n in range(4))

            def field(s, t):
                got = []
                for i in range(SPAN):
                    if (s, t, i) not in STRIPS:
                        got.append(jnp.zeros((16, 128), jnp.float32))
                        continue
                    at, q = divmod(STRIPS.index((s, t, i)), PER_ROW)
                    values = piece[pl.ds(at * SPAN, 16), :]
                    if q:
                        values = pltpu.roll(values, 128 - SPAN * q, 1)
                    x = x0 + i
                    ok = here & (first + x >= 0) & (first + x < extent)
                    ok &= (x >= -1 - t) & (x < width + 1 + t)
                    got.append(jnp.where(ok, values, 0.0))
                return jnp.stack(got)

            def up(v, axis):
                return pltpu.roll(v, v.shape[axis] - 1, axis)

            def faces(coef):
                return 0.5 * (coef[1:] + coef[:-1]), 0.5 * (coef + up(coef, 1)), 0.5 * (coef + up(coef, 2))

            def op(v, coef):
                cx, cz, cy = coef
                fx = cx * (v[1:] - v[:-1])
                fz = cz * (up(v, 1) - v)
                fy = cy * (up(v, 2) - v)
                zero = jnp.zeros((1, 16, 128), jnp.float32)
                total = jnp.concatenate([fx, zero], 0) - jnp.concatenate([zero, fx], 0)
                total += fz - pltpu.roll(fz, 1, 1)
                total += fy - pltpu.roll(fy, 1, 2)
                return total

            of_c = faces(c)
            of_b = faces(bb)
            gains = []
            for s in range(2):
                now = field(s, 1)
                laplace = op(now, of_c)
                forcing = sb * laplace + k * op(now, of_b)
                hit = here & (lane + y0 == ssy[s]) & (depth + z0 == ssz[s])
                source = []
                for i in range(SPAN):
                    on = hit & (first + x0 + i == ssx[s])
                    source.append(jnp.where(on, swavelet[s, 0], 0.0))
                later = 2.0 * now - field(s, 0) + k * laplace + jnp.stack(source)
                second = sb * op(later, of_c) + k * op(later, of_b)
                gains.append((forcing, 2.0 * forcing + k * op(forcing, of_c) + second))
            each_plane(lambda i: fetch(i).wait())
            for s in range(2):
                for t in range(2):
                    moved = pltpu.roll(gains[s][t], wrapped(y0), 2)
                    for i in range(SPAN):
                        view = planes.at[i, s, t, pl.ds(z0, 16)]
                        view[...] = view[...] + moved[i]
            each_plane(lambda i: store(i).start())
            each_plane(lambda i: store(i).wait())


def on_device(
    wavefields, stiffness, buoyancy, pert_stiffness, pert_buoyancy, xblock_index, zblock_index, yblock_index,
    source_xcell, source_zcell, source_ycell, wavelet
):
    wave = wavefields[0]
    width = wave.shape[2]
    slabs = lax.axis_size("gx")
    blocks = (xblock_index, zblock_index, yblock_index)
    sources = (source_xcell, source_zcell, source_ycell, wavelet)
    perts = [jnp.transpose(p, (1, 2, 3, 0)) for p in (pert_stiffness, pert_buoyancy)]
    f32 = functools.partial(jax.ShapeDtypeStruct, dtype=jnp.float32)
    vmem = lambda *shape: pltpu.VMEM(shape, jnp.float32)
    dma = lambda *shape: pltpu.SemaphoreType.DMA(shape)
    in_smem = lambda arrays: [pltpu.SMEM(a.shape, a.dtype) for a in arrays]

    def call(kernel, name, out_shape, in_specs, scratch, **more):
        made = pl.pallas_call(
            kernel,
            out_shape=out_shape,
            in_specs=in_specs,
            out_specs=jax.tree.map(lambda _: ANY, out_shape),
            scratch_shapes=scratch,
            compiler_params=PARAMS,
            name=name,
            **more,
        )

        def run(*args):
            keep = lambda x: pltpu.with_memory_space_constraint(x, pltpu.HBM)
            return made(*(keep(x) if spec is HBM else x for x, spec in zip(args, in_specs)))

        return run

    def along_rows(value, pairs):
        every = [(a * slabs + s, b * slabs + s) for a, b in pairs for s in range(slabs)]
        return lax.ppermute(value, ("probe", "gx"), every)

    def swap(value, start):
        pairs = [(s, s + 1) for s in range(start, slabs - 1, 2)]
        return lax.ppermute(value, "gx", pairs + [(b, a) for a, b in pairs])

    edge = f32((9, 32, 128))
    edge_a, edge_b = call(
        functools.partial(edge_kernel, width), "edges", [edge, edge], [HBM] * 3, [dma(12)]
    )(wave, stiffness, buoyancy)
    swap_b, swap_a = swap(edge_b, 1), swap(edge_a, 0)

    counts = [1 + len(rest) for rest in NEXT]
    p0, p1, p2, d0, d1, d2 = call(
        functools.partial(split_kernel, width),
        "split",
        [f32((n, *PIECE)) for n in counts] + [f32(PIECE)] * 3,
        [HBM] * 4 + [ANY] * 2,
        [*in_smem(blocks), vmem(2, 2, width + 4, 40, 128), vmem(15, *PIECE), dma(12), dma(6)],
    )(*blocks, wave, swap_a, swap_b)
    firsts = [along_rows(p, [(0, row)]) for p, row in zip((p0, p1, p2), FIRST)]
    directs = [along_rows(d, [(0, row)]) for d, row in zip((d0, d1, d2), DIRECT)]

    advanced, prep = call(
        functools.partial(march_kernel, width),
        "march",
        [f32(wave.shape), f32((4, SPAN, 16, 128))],
        [HBM] * 10 + [ANY] * 2 + [HBM] * 2,
        [
            *in_smem(blocks + sources),
            vmem(2, width + 4, 48, 128),
            vmem(2, width + 2, 32, 128),
            vmem(width + 4, 48, 128),
            vmem(width + 4, 40, 128),
            vmem(2, width + 2, 48, 128),
            vmem(2, width, 32, 128),
            vmem(2, *perts[0].shape),
            vmem(4, SPAN, 16, 128),
            dma(15),
            dma(12),
            dma(5),
        ],
    )(*blocks, *sources, wave, stiffness, buoyancy, swap_a, swap_b, *perts)

    passed = call(pass_kernel, "pass_on", [f32(PIECE)] * 4, [ANY] * 4, [dma(4)])(*firsts, prep)
    nexts = [
        along_rows(value, [(head, rest[n]) for head, rest in zip(FIRST, NEXT) if n < len(rest)])
        for n, value in enumerate(passed)
    ]
    result = call(
        functools.partial(born_kernel, width, width * slabs),
        "born",
        f32(wave.shape),
        [HBM] * 7 + [ANY] * 12,
        [
            *in_smem(blocks + sources),
            vmem(*PIECE),
            vmem(4, SPAN, 16, 128),
            vmem(SPAN, 2, 2, 40, 128),
            dma(7),
            dma(SPAN),
        ],
        input_output_aliases={18: 0},
    )(*blocks, *sources, *firsts, *directs, *nexts, prep, advanced)
    return result[None]


def solution(mesh):
    field = P("probe", None, None, "gx", None, None)
    return jax.shard_map(
        on_device,
        mesh=mesh,
        in_specs=(field, P("gx", None, None), P("gx", None, None)) + (P(),) * 9,
        out_specs=field,
        check_vma=False,
    )
```

time: 372 us -> 39.1 us (0.11)
  the two profiles are of different devices: /device:TPU:24 before, /device:TPU:29 now
where the time goes in v2:
time: 39.1 us; the launch traced here: 38.7 us
  waiting for transfers between devices  14.5 us (37%)
  starting transfers between devices  13.9 us (36%)
  Pallas kernels  10.1 us (26%)
    ppermute x10, waiting for transfers between devices, along_rows(): return lax.ppermute(value, ('probe', 'gx'), every)  11.6 us
    pallas_call x5, Pallas kernels, run(): made(*(keep(x) if spec is HBM else x for x, spec in zip(args, in_specs)))  10.1 us
    ppermute x10, starting transfers between devices, along_rows(): return lax.ppermute(value, ('probe', 'gx'), every)  7.28 us
    ppermute x2, starting transfers between devices, swap(): return lax.ppermute(value, 'gx', pairs + [(b, a) for a, b in pairs])  6.64 us
    ppermute x2, waiting for transfers between devices, swap(): return lax.ppermute(value, 'gx', pairs + [(b, a) for a, b in pairs])  2.91 us
  transfers between devices with their start and end apart: 12, of which 2 were waited for; matrix products, arithmetic and copies ran while one was open for 0% of the time, Pallas kernels for 21%

profile of v2, /device:TPU:29, one launch (start us, length us, event | category | flops | bytes accessed | tf_op | source)
XLA Modules:
  0.0 38.7 jit_solution(1597117070729716069)
XLA Ops:
  0.0 1.0 %edges.1 = (f32[9,32,128]{2,1,0:T(8,128)S(1)}, f32[9,32,128]{2,1,0:T(8,128)S(1)}) custom-call(f32[2,2,24,32,128]{4,3,2,1,0:T(8,128)} %bitcast.4, f32[24,32,128]{2,1,0:T(8,128)} %stiff.3, f32[24,32,128]{2,1,0:T(8,128)} %buoy.3), custom_call_target="tpu_custom_call" | custom-call | tf_op jit(solution)/shard_map/edges/pallas_call | solution.py:419
  1.0 2.4 %collective-permute-start = (f32[9,32,128]{2,1,0:T(8,128)S(1)}, f32[9,32,128]{2,1,0:T(8,128)S(1)}, u32[]{:S(2)}, u32[]{:S(2)}) collective-permute-start(f32[9,32,128]{2,1,0:T(8,128)S(1)} %get-tuple-element.19), channel_id=1, source_target_pairs={{0,1},{2,3},{4,5},{6,7},{8,9},{10,11},{12,13},{14,15},{16,17},{18,... | collective-permute-start | bytes 442376 | tf_op jit(solution)/shard_map/ppermute | solution.py:429
  3.4 4.3 %collective-permute-start.1 = (f32[9,32,128]{2,1,0:T(8,128)S(1)}, f32[9,32,128]{2,1,0:T(8,128)S(1)}, u32[]{:S(2)}, u32[]{:S(2)}) collective-permute-start(f32[9,32,128]{2,1,0:T(8,128)S(1)} %get-tuple-element.20), channel_id=1, source_target_pairs={{1,2},{3,4},{5,6},{7,8},{9,10},{11,12},{13,14},{15,16},{17,18},{19... | collective-permute-start | bytes 442376 | tf_op jit(solution)/shard_map/ppermute | solution.py:429
  7.7 0.0 collective-permute-done.swap_a
  7.7 2.9 %collective-permute-done.1.swap_b = f32[9,32,128]{2,1,0:T(8,128)S(1)} collective-permute-done((f32[9,32,128]{2,1,0:T(8,128)S(1)}, f32[9,32,128]{2,1,0:T(8,128)S(1)}, u32[]{:S(2)}, u32[]{:S(2)}) %collective-permute-start.1) | collective-permute-done | bytes 147488 | tf_op jit(solution)/shard_map/ppermute | solution.py:429
  10.6 0.2 split.1
  10.8 0.7 %collective-permute-start.2 = (f32[5,64,128]{2,1,0:T(8,128)S(1)}, f32[5,64,128]{2,1,0:T(8,128)S(1)}, u32[]{:S(2)}, u32[]{:S(2)}) collective-permute-start(f32[5,64,128]{2,1,0:T(8,128)S(1)} %get-tuple-element.21), channel_id=1, source_target_pairs={{0,32},{1,33},{2,34},{3,35},{4,36},{5,37},{6,38},{7,39},{8,40},{9,... | collective-permute-start | bytes 491528 | tf_op jit(solution)/shard_map/ppermute | solution.py:425
  11.4 0.7 %collective-permute-start.3 = (f32[4,64,128]{2,1,0:T(8,128)S(1)}, f32[4,64,128]{2,1,0:T(8,128)S(1)}, u32[]{:S(2)}, u32[]{:S(2)}) collective-permute-start(f32[4,64,128]{2,1,0:T(8,128)S(1)} %get-tuple-element.22), channel_id=1, source_target_pairs={{0,64},{1,65},{2,66},{3,67},{4,68},{5,69},{6,70},{7,71},{8,72},{9,... | collective-permute-start | bytes 393224 | tf_op jit(solution)/shard_map/ppermute | solution.py:425
  12.1 0.7 %collective-permute-start.4 = (f32[3,64,128]{2,1,0:T(8,128)S(1)}, f32[3,64,128]{2,1,0:T(8,128)S(1)}, u32[]{:S(2)}, u32[]{:S(2)}) collective-permute-start(f32[3,64,128]{2,1,0:T(8,128)S(1)} %get-tuple-element.23), channel_id=1, source_target_pairs={{0,192},{1,193},{2,194},{3,195},{4,196},{5,197},{6,198},{7,199},{8... | collective-permute-start | bytes 294920 | tf_op jit(solution)/shard_map/ppermute | solution.py:425
  12.8 0.7 %collective-permute-start.5 = (f32[64,128]{1,0:T(8,128)S(1)}, f32[64,128]{1,0:T(8,128)S(1)}, u32[]{:S(2)}, u32[]{:S(2)}) collective-permute-start(f32[64,128]{1,0:T(8,128)S(1)} %get-tuple-element.24), channel_id=1, source_target_pairs={{0,256},{1,257},{2,258},{3,259},{4,260},{5,261},{6,262},{7,263},{8... | collective-permute-start | bytes 98312 | tf_op jit(solution)/shard_map/ppermute | solution.py:425
  13.5 0.7 %collective-permute-start.6 = (f32[64,128]{1,0:T(8,128)S(1)}, f32[64,128]{1,0:T(8,128)S(1)}, u32[]{:S(2)}, u32[]{:S(2)}) collective-permute-start(f32[64,128]{1,0:T(8,128)S(1)} %get-tuple-element.25), channel_id=1, source_target_pairs={{0,352},{1,353},{2,354},{3,355},{4,356},{5,357},{6,358},{7,359},{8... | collective-permute-start | bytes 98312 | tf_op jit(solution)/shard_map/ppermute | solution.py:425
  14.1 7.9 %march.1 = (f32[2,2,24,32,128]{4,3,2,1,0:T(8,128)}, f32[4,12,16,128]{3,2,1,0:T(8,128)S(1)}) custom-call(s32[15]{0:T(128)} %xb.5, s32[15]{0:T(128)} %zb.5, s32[15]{0:T(128)} %yb.5, s32[2]{0:T(128)} %sx.3, s32[2]{0:T(128)} %sz.3, s32[2]{0:T(128)} %sy.3, f32[2,2]{1,0:T(2,128)} %wavelet.3, f32[2,2,24,32,128]{4,3,2,1,0:T(8,128)} %bitcast.6, ...), custom_call_target="tpu_custom_call" | custom-call | tf_op jit(solution)/shard_map/march/pallas_call | solution.py:419
  22.0 0.0 collective-permute-done.4.r2
  22.0 1.3 %collective-permute-start.7 = (f32[64,128]{1,0:T(8,128)S(1)}, f32[64,128]{1,0:T(8,128)S(1)}, u32[]{:S(2)}, u32[]{:S(2)}) collective-permute-start(f32[64,128]{1,0:T(8,128)S(1)} %get-tuple-element.26), channel_id=1, source_target_pairs={{0,416},{1,417},{2,418},{3,419},{4,420},{5,421},{6,422},{7,423},{8... | collective-permute-start | bytes 98312 | tf_op jit(solution)/shard_map/ppermute | solution.py:425
  23.3 0.0 collective-permute-done.2.r0
  23.4 0.1 pass_on.1
  23.4 0.7 %collective-permute-start.8 = (f32[64,128]{1,0:T(8,128)S(1)}, f32[64,128]{1,0:T(8,128)S(1)}, u32[]{:S(2)}, u32[]{:S(2)}) collective-permute-start(f32[64,128]{1,0:T(8,128)S(1)} %get-tuple-element.28), channel_id=1, source_target_pairs={{32,288},{33,289},{34,290},{35,291},{36,292},{37,293},{38,294},{39... | collective-permute-start | bytes 98312 | tf_op jit(solution)/shard_map/ppermute | solution.py:425
  24.1 0.7 %collective-permute-start.9 = (f32[64,128]{1,0:T(8,128)S(1)}, f32[64,128]{1,0:T(8,128)S(1)}, u32[]{:S(2)}, u32[]{:S(2)}) collective-permute-start(f32[64,128]{1,0:T(8,128)S(1)} %get-tuple-element.29), channel_id=1, source_target_pairs={{32,96},{33,97},{34,98},{35,99},{36,100},{37,101},{38,102},{39,103... | collective-permute-start | bytes 98312 | tf_op jit(solution)/shard_map/ppermute | solution.py:425
  24.8 0.7 %collective-permute-start.10 = (f32[64,128]{1,0:T(8,128)S(1)}, f32[64,128]{1,0:T(8,128)S(1)}, u32[]{:S(2)}, u32[]{:S(2)}) collective-permute-start(f32[64,128]{1,0:T(8,128)S(1)} %get-tuple-element.30), channel_id=1, source_target_pairs={{32,224},{33,225},{34,226},{35,227},{36,228},{37,229},{38,230},{39... | collective-permute-start | bytes 98312 | tf_op jit(solution)/shard_map/ppermute | solution.py:425
  25.5 0.7 %collective-permute-start.11 = (f32[64,128]{1,0:T(8,128)S(1)}, f32[64,128]{1,0:T(8,128)S(1)}, u32[]{:S(2)}, u32[]{:S(2)}) collective-permute-start(f32[64,128]{1,0:T(8,128)S(1)} %get-tuple-element.31), channel_id=1, source_target_pairs={{32,160},{33,161},{34,162},{35,163},{36,164},{37,165},{38,166},{39... | collective-permute-start | bytes 98312 | tf_op jit(solution)/shard_map/ppermute | solution.py:425
  26.1 11.6 %collective-permute-done.7.d2 = f32[64,128]{1,0:T(8,128)S(1)} collective-permute-done((f32[64,128]{1,0:T(8,128)S(1)}, f32[64,128]{1,0:T(8,128)S(1)}, u32[]{:S(2)}, u32[]{:S(2)}) %collective-permute-start.7) | collective-permute-done | bytes 32800 | tf_op jit(solution)/shard_map/ppermute | solution.py:425
  37.7 0.0 collective-permute-done.9.q1
  37.7 0.0 collective-permute-done.10.q2
  37.7 0.9 %born.1 = f32[2,2,24,32,128]{4,3,2,1,0:T(8,128)} custom-call(s32[15]{0:T(128)} %xb.5, s32[15]{0:T(128)} %zb.5, s32[15]{0:T(128)} %yb.5, s32[2]{0:T(128)} %sx.3, s32[2]{0:T(128)} %sz.3, s32[2]{0:T(128)} %sy.3, f32[2,2]{1,0:T(2,128)} %wavelet.3, f32[5,64,128]{2,1,0:T(8,128)S(1)} %collective-permute-done.2.r0, ...), custom_call_target="tpu_custom_call", output_to_operand_aliasing={{}: (18, {})} | custom-call | tf_op jit(solution)/shard_map/born/pallas_call | solution.py:419
  (5 shorter events, 0.0 us)
Async XLA Ops:
  1.0 6.7 %collective-permute-start = (f32[9,32,128]{2,1,0:T(8,128)S(1)}, f32[9,32,128]{2,1,0:T(8,128)S(1)}, u32[]{:S(2)}, u32[]{:S(2)}) collective-permute-start(f32[9,32,128]{2,1,0:T(8,128)S(1)} %get-tuple-element.19), channel_id=1, source_target_pairs={{0,1},{2,3},{4,5},{6,7},{8,9},{10,11},{12,13},{14,15},{16,17},{18,... | collective-permute-start | bytes 442376 | tf_op jit(solution)/shard_map/ppermute | solution.py:429
  3.4 7.2 %collective-permute-start.1 = (f32[9,32,128]{2,1,0:T(8,128)S(1)}, f32[9,32,128]{2,1,0:T(8,128)S(1)}, u32[]{:S(2)}, u32[]{:S(2)}) collective-permute-start(f32[9,32,128]{2,1,0:T(8,128)S(1)} %get-tuple-element.20), channel_id=1, source_target_pairs={{1,2},{3,4},{5,6},{7,8},{9,10},{11,12},{13,14},{15,16},{17,18},{19... | collective-permute-start | bytes 442376 | tf_op jit(solution)/shard_map/ppermute | solution.py:429
  10.8 12.6 %collective-permute-start.2 = (f32[5,64,128]{2,1,0:T(8,128)S(1)}, f32[5,64,128]{2,1,0:T(8,128)S(1)}, u32[]{:S(2)}, u32[]{:S(2)}) collective-permute-start(f32[5,64,128]{2,1,0:T(8,128)S(1)} %get-tuple-element.21), channel_id=1, source_target_pairs={{0,32},{1,33},{2,34},{3,35},{4,36},{5,37},{6,38},{7,39},{8,40},{9,... | collective-permute-start | bytes 491528 | tf_op jit(solution)/shard_map/ppermute | solution.py:425
  11.4 11.9 %collective-permute-start.3 = (f32[4,64,128]{2,1,0:T(8,128)S(1)}, f32[4,64,128]{2,1,0:T(8,128)S(1)}, u32[]{:S(2)}, u32[]{:S(2)}) collective-permute-start(f32[4,64,128]{2,1,0:T(8,128)S(1)} %get-tuple-element.22), channel_id=1, source_target_pairs={{0,64},{1,65},{2,66},{3,67},{4,68},{5,69},{6,70},{7,71},{8,72},{9,... | collective-permute-start | bytes 393224 | tf_op jit(solution)/shard_map/ppermute | solution.py:425
  12.1 9.9 %collective-permute-start.4 = (f32[3,64,128]{2,1,0:T(8,128)S(1)}, f32[3,64,128]{2,1,0:T(8,128)S(1)}, u32[]{:S(2)}, u32[]{:S(2)}) collective-permute-start(f32[3,64,128]{2,1,0:T(8,128)S(1)} %get-tuple-element.23), channel_id=1, source_target_pairs={{0,192},{1,193},{2,194},{3,195},{4,196},{5,197},{6,198},{7,199},{8... | collective-permute-start | bytes 294920 | tf_op jit(solution)/shard_map/ppermute | solution.py:425
  12.8 12.0 %collective-permute-start.5 = (f32[64,128]{1,0:T(8,128)S(1)}, f32[64,128]{1,0:T(8,128)S(1)}, u32[]{:S(2)}, u32[]{:S(2)}) collective-permute-start(f32[64,128]{1,0:T(8,128)S(1)} %get-tuple-element.24), channel_id=1, source_target_pairs={{0,256},{1,257},{2,258},{3,259},{4,260},{5,261},{6,262},{7,263},{8... | collective-permute-start | bytes 98312 | tf_op jit(solution)/shard_map/ppermute | solution.py:425
  13.5 12.0 %collective-permute-start.6 = (f32[64,128]{1,0:T(8,128)S(1)}, f32[64,128]{1,0:T(8,128)S(1)}, u32[]{:S(2)}, u32[]{:S(2)}) collective-permute-start(f32[64,128]{1,0:T(8,128)S(1)} %get-tuple-element.25), channel_id=1, source_target_pairs={{0,352},{1,353},{2,354},{3,355},{4,356},{5,357},{6,358},{7,359},{8... | collective-permute-start | bytes 98312 | tf_op jit(solution)/shard_map/ppermute | solution.py:425
  22.0 15.7 %collective-permute-start.7 = (f32[64,128]{1,0:T(8,128)S(1)}, f32[64,128]{1,0:T(8,128)S(1)}, u32[]{:S(2)}, u32[]{:S(2)}) collective-permute-start(f32[64,128]{1,0:T(8,128)S(1)} %get-tuple-element.26), channel_id=1, source_target_pairs={{0,416},{1,417},{2,418},{3,419},{4,420},{5,421},{6,422},{7,423},{8... | collective-permute-start | bytes 98312 | tf_op jit(solution)/shard_map/ppermute | solution.py:425
  23.4 14.3 %collective-permute-start.8 = (f32[64,128]{1,0:T(8,128)S(1)}, f32[64,128]{1,0:T(8,128)S(1)}, u32[]{:S(2)}, u32[]{:S(2)}) collective-permute-start(f32[64,128]{1,0:T(8,128)S(1)} %get-tuple-element.28), channel_id=1, source_target_pairs={{32,288},{33,289},{34,290},{35,291},{36,292},{37,293},{38,294},{39... | collective-permute-start | bytes 98312 | tf_op jit(solution)/shard_map/ppermute | solution.py:425
  24.1 13.6 %collective-permute-start.9 = (f32[64,128]{1,0:T(8,128)S(1)}, f32[64,128]{1,0:T(8,128)S(1)}, u32[]{:S(2)}, u32[]{:S(2)}) collective-permute-start(f32[64,128]{1,0:T(8,128)S(1)} %get-tuple-element.29), channel_id=1, source_target_pairs={{32,96},{33,97},{34,98},{35,99},{36,100},{37,101},{38,102},{39,103... | collective-permute-start | bytes 98312 | tf_op jit(solution)/shard_map/ppermute | solution.py:425
  24.8 12.9 %collective-permute-start.10 = (f32[64,128]{1,0:T(8,128)S(1)}, f32[64,128]{1,0:T(8,128)S(1)}, u32[]{:S(2)}, u32[]{:S(2)}) collective-permute-start(f32[64,128]{1,0:T(8,128)S(1)} %get-tuple-element.30), channel_id=1, source_target_pairs={{32,224},{33,225},{34,226},{35,227},{36,228},{37,229},{38,230},{39... | collective-permute-start | bytes 98312 | tf_op jit(solution)/shard_map/ppermute | solution.py:425
  25.5 12.3 %collective-permute-start.11 = (f32[64,128]{1,0:T(8,128)S(1)}, f32[64,128]{1,0:T(8,128)S(1)}, u32[]{:S(2)}, u32[]{:S(2)}) collective-permute-start(f32[64,128]{1,0:T(8,128)S(1)} %get-tuple-element.31), channel_id=1, source_target_pairs={{32,160},{33,161},{34,162},{35,163},{36,164},{37,165},{38,166},{39... | collective-permute-start | bytes 98312 | tf_op jit(solution)/shard_map/ppermute | solution.py:425

commit v3 on v0

v3 whole, which is shorter than its diff:
```python
import functools

import jax
import jax.numpy as jnp
from jax import lax
from jax.experimental import pallas as pl
from jax.experimental.pallas import tpu as pltpu
from jax.sharding import PartitionSpec as P

EDGE = 8
SPAN = EDGE + 4
DEPTH = 32
PER_ROW = 10
STRIPS = [(s, 1, i) for s in range(2) for i in range(SPAN)] + [
    (s, 0, i) for s in range(2) for i in range(1, SPAN - 1)
]
ROWS = 64

FIRST = (1, 2, 6, 8)
NEXT = ((9, 3, 7, 5), (10, 4, 12), (14, 15), (11,))
DIRECT = (13,)

PARAMS = pltpu.CompilerParams(vmem_limit_bytes=32 * 1024 * 1024)


def copy_all(pairs, sems, start=0):
    copies = [pltpu.make_async_copy(a, b, sems.at[start + n]) for n, (a, b) in enumerate(pairs)]
    for copy in copies:
        copy.start()
    return copies


def wait_all(copies):
    for copy in copies:
        copy.wait()


def wrapped(shift):
    return jnp.bitwise_and(shift + 128, 127)


def plane_rows(p, count=1):
    start = p * DEPTH
    return pl.ds(start if isinstance(p, int) else pl.multiple_of(start, DEPTH), count * DEPTH)


def window(blocks, g, first):
    xb, zb, yb = blocks
    return xb[g] * EDGE - 2 - first, jnp.clip(zb[g] * EDGE - 2, 0, DEPTH - SPAN), yb[g] * EDGE - 2


def met(x0, width):
    return (x0 < width) & (x0 + SPAN > 0)


def from_sides(swap_a, swap_b, act):
    even = lax.rem(lax.axis_index("gx"), 2) == 0

    @pl.when(even)
    def _():
        act(swap_b, swap_a)

    @pl.when(jnp.logical_not(even))
    def _():
        act(swap_a, swap_b)


def edge_kernel(width, wave, stiff, buoy, swap_a, swap_b, sem):
    def pack(low, high):
        pairs = []
        for out, outer, inner in ((low, 0, 0), (high, width - 1, width - 2)):
            for s in range(2):
                pairs.append((wave.at[s, 1, plane_rows(inner, 2)], out.at[plane_rows(2 * s, 2)]))
                pairs.append((wave.at[s, 0, plane_rows(outer)], out.at[plane_rows(4 + s)]))
            pairs.append((buoy.at[plane_rows(inner, 2)], out.at[plane_rows(6, 2)]))
            pairs.append((stiff.at[plane_rows(outer)], out.at[plane_rows(8)]))
        wait_all(copy_all(pairs, sem))

    from_sides(swap_a, swap_b, pack)


def keep_sides(swap_a, swap_b, sides):
    def act(below, above):
        sides[0] = below[...]
        sides[1] = above[...]

    from_sides(swap_a, swap_b, act)


def split_kernel(width, xb, zb, yb, wave, swap_a, swap_b, *refs):
    outs, sides = refs[:-1], refs[-1]
    packs = [(head, *rest) for head, rest in zip(FIRST, NEXT)] + [(row,) for row in DIRECT]

    @pl.when(lax.axis_index("probe") == 0)
    def _():
        first = lax.axis_index("gx") * width
        keep_sides(swap_a, swap_b, sides)
        lane = lax.broadcasted_iota(jnp.int32, (8, 128), 1)

        def cut(g, out, at):
            x0, z0, y0 = window((xb, zb, yb), g, first)

            def place(n, load):
                k, q = divmod(n, PER_ROW)
                for half in (0, SPAN - 8):
                    spot = pl.ds(at * ROWS + k * SPAN + half, 8)
                    values = pltpu.roll(load(half), wrapped(SPAN * q - y0), 1)
                    mine = (lane >= SPAN * q) & (lane < SPAN * (q + 1))
                    out[spot, :] = jnp.where(mine, values, out[spot, :])

            @pl.when(met(x0, width))
            def _():
                for i in range(SPAN):
                    p = x0 + i
                    strips = [(n, s, t) for n, (s, t, j) in enumerate(STRIPS) if j == i]

                    @pl.when((p >= 0) & (p < width))
                    def _():
                        for n, s, t in strips:
                            place(n, lambda half: wave[s, t, pl.ds(p * DEPTH + z0 + half, 8), :])

                    @pl.when(((p >= -2) & (p < 0)) | ((p >= width) & (p < width + 2)))
                    def _():
                        side = jnp.where(p < 0, 0, 1)
                        j = jnp.where(p < 0, p + 2, p - width)
                        for n, s, t in strips:
                            top = (2 * s + j if t else 4 + s) * DEPTH + z0
                            place(n, lambda half: sides[side, pl.ds(top + half, 8), :])

        for out, members in zip(outs, packs):

            def each(at, carry):
                row = jnp.int32(members[0])
                for n, member in enumerate(members[1:], 1):
                    row = jnp.where(at == n, member, row)
                cut(row - 1, out, at)
                return carry

            lax.fori_loop(0, len(members), each, 0)


def pass_kernel(*refs):
    got, outs = refs[: len(FIRST)], refs[len(FIRST) + 1 :]
    row = lax.axis_index("probe")
    for head, rest, source in zip(FIRST, NEXT, got):

        @pl.when(row == head)
        def _():
            for n, out in zip(range(len(rest)), outs):
                out[...] = source[pl.ds((1 + n) * ROWS, ROWS), :]


def march_kernel(
    width, xb, zb, yb, sx, sz, sy, wavelet, wave, stiff, buoy, swap_a, swap_b, pstiff, pbuoy, out, prep, fields,
    sides, mid, later, weights, sem_out,
):
    first = lax.axis_index("gx") * width
    row = lax.axis_index("probe")
    keep_sides(swap_a, swap_b, sides)
    lane = lax.broadcasted_iota(jnp.int32, (DEPTH, 128), 1)
    depth = lax.broadcasted_iota(jnp.int32, (DEPTH, 128), 0)
    top, bottom = depth == 0, depth == DEPTH - 1
    left, right = lane == 0, lane == 127

    def present(s, p):
        if isinstance(p, int) and p < 0:
            return sides[0, plane_rows(2 * s + p + 2), :]
        if isinstance(p, int) and p >= width:
            return sides[1, plane_rows(2 * s + p - width), :]
        return wave[s, 1, plane_rows(p), :]

    def earlier(s, p):
        if isinstance(p, int) and (p < 0 or p >= width):
            return sides[0 if p < 0 else 1, plane_rows(4 + s), :]
        return wave[s, 0, plane_rows(p), :]

    def coefficients(p):
        if isinstance(p, int) and (p < 0 or p >= width):
            side = 0 if p < 0 else 1
            return sides[side, plane_rows(6 + (p + 2 if p < 0 else p - width)), :], sides[side, plane_rows(8), :]
        return buoy[plane_rows(p), :], stiff[plane_rows(p), :]

    def weigh(c, cxm, cxp, czm, czp, k):
        k = 0.5 * k
        edge = k * c
        wide = [k * (c + cxm), k * (c + cxp)]
        total = wide[0] + wide[1]
        for value, outside in (
            (czm, top),
            (czp, bottom),
            (pltpu.roll(c, 1, 1), left),
            (pltpu.roll(c, 127, 1), right),
        ):
            full = k * (c + value)
            total += jnp.where(outside, edge, full)
            wide.append(jnp.where(outside, 0.0, full))
        return wide + [2.0 - total]

    def weighted(w, v, vxm, vxp, vzm, vzp, before):
        near = (w[0] * vxm + w[1] * vxp) + (w[2] * vzm + w[3] * vzp)
        near += w[4] * pltpu.roll(v, 1, 1) + w[5] * pltpu.roll(v, 127, 1)
        return (w[6] * v - before) + near

    def save(w, p):
        for n in range(7):
            weights[n, plane_rows(p), :] = w[n]

    def up(v):
        return pltpu.roll(v, 1, 0)

    def down(v):
        return pltpu.roll(v, DEPTH - 1, 0)

    for p in (-1, 0, width - 1, width):
        c, k = coefficients(p)
        w = weigh(c, coefficients(p - 1)[0], coefficients(p + 1)[0], up(c), down(c), k)
        if 0 <= p < width:
            save(w, p)
        for s in range(2):
            v = present(s, p)
            mid[s, plane_rows(p + 1), :] = weighted(
                w, v, present(s, p - 1), present(s, p + 1), up(v), down(v), earlier(s, p)
            )

    def step_one(p, carry):
        above, below = pl.ds(p * DEPTH - 1, DEPTH), pl.ds(p * DEPTH + 1, DEPTH)
        c, k = coefficients(p)
        w = weigh(c, buoy[plane_rows(p - 1), :], buoy[plane_rows(p + 1), :], buoy[above, :], buoy[below, :], k)
        save(w, p)
        for s in range(2):
            mid[s, plane_rows(p + 1), :] = weighted(
                w, present(s, p), present(s, p - 1), present(s, p + 1), wave[s, 1, above, :], wave[s, 1, below, :],
                earlier(s, p),
            )
        return carry

    lax.fori_loop(1, width - 1, step_one, 0)

    def inject(ref, step, low, high, shift):
        for s in range(2):
            x = sx[s] - first

            @pl.when((row == 0) & (x >= low) & (x < high))
            def _():
                hit = (lane == sy[s]) & (depth == sz[s])
                spot = plane_rows(x + shift)
                ref[s, spot, :] = ref[s, spot, :] + jnp.where(hit, wavelet[s, step], 0.0)

    inject(mid, 0, -1, width + 1, 1)
    outs = copy_all([(mid.at[s, plane_rows(1, width)], out.at[s, 0]) for s in range(2)], sem_out)

    def step_two(p, carry):
        above, below = pl.ds((p + 1) * DEPTH - 1, DEPTH), pl.ds((p + 1) * DEPTH + 1, DEPTH)
        w = [weights[n, plane_rows(p), :] for n in range(7)]
        for s in range(2):
            later[s, plane_rows(p), :] = weighted(
                w, mid[s, plane_rows(p + 1), :], mid[s, plane_rows(p), :], mid[s, plane_rows(p + 2), :],
                mid[s, above, :], mid[s, below, :], present(s, p),
            )
        return carry

    part = width // 3
    for n in range(3):
        low, high = n * part, (n + 1) * part
        lax.fori_loop(low, high, step_two, 0)
        inject(later, 1, low, high, 0)
        pairs = [(later.at[s, plane_rows(low, part)], out.at[s, 1, plane_rows(low, part)]) for s in range(2)]
        outs += copy_all(pairs, sem_out, 2 + 2 * n)

    g = jnp.maximum(row - 1, 0)
    x0, z0, y0 = window((xb, zb, yb), g, first)

    @pl.when((row > 0) & met(x0, width))
    def _():
        strip = lax.broadcasted_iota(jnp.int32, (8, 128), 1)
        here = (strip < SPAN) & (strip + y0 >= 0) & (strip + y0 < 128)
        prep[...] = jnp.zeros(prep.shape, jnp.float32)

        def bring(n, i, load):
            for half in (0, SPAN - 8):
                prep[n, i, pl.ds(half, 8), :] = jnp.where(here, pltpu.roll(load(half), wrapped(-y0), 1), 0.0)

        for i in range(SPAN):
            p = x0 + i

            @pl.when((p >= 0) & (p < width))
            def _():
                bring(0, i, lambda half: buoy[pl.ds(p * DEPTH + z0 + half, 8), :])
                bring(1, i, lambda half: stiff[pl.ds(p * DEPTH + z0 + half, 8), :])
                for s in range(2):
                    fields[i, s, 0] = mid[s, plane_rows(p + 1), :]
                    fields[i, s, 1] = later[s, plane_rows(p), :]

            side = jnp.where(p < 0, 0, 1)
            j = jnp.where(p < 0, p + 2, p - width)

            @pl.when(((p >= -2) & (p < 0)) | ((p >= width) & (p < width + 2)))
            def _():
                bring(0, i, lambda half: sides[side, pl.ds((6 + j) * DEPTH + z0 + half, 8), :])

            @pl.when((p == -1) | (p == width))
            def _():
                bring(1, i, lambda half: sides[side, pl.ds(8 * DEPTH + z0 + half, 8), :])

        wide = lax.broadcasted_iota(jnp.int32, (EDGE, EDGE, pstiff.shape[-1]), 2)
        diagonal = lax.broadcasted_iota(jnp.int32, (EDGE, EDGE, 128), 2)
        diagonal = diagonal == lax.broadcasted_iota(jnp.int32, (EDGE, EDGE, 128), 1) + 2
        dz = zb[g] * EDGE - z0
        for n, ref in ((2, pstiff), (3, pbuoy)):
            for i in range(EDGE):
                column = jnp.sum(jnp.where(wide == g, ref[i], 0.0), axis=2, keepdims=True)
                prep[n, 2 + i, pl.ds(dz, EDGE), :] = jnp.sum(jnp.where(diagonal, column, 0.0), axis=1)

    wait_all(outs)


def born_kernel(width, extent, xb, zb, yb, sx, sz, sy, wavelet, *refs):
    count = len(FIRST) + len(DIRECT)
    longest = max(len(rest) for rest in NEXT)
    firsts, directs, nexts = refs[: len(FIRST)], refs[len(FIRST) : count], refs[count : count + longest]
    prep, fields, _, out, piece, planes, sem = refs[count + longest :]
    row = lax.axis_index("probe")
    g = jnp.maximum(row - 1, 0)
    first = lax.axis_index("gx") * width
    x0, z0, y0 = window((xb, zb, yb), g, first)

    @pl.when((row > 0) & met(x0, width))
    def _():
        def bring(where, source):
            @pl.when(where)
            def _():
                piece[...] = source[pl.ds(0, ROWS), :]

        for target, source in zip(FIRST + DIRECT, (*firsts, *directs)):
            bring(row == target, source)
        for n, source in enumerate(nexts):
            where = row < 0
            for rest in NEXT:
                if n < len(rest):
                    where = where | (row == rest[n])
            bring(where, source)

        lane = lax.broadcasted_iota(jnp.int32, (16, 128), 1)
        depth = lax.broadcasted_iota(jnp.int32, (16, 128), 0)
        here = (lane < SPAN) & (depth < SPAN) & (lane + y0 >= 0) & (lane + y0 < 128)
        c, k, sb, bb = (prep[n] for n in range(4))

        def field(s, t):
            got = []
            for i in range(SPAN):
                if (s, t, i) not in STRIPS:
                    got.append(jnp.zeros((16, 128), jnp.float32))
                    continue
                at, q = divmod(STRIPS.index((s, t, i)), PER_ROW)
                values = piece[pl.ds(at * SPAN, 16), :]
                if q:
                    values = pltpu.roll(values, 128 - SPAN * q, 1)
                x = x0 + i
                ok = (first + x >= 0) & (first + x < extent) & (x >= -1 - t) & (x < width + 1 + t)
                got.append(jnp.where(here & ok, values, 0.0))
            return jnp.stack(got)

        def up(v, axis):
            return pltpu.roll(v, v.shape[axis] - 1, axis)

        def faces(coef):
            return 0.5 * (coef[1:] + coef[:-1]), 0.5 * (coef + up(coef, 1)), 0.5 * (coef + up(coef, 2))

        def steps(v):
            return v[1:] - v[:-1], up(v, 1) - v, up(v, 2) - v

        def gather(coef, step):
            fx, fz, fy = (a * b for a, b in zip(coef, step))
            zero = jnp.zeros((1, 16, 128), jnp.float32)
            total = jnp.concatenate([fx, zero], 0) - jnp.concatenate([zero, fx], 0)
            total += fz - pltpu.roll(fz, 1, 1)
            total += fy - pltpu.roll(fy, 1, 2)
            return total

        of_c = faces(c)
        of_b = faces(bb)
        for s in range(2):
            now = field(s, 1)
            step = steps(now)
            laplace = gather(of_c, step)
            forcing = sb * laplace + k * gather(of_b, step)
            hit = here & (lane + y0 == sy[s]) & (depth + z0 == sz[s])
            source = []
            for i in range(SPAN):
                on = hit & (first + x0 + i == sx[s])
                source.append(jnp.where(on, wavelet[s, 0], 0.0))
            then = steps(2.0 * now - field(s, 0) + k * laplace + jnp.stack(source))
            second = sb * gather(of_c, then) + k * gather(of_b, then)
            gains = (forcing, 2.0 * forcing + k * gather(of_c, steps(forcing)) + second)
            for t in range(2):
                moved = pltpu.roll(gains[t], wrapped(y0), 2)
                for i in range(SPAN):
                    planes[i, s, t, pl.ds(0, DEPTH), :] = fields[i, s, t]
                    spot = pl.ds(z0, 16)
                    planes[i, s, t, spot, :] = planes[i, s, t, spot, :] + moved[i]

        def each_plane(act):
            for i in range(SPAN):

                @pl.when((x0 + i >= 0) & (x0 + i < width))
                def _():
                    target = out.at[:, :, plane_rows(x0 + i)]
                    act(pltpu.make_async_copy(planes.at[i, :, :, pl.ds(0, DEPTH)], target, sem.at[i]))

        each_plane(lambda copy: copy.start())
        each_plane(lambda copy: copy.wait())


def on_device(
    wavefields, stiffness, buoyancy, pert_stiffness, pert_buoyancy, xblock_index, zblock_index, yblock_index,
    source_xcell, source_zcell, source_ycell, wavelet
):
    width = wavefields.shape[3]
    slabs = lax.axis_size("gx")
    rows = width * DEPTH
    wave = wavefields.reshape(2, 2, rows, 128)
    stiff, buoy = stiffness.reshape(rows, 128), buoyancy.reshape(rows, 128)
    blocks = (xblock_index, zblock_index, yblock_index)
    sources = (source_xcell, source_zcell, source_ycell, wavelet)
    perts = [jnp.transpose(p, (1, 2, 3, 0)) for p in (pert_stiffness, pert_buoyancy)]
    hbm = lambda *shape: pltpu.HBM(shape, jnp.float32)
    vmem = lambda *shape: pltpu.VMEM(shape, jnp.float32)
    dma = lambda *shape: pltpu.SemaphoreType.DMA(shape)

    def call(kernel, name, out_shape, spaces, scratch, **more):
        made = pl.pallas_call(
            kernel,
            out_shape=out_shape,
            in_specs=[pl.BlockSpec(memory_space=space) for space in spaces],
            out_specs=jax.tree.map(lambda s: pl.BlockSpec(memory_space=s.memory_space), out_shape),
            scratch_shapes=scratch,
            compiler_params=PARAMS,
            name=name,
            **more,
        )
        return lambda *args: made(*map(pltpu.with_memory_space_constraint, args, spaces))

    def along_rows(value, pairs):
        every = [(a * slabs + s, b * slabs + s) for a, b in pairs for s in range(slabs)]
        return lax.ppermute(value, ("probe", "gx"), every)

    def swap(value, start):
        pairs = [(s, s + 1) for s in range(start, slabs - 1, 2)]
        return lax.ppermute(value, "gx", pairs + [(b, a) for a, b in pairs])

    smem = pltpu.SMEM
    edge = vmem(9 * DEPTH, 128)
    edge_a, edge_b = call(
        functools.partial(edge_kernel, width), "edges", [edge, edge], [pltpu.HBM] * 3, [dma(12)]
    )(wave, stiff, buoy)
    swap_a, swap_b = swap(edge_a, 0), swap(edge_b, 1)

    counts = [1 + len(rest) for rest in NEXT] + [1] * len(DIRECT)
    packs = call(
        functools.partial(split_kernel, width),
        "split",
        [vmem(n * ROWS, 128) for n in counts],
        [smem] * 3 + [pltpu.VMEM] * 3,
        [vmem(2, 9 * DEPTH, 128)],
    )(*blocks, wave, swap_a, swap_b)
    got = [along_rows(p, [(0, row)]) for p, row in zip(packs, FIRST + DIRECT)]

    advanced, prep, fields = call(
        functools.partial(march_kernel, width),
        "march",
        [hbm(2, 2, rows, 128), vmem(4, SPAN, 16, 128), vmem(SPAN, 2, 2, DEPTH, 128)],
        [smem] * 7 + [pltpu.VMEM] * 7,
        [
            vmem(2, 9 * DEPTH, 128),
            vmem(2, (width + 2) * DEPTH, 128),
            vmem(2, rows, 128),
            vmem(7, rows, 128),
            dma(8),
        ],
    )(*blocks, *sources, wave, stiff, buoy, swap_a, swap_b, *perts)

    longest = max(len(rest) for rest in NEXT)
    passed = call(
        pass_kernel, "pass_on", [vmem(ROWS, 128)] * longest, [pltpu.VMEM] * (len(FIRST) + 1), []
    )(*got[: len(FIRST)], prep)
    nexts = [
        along_rows(value, [(head, rest[n]) for head, rest in zip(FIRST, NEXT) if n < len(rest)])
        for n, value in enumerate(passed)
    ]
    operands = (*blocks, *sources, *got, *nexts, prep, fields, advanced)
    result = call(
        functools.partial(born_kernel, width, width * slabs),
        "born",
        hbm(2, 2, rows, 128),
        [smem] * 7 + [pltpu.VMEM] * (len(operands) - 8) + [pltpu.HBM],
        [vmem(ROWS, 128), vmem(SPAN, 2, 2, DEPTH + 8, 128), dma(SPAN)],
        input_output_aliases={len(operands) - 1: 0},
    )(*operands)
    return result.reshape(wavefields.shape)


def solution(mesh):
    field = P("probe", None, None, "gx", None, None)
    return jax.shard_map(
        on_device,
        mesh=mesh,
        in_specs=(field, P("gx", None, None), P("gx", None, None)) + (P(),) * 9,
        out_specs=field,
        check_vma=False,
    )
```

time: 372 us -> 36 us (0.10)
  the two profiles are of different devices: /device:TPU:24 before, /device:TPU:389 now
where the time goes in v3:
time: 36 us; the launch traced here: 35.7 us
  starting transfers between devices  13.6 us (38%)
  waiting for transfers between devices  11.4 us (32%)
  Pallas kernels  10.4 us (29%)
    pallas_call x5, Pallas kernels, call(): made(*map(pltpu.with_memory_space_constraint, args, spaces))  10.4 us
    ppermute x2, starting transfers between devices, swap(): return lax.ppermute(value, 'gx', pairs + [(b, a) for a, b in pairs])  6.94 us
    ppermute x9, waiting for transfers between devices, along_rows(): return lax.ppermute(value, ('probe', 'gx'), every)  6.71 us
    ppermute x9, starting transfers between devices, along_rows(): return lax.ppermute(value, ('probe', 'gx'), every)  6.62 us
    ppermute x2, waiting for transfers between devices, swap(): return lax.ppermute(value, 'gx', pairs + [(b, a) for a, b in pairs])  4.68 us
  transfers between devices with their start and end apart: 11, of which 2 were waited for; matrix products, arithmetic and copies ran while one was open for 0% of the time, Pallas kernels for 17%

profile of v3, /device:TPU:389, one launch (start us, length us, event | category | flops | bytes accessed | tf_op | source)
XLA Modules:
  0.0 35.7 jit_solution(115087271827644921)
XLA Ops:
  0.1 1.1 %edges.1 = (f32[288,128]{1,0:T(8,128)S(1)}, f32[288,128]{1,0:T(8,128)S(1)}) custom-call(f32[2,2,768,128]{3,2,1,0:T(8,128)} %bitcast.6, f32[768,128]{1,0:T(8,128)} %bitcast.9, f32[768,128]{1,0:T(8,128)} %bitcast.11), custom_call_target="tpu_custom_call" | custom-call | tf_op jit(solution)/shard_map/edges/pallas_call | solution.py:441
  1.2 3.2 %collective-permute-start = (f32[288,128]{1,0:T(8,128)S(1)}, f32[288,128]{1,0:T(8,128)S(1)}, u32[]{:S(2)}, u32[]{:S(2)}) collective-permute-start(f32[288,128]{1,0:T(8,128)S(1)} %get-tuple-element.19), channel_id=1, source_target_pairs={{0,1},{2,3},{4,5},{6,7},{8,9},{10,11},{12,13},{14,15},{16,17},{18,... | collective-permute-start | bytes 442376 | tf_op jit(solution)/shard_map/ppermute | solution.py:449
  4.5 3.7 %collective-permute-start.1 = (f32[288,128]{1,0:T(8,128)S(1)}, f32[288,128]{1,0:T(8,128)S(1)}, u32[]{:S(2)}, u32[]{:S(2)}) collective-permute-start(f32[288,128]{1,0:T(8,128)S(1)} %get-tuple-element.20), channel_id=1, source_target_pairs={{1,2},{3,4},{5,6},{7,8},{9,10},{11,12},{13,14},{15,16},{17,18},{19... | collective-permute-start | bytes 442376 | tf_op jit(solution)/shard_map/ppermute | solution.py:449
  8.2 0.0 collective-permute-done.swap_a
  8.2 4.7 %collective-permute-done.1.swap_b = f32[288,128]{1,0:T(8,128)S(1)} collective-permute-done((f32[288,128]{1,0:T(8,128)S(1)}, f32[288,128]{1,0:T(8,128)S(1)}, u32[]{:S(2)}, u32[]{:S(2)}) %collective-permute-start.1) | collective-permute-done | bytes 147488 | tf_op jit(solution)/shard_map/ppermute | solution.py:449
  12.9 0.6 %split.1 = (f32[320,128]{1,0:T(8,128)S(1)}, f32[256,128]{1,0:T(8,128)S(1)}, f32[192,128]{1,0:T(8,128)S(1)}, f32[128,128]{1,0:T(8,128)S(1)}, f32[64,128]{1,0:T(8,128)S(1)}) custom-call(s32[15]{0:T(128)S(1)} %copy-done.5, s32[15]{0:T(128)S(1)} %copy-done.6, s32[15]{0:T(128)S(1)} %copy-done.7, f32[2,2,768,128]{3,2,1,0:T(8,128)S(1)} %bitcast.7, ...), custom_call_target="tpu_custom_call" | custom-call | tf_op jit(solution)/shard_map/split/pallas_call | solution.py:441
  13.5 0.7 %collective-permute-start.2 = (f32[320,128]{1,0:T(8,128)S(1)}, f32[320,128]{1,0:T(8,128)S(1)}, u32[]{:S(2)}, u32[]{:S(2)}) collective-permute-start(f32[320,128]{1,0:T(8,128)S(1)} %get-tuple-element.21), channel_id=1, source_target_pairs={{0,32},{1,33},{2,34},{3,35},{4,36},{5,37},{6,38},{7,39},{8,40},{9,... | collective-permute-start | bytes 491528 | tf_op jit(solution)/shard_map/ppermute | solution.py:445
  14.1 0.7 %collective-permute-start.3 = (f32[256,128]{1,0:T(8,128)S(1)}, f32[256,128]{1,0:T(8,128)S(1)}, u32[]{:S(2)}, u32[]{:S(2)}) collective-permute-start(f32[256,128]{1,0:T(8,128)S(1)} %get-tuple-element.22), channel_id=1, source_target_pairs={{0,64},{1,65},{2,66},{3,67},{4,68},{5,69},{6,70},{7,71},{8,72},{9,... | collective-permute-start | bytes 393224 | tf_op jit(solution)/shard_map/ppermute | solution.py:445
  14.8 0.7 %collective-permute-start.4 = (f32[192,128]{1,0:T(8,128)S(1)}, f32[192,128]{1,0:T(8,128)S(1)}, u32[]{:S(2)}, u32[]{:S(2)}) collective-permute-start(f32[192,128]{1,0:T(8,128)S(1)} %get-tuple-element.23), channel_id=1, source_target_pairs={{0,192},{1,193},{2,194},{3,195},{4,196},{5,197},{6,198},{7,199},{8... | collective-permute-start | bytes 294920 | tf_op jit(solution)/shard_map/ppermute | solution.py:445
  15.5 0.7 %collective-permute-start.5 = (f32[128,128]{1,0:T(8,128)S(1)}, f32[128,128]{1,0:T(8,128)S(1)}, u32[]{:S(2)}, u32[]{:S(2)}) collective-permute-start(f32[128,128]{1,0:T(8,128)S(1)} %get-tuple-element.24), channel_id=1, source_target_pairs={{0,256},{1,257},{2,258},{3,259},{4,260},{5,261},{6,262},{7,263},{8... | collective-permute-start | bytes 196616 | tf_op jit(solution)/shard_map/ppermute | solution.py:445
  16.2 0.7 %collective-permute-start.6 = (f32[64,128]{1,0:T(8,128)S(1)}, f32[64,128]{1,0:T(8,128)S(1)}, u32[]{:S(2)}, u32[]{:S(2)}) collective-permute-start(f32[64,128]{1,0:T(8,128)S(1)} %get-tuple-element.25), channel_id=1, source_target_pairs={{0,416},{1,417},{2,418},{3,419},{4,420},{5,421},{6,422},{7,423},{8... | collective-permute-start | bytes 98312 | tf_op jit(solution)/shard_map/ppermute | solution.py:445
  16.9 5.9 %march.1 = (f32[2,2,768,128]{3,2,1,0:T(8,128)}, f32[4,12,16,128]{3,2,1,0:T(8,128)S(1)}, f32[12,2,2,32,128]{4,3,2,1,0:T(8,128)S(1)}) custom-call(s32[15]{0:T(128)S(1)} %copy-done.5, s32[15]{0:T(128)S(1)} %copy-done.6, s32[15]{0:T(128)S(1)} %copy-done.7, s32[2]{0:T(128)S(1)} %copy-done.9, s32[2]{0:T(128)S(1)} %copy-done.10, s32[2]{0:T(128)S(1)} %copy-done.11, ...), custom_call_target="tpu_custom_call" | custom-call | tf_op jit(solution)/shard_map/march/pallas_call | solution.py:441
  22.9 0.0 collective-permute-done.5.refs_3_
  22.9 0.0 collective-permute-done.4.refs_2_
  22.9 0.0 collective-permute-done.3.refs_1_
  22.9 0.0 collective-permute-done.2.refs_0_
  22.9 0.7 %collective-permute-start.7 = (f32[64,128]{1,0:T(8,128)S(1)}, f32[64,128]{1,0:T(8,128)S(1)}, u32[]{:S(2)}, u32[]{:S(2)}) collective-permute-start(f32[64,128]{1,0:T(8,128)S(1)} %get-tuple-element.27), channel_id=1, source_target_pairs={{32,288},{33,289},{34,290},{35,291},{36,292},{37,293},{38,294},{39... | collective-permute-start | bytes 98312 | tf_op jit(solution)/shard_map/ppermute | solution.py:445
  23.6 0.7 %collective-permute-start.8 = (f32[64,128]{1,0:T(8,128)S(1)}, f32[64,128]{1,0:T(8,128)S(1)}, u32[]{:S(2)}, u32[]{:S(2)}) collective-permute-start(f32[64,128]{1,0:T(8,128)S(1)} %get-tuple-element.28), channel_id=1, source_target_pairs={{32,96},{33,97},{34,98},{35,99},{36,100},{37,101},{38,102},{39,103... | collective-permute-start | bytes 98312 | tf_op jit(solution)/shard_map/ppermute | solution.py:445
  24.3 0.7 %collective-permute-start.9 = (f32[64,128]{1,0:T(8,128)S(1)}, f32[64,128]{1,0:T(8,128)S(1)}, u32[]{:S(2)}, u32[]{:S(2)}) collective-permute-start(f32[64,128]{1,0:T(8,128)S(1)} %get-tuple-element.29), channel_id=1, source_target_pairs={{32,224},{33,225},{34,226},{35,227},{36,228},{37,229},{38,230},{39... | collective-permute-start | bytes 98312 | tf_op jit(solution)/shard_map/ppermute | solution.py:445
  25.0 1.3 %collective-permute-start.10 = (f32[64,128]{1,0:T(8,128)S(1)}, f32[64,128]{1,0:T(8,128)S(1)}, u32[]{:S(2)}, u32[]{:S(2)}) collective-permute-start(f32[64,128]{1,0:T(8,128)S(1)} %get-tuple-element.30), channel_id=1, source_target_pairs={{32,160},{33,161},{34,162},{35,163},{36,164},{37,165},{38,166},{39... | collective-permute-start | bytes 98312 | tf_op jit(solution)/shard_map/ppermute | solution.py:445
  26.3 0.0 collective-permute-done.6.refs_4_
  26.3 0.0 collective-permute-done.7.refs_5_
  26.3 6.7 %collective-permute-done.10.refs_8_ = f32[64,128]{1,0:T(8,128)S(1)} collective-permute-done((f32[64,128]{1,0:T(8,128)S(1)}, f32[64,128]{1,0:T(8,128)S(1)}, u32[]{:S(2)}, u32[]{:S(2)}) %collective-permute-start.10) | collective-permute-done | bytes 32800 | tf_op jit(solution)/shard_map/ppermute | solution.py:445
  33.0 2.7 %born.1 = f32[2,2,768,128]{3,2,1,0:T(8,128)} custom-call(s32[15]{0:T(128)S(1)} %copy-done.5, s32[15]{0:T(128)S(1)} %copy-done.6, s32[15]{0:T(128)S(1)} %copy-done.7, s32[2]{0:T(128)S(1)} %copy-done.9, s32[2]{0:T(128)S(1)} %copy-done.10, s32[2]{0:T(128)S(1)} %copy-done.11, f32[2,2]{1,0:T(2,128)S(1)} %copy-done.8, ...), custom_call_target="tpu_custom_call", output_to_operand_aliasing={{}: (18, {})} | custom-call | tf_op jit(solution)/shard_map/born/pallas_call | solution.py:441
  (27 shorter events, 0.1 us)
Async XLA Ops:
  0.0 12.9 %copy-start = (f32[1,2,2,24,32,128]{5,4,3,2,1,0:T(8,128)S(1)}, f32[1,2,2,24,32,128]{5,4,3,2,1,0:T(8,128)}, u32[]{:S(2)}) copy-start(f32[1,2,2,24,32,128]{5,4,3,2,1,0:T(8,128)} %param.12) | copy-start | bytes 4718596
  0.0 12.9 %copy-start.7 = (s32[15]{0:T(128)S(1)}, s32[15]{0:T(128)}, u32[]{:S(2)}) copy-start(s32[15]{0:T(128)} %yb.5) | copy-start | bytes 184
  0.0 12.9 %copy-start.6 = (s32[15]{0:T(128)S(1)}, s32[15]{0:T(128)}, u32[]{:S(2)}) copy-start(s32[15]{0:T(128)} %zb.5) | copy-start | bytes 184
  0.0 12.9 %copy-start.5 = (s32[15]{0:T(128)S(1)}, s32[15]{0:T(128)}, u32[]{:S(2)}) copy-start(s32[15]{0:T(128)} %xb.5) | copy-start | bytes 184
  0.0 16.8 %copy-start.1 = (f32[24,32,128]{2,1,0:T(8,128)S(1)}, f32[24,32,128]{2,1,0:T(8,128)}, u32[]{:S(2)}) copy-start(f32[24,32,128]{2,1,0:T(8,128)} %param.13) | copy-start | bytes 1179652
  0.0 16.8 %copy-start.2 = (f32[24,32,128]{2,1,0:T(8,128)S(1)}, f32[24,32,128]{2,1,0:T(8,128)}, u32[]{:S(2)}) copy-start(f32[24,32,128]{2,1,0:T(8,128)} %param.14) | copy-start | bytes 1179652
  0.0 16.8 %copy-start.3 = (f32[15,8,8,8]{0,3,2,1:T(8,128)S(1)}, f32[15,8,8,8]{0,3,2,1:T(8,128)}, u32[]{:S(2)}) copy-start(f32[15,8,8,8]{0,3,2,1:T(8,128)} %param.15) | copy-start | bytes 92164
  0.0 16.8 %copy-start.4 = (f32[15,8,8,8]{0,3,2,1:T(8,128)S(1)}, f32[15,8,8,8]{0,3,2,1:T(8,128)}, u32[]{:S(2)}) copy-start(f32[15,8,8,8]{0,3,2,1:T(8,128)} %param.16) | copy-start | bytes 92164
  0.1 16.8 %copy-start.8 = (f32[2,2]{1,0:T(2,128)S(1)}, f32[2,2]{1,0:T(2,128)}, u32[]{:S(2)}) copy-start(f32[2,2]{1,0:T(2,128)} %wavelet.3) | copy-start | bytes 52
  0.1 16.8 %copy-start.9 = (s32[2]{0:T(128)S(1)}, s32[2]{0:T(128)}, u32[]{:S(2)}) copy-start(s32[2]{0:T(128)} %sx.3) | copy-start | bytes 28
  0.1 16.8 %copy-start.10 = (s32[2]{0:T(128)S(1)}, s32[2]{0:T(128)}, u32[]{:S(2)}) copy-start(s32[2]{0:T(128)} %sz.3) | copy-start | bytes 28
  0.1 16.8 %copy-start.11 = (s32[2]{0:T(128)S(1)}, s32[2]{0:T(128)}, u32[]{:S(2)}) copy-start(s32[2]{0:T(128)} %sy.3) | copy-start | bytes 28
  1.2 7.0 %collective-permute-start = (f32[288,128]{1,0:T(8,128)S(1)}, f32[288,128]{1,0:T(8,128)S(1)}, u32[]{:S(2)}, u32[]{:S(2)}) collective-permute-start(f32[288,128]{1,0:T(8,128)S(1)} %get-tuple-element.19), channel_id=1, source_target_pairs={{0,1},{2,3},{4,5},{6,7},{8,9},{10,11},{12,13},{14,15},{16,17},{18,... | collective-permute-start | bytes 442376 | tf_op jit(solution)/shard_map/ppermute | solution.py:449
  4.5 8.4 %collective-permute-start.1 = (f32[288,128]{1,0:T(8,128)S(1)}, f32[288,128]{1,0:T(8,128)S(1)}, u32[]{:S(2)}, u32[]{:S(2)}) collective-permute-start(f32[288,128]{1,0:T(8,128)S(1)} %get-tuple-element.20), channel_id=1, source_target_pairs={{1,2},{3,4},{5,6},{7,8},{9,10},{11,12},{13,14},{15,16},{17,18},{19... | collective-permute-start | bytes 442376 | tf_op jit(solution)/shard_map/ppermute | solution.py:449
  13.5 9.4 %collective-permute-start.2 = (f32[320,128]{1,0:T(8,128)S(1)}, f32[320,128]{1,0:T(8,128)S(1)}, u32[]{:S(2)}, u32[]{:S(2)}) collective-permute-start(f32[320,128]{1,0:T(8,128)S(1)} %get-tuple-element.21), channel_id=1, source_target_pairs={{0,32},{1,33},{2,34},{3,35},{4,36},{5,37},{6,38},{7,39},{8,40},{9,... | collective-permute-start | bytes 491528 | tf_op jit(solution)/shard_map/ppermute | solution.py:445
  14.1 8.7 %collective-permute-start.3 = (f32[256,128]{1,0:T(8,128)S(1)}, f32[256,128]{1,0:T(8,128)S(1)}, u32[]{:S(2)}, u32[]{:S(2)}) collective-permute-start(f32[256,128]{1,0:T(8,128)S(1)} %get-tuple-element.22), channel_id=1, source_target_pairs={{0,64},{1,65},{2,66},{3,67},{4,68},{5,69},{6,70},{7,71},{8,72},{9,... | collective-permute-start | bytes 393224 | tf_op jit(solution)/shard_map/ppermute | solution.py:445
  14.8 8.1 %collective-permute-start.4 = (f32[192,128]{1,0:T(8,128)S(1)}, f32[192,128]{1,0:T(8,128)S(1)}, u32[]{:S(2)}, u32[]{:S(2)}) collective-permute-start(f32[192,128]{1,0:T(8,128)S(1)} %get-tuple-element.23), channel_id=1, source_target_pairs={{0,192},{1,193},{2,194},{3,195},{4,196},{5,197},{6,198},{7,199},{8... | collective-permute-start | bytes 294920 | tf_op jit(solution)/shard_map/ppermute | solution.py:445
  15.5 7.4 %collective-permute-start.5 = (f32[128,128]{1,0:T(8,128)S(1)}, f32[128,128]{1,0:T(8,128)S(1)}, u32[]{:S(2)}, u32[]{:S(2)}) collective-permute-start(f32[128,128]{1,0:T(8,128)S(1)} %get-tuple-element.24), channel_id=1, source_target_pairs={{0,256},{1,257},{2,258},{3,259},{4,260},{5,261},{6,262},{7,263},{8... | collective-permute-start | bytes 196616 | tf_op jit(solution)/shard_map/ppermute | solution.py:445
  16.2 10.1 %collective-permute-start.6 = (f32[64,128]{1,0:T(8,128)S(1)}, f32[64,128]{1,0:T(8,128)S(1)}, u32[]{:S(2)}, u32[]{:S(2)}) collective-permute-start(f32[64,128]{1,0:T(8,128)S(1)} %get-tuple-element.25), channel_id=1, source_target_pairs={{0,416},{1,417},{2,418},{3,419},{4,420},{5,421},{6,422},{7,423},{8... | collective-permute-start | bytes 98312 | tf_op jit(solution)/shard_map/ppermute | solution.py:445
  22.9 3.3 %collective-permute-start.7 = (f32[64,128]{1,0:T(8,128)S(1)}, f32[64,128]{1,0:T(8,128)S(1)}, u32[]{:S(2)}, u32[]{:S(2)}) collective-permute-start(f32[64,128]{1,0:T(8,128)S(1)} %get-tuple-element.27), channel_id=1, source_target_pairs={{32,288},{33,289},{34,290},{35,291},{36,292},{37,293},{38,294},{39... | collective-permute-start | bytes 98312 | tf_op jit(solution)/shard_map/ppermute | solution.py:445
  23.6 2.7 %collective-permute-start.8 = (f32[64,128]{1,0:T(8,128)S(1)}, f32[64,128]{1,0:T(8,128)S(1)}, u32[]{:S(2)}, u32[]{:S(2)}) collective-permute-start(f32[64,128]{1,0:T(8,128)S(1)} %get-tuple-element.28), channel_id=1, source_target_pairs={{32,96},{33,97},{34,98},{35,99},{36,100},{37,101},{38,102},{39,103... | collective-permute-start | bytes 98312 | tf_op jit(solution)/shard_map/ppermute | solution.py:445
  24.3 2.0 %collective-permute-start.9 = (f32[64,128]{1,0:T(8,128)S(1)}, f32[64,128]{1,0:T(8,128)S(1)}, u32[]{:S(2)}, u32[]{:S(2)}) collective-permute-start(f32[64,128]{1,0:T(8,128)S(1)} %get-tuple-element.29), channel_id=1, source_target_pairs={{32,224},{33,225},{34,226},{35,227},{36,228},{37,229},{38,230},{39... | collective-permute-start | bytes 98312 | tf_op jit(solution)/shard_map/ppermute | solution.py:445
  25.0 8.0 %collective-permute-start.10 = (f32[64,128]{1,0:T(8,128)S(1)}, f32[64,128]{1,0:T(8,128)S(1)}, u32[]{:S(2)}, u32[]{:S(2)}) collective-permute-start(f32[64,128]{1,0:T(8,128)S(1)} %get-tuple-element.30), channel_id=1, source_target_pairs={{32,160},{33,161},{34,162},{35,163},{36,164},{37,165},{38,166},{39... | collective-permute-start | bytes 98312 | tf_op jit(solution)/shard_map/ppermute | solution.py:445

commit v4 on v3

--- a/solution.py
+++ b/solution.py
@@ -44,9 +44,15 @@
     return pl.ds(start if isinstance(p, int) else pl.multiple_of(start, DEPTH), count * DEPTH)
 
 
+def at(ref, n):
+    values = ref[...].reshape(1, -1)
+    lane = lax.broadcasted_iota(jnp.int32, values.shape, 1)
+    return jnp.sum(jnp.where(lane == n, values, jnp.zeros_like(values)))
+
+
 def window(blocks, g, first):
-    xb, zb, yb = blocks
-    return xb[g] * EDGE - 2 - first, jnp.clip(zb[g] * EDGE - 2, 0, DEPTH - SPAN), yb[g] * EDGE - 2
+    xb, zb, yb = (at(ref, g) for ref in blocks)
+    return xb * EDGE - 2 - first, jnp.clip(zb * EDGE - 2, 0, DEPTH - SPAN), yb * EDGE - 2
 
 
 def met(x0, width):
@@ -87,7 +93,7 @@
     from_sides(swap_a, swap_b, act)
 
 
-def split_kernel(width, xb, zb, yb, wave, swap_a, swap_b, *refs):
+def split_kernel(width, xb, zb, yb, wave, swap_b, swap_a, *refs):
     outs, sides = refs[:-1], refs[-1]
     packs = [(head, *rest) for head, rest in zip(FIRST, NEXT)] + [(row,) for row in DIRECT]
 
@@ -97,19 +103,24 @@
         keep_sides(swap_a, swap_b, sides)
         lane = lax.broadcasted_iota(jnp.int32, (8, 128), 1)
 
-        def cut(g, out, at):
-            x0, z0, y0 = window((xb, zb, yb), g, first)
-
-            def place(n, load):
-                k, q = divmod(n, PER_ROW)
-                for half in (0, SPAN - 8):
-                    spot = pl.ds(at * ROWS + k * SPAN + half, 8)
-                    values = pltpu.roll(load(half), wrapped(SPAN * q - y0), 1)
-                    mine = (lane >= SPAN * q) & (lane < SPAN * (q + 1))
-                    out[spot, :] = jnp.where(mine, values, out[spot, :])
-
-            @pl.when(met(x0, width))
+        starts = xb[...].reshape(1, -1) * EDGE - 2 - first
+        each_bit = jnp.left_shift(1, lax.broadcasted_iota(jnp.int32, starts.shape, 1))
+        bits = jnp.sum(jnp.where(met(starts, width), each_bit, 0))
+
+        def cut(g, out, spot_of):
+
+            @pl.when(jnp.bitwise_and(jnp.right_shift(bits, g), 1) == 1)
             def _():
+                x0, z0, y0 = window((xb, zb, yb), g, first)
+
+                def place(n, load):
+                    k, q = divmod(n, PER_ROW)
+                    for half in (0, SPAN - 8):
+                        spot = pl.ds(spot_of * ROWS + k * SPAN + half, 8)
+                        values = pltpu.roll(load(half), wrapped(SPAN * q - y0), 1)
+                        mine = (lane >= SPAN * q) & (lane < SPAN * (q + 1))
+                        out[spot, :] = jnp.where(mine, values, out[spot, :])
+
                 for i in range(SPAN):
                     p = x0 + i
                     strips = [(n, s, t) for n, (s, t, j) in enumerate(STRIPS) if j == i]
@@ -129,11 +140,11 @@
 
         for out, members in zip(outs, packs):
 
-            def each(at, carry):
+            def each(n, carry):
                 row = jnp.int32(members[0])
-                for n, member in enumerate(members[1:], 1):
-                    row = jnp.where(at == n, member, row)
-                cut(row - 1, out, at)
+                for m, member in enumerate(members[1:], 1):
+                    row = jnp.where(n == m, member, row)
+                cut(row - 1, out, n)
                 return carry
 
             lax.fori_loop(0, len(members), each, 0)
@@ -150,8 +161,14 @@
                 out[...] = source[pl.ds((1 + n) * ROWS, ROWS), :]
 
 
-def march_kernel(
-    width, xb, zb, yb, sx, sz, sy, wavelet, wave, stiff, buoy, swap_a, swap_b, pstiff, pbuoy, out, prep, fields,
+def march_kernel(width, rows_of, *refs):
+    @pl.when(rows_of(lax.axis_index("probe")))
+    def _():
+        march(width, *refs[:14], *refs[-8:])
+
+
+def march(
+    width, xb, zb, yb, sx, sz, sy, wavelet, wave, stiff, buoy, swap_b, swap_a, pstiff, pbuoy, out, prep, fields,
     sides, mid, later, weights, sem_out,
 ):
     first = lax.axis_index("gx") * width
@@ -234,17 +251,19 @@
             )
         return carry
 
-    lax.fori_loop(1, width - 1, step_one, 0)
+    lax.fori_loop(1, width - 1, step_one, 0, unroll=width - 2)
 
     def inject(ref, step, low, high, shift):
         for s in range(2):
-            x = sx[s] - first
-
-            @pl.when((row == 0) & (x >= low) & (x < high))
+            @pl.when(row == 0)
             def _():
-                hit = (lane == sy[s]) & (depth == sz[s])
-                spot = plane_rows(x + shift)
-                ref[s, spot, :] = ref[s, spot, :] + jnp.where(hit, wavelet[s, step], 0.0)
+                x = at(sx, s) - first
+
+                @pl.when((x >= low) & (x < high))
+                def _():
+                    hit = (lane == at(sy, s)) & (depth == at(sz, s))
+                    spot = plane_rows(x + shift)
+                    ref[s, spot, :] = ref[s, spot, :] + jnp.where(hit, at(wavelet.at[s], step), 0.0)
 
     inject(mid, 0, -1, width + 1, 1)
     outs = copy_all([(mid.at[s, plane_rows(1, width)], out.at[s, 0]) for s in range(2)], sem_out)
@@ -262,7 +281,7 @@
     part = width // 3
     for n in range(3):
         low, high = n * part, (n + 1) * part
-        lax.fori_loop(low, high, step_two, 0)
+        lax.fori_loop(low, high, step_two, 0, unroll=part)
         inject(later, 1, low, high, 0)
         pairs = [(later.at[s, plane_rows(low, part)], out.at[s, 1, plane_rows(low, part)]) for s in range(2)]
         outs += copy_all(pairs, sem_out, 2 + 2 * n)
@@ -305,7 +324,7 @@
         wide = lax.broadcasted_iota(jnp.int32, (EDGE, EDGE, pstiff.shape[-1]), 2)
         diagonal = lax.broadcasted_iota(jnp.int32, (EDGE, EDGE, 128), 2)
         diagonal = diagonal == lax.broadcasted_iota(jnp.int32, (EDGE, EDGE, 128), 1) + 2
-        dz = zb[g] * EDGE - z0
+        dz = at(zb, g) * EDGE - z0
         for n, ref in ((2, pstiff), (3, pbuoy)):
             for i in range(EDGE):
                 column = jnp.sum(jnp.where(wide == g, ref[i], 0.0), axis=2, keepdims=True)
@@ -351,8 +370,8 @@
                 if (s, t, i) not in STRIPS:
                     got.append(jnp.zeros((16, 128), jnp.float32))
                     continue
-                at, q = divmod(STRIPS.index((s, t, i)), PER_ROW)
-                values = piece[pl.ds(at * SPAN, 16), :]
+                n, q = divmod(STRIPS.index((s, t, i)), PER_ROW)
+                values = piece[pl.ds(n * SPAN, 16), :]
                 if q:
                     values = pltpu.roll(values, 128 - SPAN * q, 1)
                 x = x0 + i
@@ -384,11 +403,11 @@
             step = steps(now)
             laplace = gather(of_c, step)
             forcing = sb * laplace + k * gather(of_b, step)
-            hit = here & (lane + y0 == sy[s]) & (depth + z0 == sz[s])
+            hit = here & (lane + y0 == at(sy, s)) & (depth + z0 == at(sz, s))
+            x, amplitude = at(sx, s), at(wavelet.at[s], 0)
             source = []
             for i in range(SPAN):
-                on = hit & (first + x0 + i == sx[s])
-                source.append(jnp.where(on, wavelet[s, 0], 0.0))
+                source.append(jnp.where(hit & (first + x0 + i == x), amplitude, 0.0))
             then = steps(2.0 * now - field(s, 0) + k * laplace + jnp.stack(source))
             second = sb * gather(of_c, then) + k * gather(of_b, then)
             gains = (forcing, 2.0 * forcing + k * gather(of_c, steps(forcing)) + second)
@@ -448,7 +467,6 @@
         pairs = [(s, s + 1) for s in range(start, slabs - 1, 2)]
         return lax.ppermute(value, "gx", pairs + [(b, a) for a, b in pairs])
 
-    smem = pltpu.SMEM
     edge = vmem(9 * DEPTH, 128)
     edge_a, edge_b = call(
         functools.partial(edge_kernel, width), "edges", [edge, edge], [pltpu.HBM] * 3, [dma(12)]
@@ -460,39 +478,47 @@
         functools.partial(split_kernel, width),
         "split",
         [vmem(n * ROWS, 128) for n in counts],
-        [smem] * 3 + [pltpu.VMEM] * 3,
+        [pltpu.VMEM] * 6,
         [vmem(2, 9 * DEPTH, 128)],
-    )(*blocks, wave, swap_a, swap_b)
+    )(*blocks, wave, swap_b, swap_a)
     got = [along_rows(p, [(0, row)]) for p, row in zip(packs, FIRST + DIRECT)]
 
-    advanced, prep, fields = call(
-        functools.partial(march_kernel, width),
-        "march",
-        [hbm(2, 2, rows, 128), vmem(4, SPAN, 16, 128), vmem(SPAN, 2, 2, DEPTH, 128)],
-        [smem] * 7 + [pltpu.VMEM] * 7,
-        [
-            vmem(2, 9 * DEPTH, 128),
-            vmem(2, (width + 2) * DEPTH, 128),
-            vmem(2, rows, 128),
-            vmem(7, rows, 128),
-            dma(8),
-        ],
-    )(*blocks, *sources, wave, stiff, buoy, swap_a, swap_b, *perts)
+    def march_on(name, rows_of, before=()):
+        marched = [hbm(2, 2, rows, 128), vmem(4, SPAN, 16, 128), vmem(SPAN, 2, 2, DEPTH, 128)]
+        operands = (*blocks, *sources, wave, stiff, buoy, swap_b, swap_a, *perts, *before)
+        return call(
+            functools.partial(march_kernel, width, rows_of),
+            name,
+            marched,
+            [pltpu.VMEM] * 14 + [pltpu.HBM, pltpu.VMEM, pltpu.VMEM, pltpu.VMEM][: len(before)],
+            [
+                vmem(2, 9 * DEPTH, 128),
+                vmem(2, (width + 2) * DEPTH, 128),
+                vmem(2, rows, 128),
+                vmem(7, rows, 128),
+                dma(8),
+            ],
+            input_output_aliases={14: 0, 15: 1, 16: 2} if before else {},
+        )(*operands)
+
+    late = lambda row: functools.reduce(jnp.logical_or, [row == r for r in FIRST[1:]])
+    marched = march_on("march_first", late)
 
     longest = max(len(rest) for rest in NEXT)
     passed = call(
         pass_kernel, "pass_on", [vmem(ROWS, 128)] * longest, [pltpu.VMEM] * (len(FIRST) + 1), []
-    )(*got[: len(FIRST)], prep)
+    )(*got[: len(FIRST)], marched[1])
     nexts = [
         along_rows(value, [(head, rest[n]) for head, rest in zip(FIRST, NEXT) if n < len(rest)])
         for n, value in enumerate(passed)
     ]
+    advanced, prep, fields = march_on("march_rest", lambda row: jnp.logical_not(late(row)), (*marched, passed[-1]))
     operands = (*blocks, *sources, *got, *nexts, prep, fields, advanced)
     result = call(
         functools.partial(born_kernel, width, width * slabs),
         "born",
         hbm(2, 2, rows, 128),
-        [smem] * 7 + [pltpu.VMEM] * (len(operands) - 8) + [pltpu.HBM],
+        [pltpu.VMEM] * (len(operands) - 1) + [pltpu.HBM],
         [vmem(ROWS, 128), vmem(SPAN, 2, 2, DEPTH + 8, 128), dma(SPAN)],
         input_output_aliases={len(operands) - 1: 0},
     )(*operands)

time: 36 us -> 31.7 us (0.88)
  the two profiles are of different devices: /device:TPU:389 before, /device:TPU:361 now
where the time goes in v4:
time: 31.7 us; the launch traced here: 31.4 us
  starting transfers between devices  16.9 us (53%)
  waiting for transfers between devices  7.21 us (23%)
  Pallas kernels  6.92 us (22%)
  between operations  0.35 us (1%)
    ppermute x9, starting transfers between devices, along_rows(): return lax.ppermute(value, ('probe', 'gx'), every)  11.1 us
    ppermute x2, waiting for transfers between devices, swap(): return lax.ppermute(value, 'gx', pairs + [(b, a) for a, b in pairs])  7.19 us
    pallas_call x6, Pallas kernels, call(): made(*map(pltpu.with_memory_space_constraint, args, spaces))  6.92 us
    ppermute x2, starting transfers between devices, swap(): return lax.ppermute(value, 'gx', pairs + [(b, a) for a, b in pairs])  5.73 us
  transfers between devices with their start and end apart: 11, of which 2 were waited for; matrix products, arithmetic and copies ran while one was open for 0% of the time, Pallas kernels for 10%

profile of v4, /device:TPU:361, one launch (start us, length us, event | category | flops | bytes accessed | tf_op | source)
XLA Modules:
  0.0 31.4 jit_solution(11023190588306886634)
XLA Ops:
  0.1 1.1 %edges.1 = (f32[288,128]{1,0:T(8,128)S(1)}, f32[288,128]{1,0:T(8,128)S(1)}) custom-call(f32[2,2,768,128]{3,2,1,0:T(8,128)} %bitcast.6, f32[768,128]{1,0:T(8,128)} %bitcast.10, f32[768,128]{1,0:T(8,128)} %bitcast.13), custom_call_target="tpu_custom_call" | custom-call | tf_op jit(solution)/shard_map/edges/pallas_call | solution.py:460
  1.3 2.5 %collective-permute-start = (f32[288,128]{1,0:T(8,128)S(1)}, f32[288,128]{1,0:T(8,128)S(1)}, u32[]{:S(2)}, u32[]{:S(2)}) collective-permute-start(f32[288,128]{1,0:T(8,128)S(1)} %get-tuple-element.22), channel_id=1, source_target_pairs={{1,2},{3,4},{5,6},{7,8},{9,10},{11,12},{13,14},{15,16},{17,18},{19... | collective-permute-start | bytes 442376 | tf_op jit(solution)/shard_map/ppermute | solution.py:468
  3.8 3.2 %collective-permute-start.1 = (f32[288,128]{1,0:T(8,128)S(1)}, f32[288,128]{1,0:T(8,128)S(1)}, u32[]{:S(2)}, u32[]{:S(2)}) collective-permute-start(f32[288,128]{1,0:T(8,128)S(1)} %get-tuple-element.23), channel_id=1, source_target_pairs={{0,1},{2,3},{4,5},{6,7},{8,9},{10,11},{12,13},{14,15},{16,17},{18,... | collective-permute-start | bytes 442376 | tf_op jit(solution)/shard_map/ppermute | solution.py:468
  7.0 3.0 %collective-permute-done.swap_b.refs_10_ = f32[288,128]{1,0:T(8,128)S(1)} collective-permute-done((f32[288,128]{1,0:T(8,128)S(1)}, f32[288,128]{1,0:T(8,128)S(1)}, u32[]{:S(2)}, u32[]{:S(2)}) %collective-permute-start) | collective-permute-done | bytes 147488 | tf_op jit(solution)/shard_map/ppermute | solution.py:468
  10.0 4.2 %collective-permute-done.1.swap_a.refs_11_ = f32[288,128]{1,0:T(8,128)S(1)} collective-permute-done((f32[288,128]{1,0:T(8,128)S(1)}, f32[288,128]{1,0:T(8,128)S(1)}, u32[]{:S(2)}, u32[]{:S(2)}) %collective-permute-start.1) | collective-permute-done | bytes 147488 | tf_op jit(solution)/shard_map/ppermute | solution.py:468
  14.2 1.3 %collective-permute-start.2 = (f32[320,128]{1,0:T(8,128)S(1)}, f32[320,128]{1,0:T(8,128)S(1)}, u32[]{:S(2)}, u32[]{:S(2)}) collective-permute-start(f32[320,128]{1,0:T(8,128)S(1)} %get-tuple-element.24), channel_id=1, source_target_pairs={{0,32},{1,33},{2,34},{3,35},{4,36},{5,37},{6,38},{7,39},{8,40},{9,... | collective-permute-start | bytes 491528 | tf_op jit(solution)/shard_map/ppermute | solution.py:464
  15.5 0.7 %collective-permute-start.3 = (f32[256,128]{1,0:T(8,128)S(1)}, f32[256,128]{1,0:T(8,128)S(1)}, u32[]{:S(2)}, u32[]{:S(2)}) collective-permute-start(f32[256,128]{1,0:T(8,128)S(1)} %get-tuple-element.25), channel_id=1, source_target_pairs={{0,64},{1,65},{2,66},{3,67},{4,68},{5,69},{6,70},{7,71},{8,72},{9,... | collective-permute-start | bytes 393224 | tf_op jit(solution)/shard_map/ppermute | solution.py:464
  16.2 0.7 %collective-permute-start.4 = (f32[192,128]{1,0:T(8,128)S(1)}, f32[192,128]{1,0:T(8,128)S(1)}, u32[]{:S(2)}, u32[]{:S(2)}) collective-permute-start(f32[192,128]{1,0:T(8,128)S(1)} %get-tuple-element.26), channel_id=1, source_target_pairs={{0,192},{1,193},{2,194},{3,195},{4,196},{5,197},{6,198},{7,199},{8... | collective-permute-start | bytes 294920 | tf_op jit(solution)/shard_map/ppermute | solution.py:464
  16.9 0.7 %collective-permute-start.5 = (f32[128,128]{1,0:T(8,128)S(1)}, f32[128,128]{1,0:T(8,128)S(1)}, u32[]{:S(2)}, u32[]{:S(2)}) collective-permute-start(f32[128,128]{1,0:T(8,128)S(1)} %get-tuple-element.27), channel_id=1, source_target_pairs={{0,256},{1,257},{2,258},{3,259},{4,260},{5,261},{6,262},{7,263},{8... | collective-permute-start | bytes 196616 | tf_op jit(solution)/shard_map/ppermute | solution.py:464
  17.6 0.7 %collective-permute-start.6 = (f32[64,128]{1,0:T(8,128)S(1)}, f32[64,128]{1,0:T(8,128)S(1)}, u32[]{:S(2)}, u32[]{:S(2)}) collective-permute-start(f32[64,128]{1,0:T(8,128)S(1)} %get-tuple-element.28), channel_id=1, source_target_pairs={{0,416},{1,417},{2,418},{3,419},{4,420},{5,421},{6,422},{7,423},{8... | collective-permute-start | bytes 98312 | tf_op jit(solution)/shard_map/ppermute | solution.py:464
  18.3 0.1 march_first.1
  18.4 0.0 collective-permute-done.5.refs_3_
  18.4 0.0 collective-permute-done.3.refs_1_
  18.4 0.0 collective-permute-done.2.refs_0_
  18.5 3.3 %collective-permute-start.7 = (f32[64,128]{1,0:T(8,128)S(1)}, f32[64,128]{1,0:T(8,128)S(1)}, u32[]{:S(2)}, u32[]{:S(2)}) collective-permute-start(f32[64,128]{1,0:T(8,128)S(1)} %get-tuple-element.30), channel_id=1, source_target_pairs={{32,288},{33,289},{34,290},{35,291},{36,292},{37,293},{38,294},{39... | collective-permute-start | bytes 98312 | tf_op jit(solution)/shard_map/ppermute | solution.py:464
  21.8 1.3 %collective-permute-start.8 = (f32[64,128]{1,0:T(8,128)S(1)}, f32[64,128]{1,0:T(8,128)S(1)}, u32[]{:S(2)}, u32[]{:S(2)}) collective-permute-start(f32[64,128]{1,0:T(8,128)S(1)} %get-tuple-element.31), channel_id=1, source_target_pairs={{32,96},{33,97},{34,98},{35,99},{36,100},{37,101},{38,102},{39,103... | collective-permute-start | bytes 98312 | tf_op jit(solution)/shard_map/ppermute | solution.py:464
  23.1 1.3 %collective-permute-start.9 = (f32[64,128]{1,0:T(8,128)S(1)}, f32[64,128]{1,0:T(8,128)S(1)}, u32[]{:S(2)}, u32[]{:S(2)}) collective-permute-start(f32[64,128]{1,0:T(8,128)S(1)} %get-tuple-element.32), channel_id=1, source_target_pairs={{32,224},{33,225},{34,226},{35,227},{36,228},{37,229},{38,230},{39... | collective-permute-start | bytes 98312 | tf_op jit(solution)/shard_map/ppermute | solution.py:464
  24.4 1.3 %collective-permute-start.10 = (f32[64,128]{1,0:T(8,128)S(1)}, f32[64,128]{1,0:T(8,128)S(1)}, u32[]{:S(2)}, u32[]{:S(2)}) collective-permute-start(f32[64,128]{1,0:T(8,128)S(1)} %get-tuple-element.33.refs_17_), channel_id=1, source_target_pairs={{32,160},{33,161},{34,162},{35,163},{36,164},{37,165},{38,166},{39... | collective-permute-start | bytes 98312 | tf_op jit(solution)/shard_map/ppermute | solution.py:464
  25.7 3.0 %march_rest.1 = (f32[2,2,768,128]{3,2,1,0:T(8,128)}, f32[4,12,16,128]{3,2,1,0:T(8,128)S(1)}, f32[12,2,2,32,128]{4,3,2,1,0:T(8,128)S(1)}) custom-call(s32[15]{0:T(128)S(1)} %copy-done.6, s32[15]{0:T(128)S(1)} %copy-done.7, s32[15]{0:T(128)S(1)} %copy-done.8, s32[2]{0:T(128)S(1)} %copy-done.9, ...), custom_call_target="tpu_custom_call", output_to_operand_aliasing={{0}: (14, {}), {1}: (15, {}), {2}: (16, {})} | custom-call | tf_op jit(solution)/shard_map/march_rest/pallas_call | solution.py:460
  28.7 0.0 collective-permute-done.6.refs_4_
  28.7 0.0 collective-permute-done.7.refs_5_
  28.7 0.0 collective-permute-done.9.refs_7_
  28.7 0.0 collective-permute-done.10.refs_8_
  28.7 2.7 %born.1 = f32[2,2,768,128]{3,2,1,0:T(8,128)} custom-call(s32[15]{0:T(128)S(1)} %copy-done.6, s32[15]{0:T(128)S(1)} %copy-done.7, s32[15]{0:T(128)S(1)} %copy-done.8, s32[2]{0:T(128)S(1)} %copy-done.9, s32[2]{0:T(128)S(1)} %copy-done.10, s32[2]{0:T(128)S(1)} %copy-done.11, f32[2,2]{1,0:T(2,128)S(1)} %copy-done.5, ...), custom_call_target="tpu_custom_call", output_to_operand_aliasing={{}: (18, {})} | custom-call | tf_op jit(solution)/shard_map/born/pallas_call | solution.py:460
  (28 shorter events, 0.1 us)
Async XLA Ops:
  0.0 14.2 %copy-start = (f32[1,2,2,24,32,128]{5,4,3,2,1,0:T(8,128)S(1)}, f32[1,2,2,24,32,128]{5,4,3,2,1,0:T(8,128)}, u32[]{:S(2)}) copy-start(f32[1,2,2,24,32,128]{5,4,3,2,1,0:T(8,128)} %param.12) | copy-start | bytes 4718596
  0.0 14.2 %copy-start.8 = (s32[15]{0:T(128)S(1)}, s32[15]{0:T(128)}, u32[]{:S(2)}) copy-start(s32[15]{0:T(128)} %yb.3) | copy-start | bytes 184
  0.0 14.2 %copy-start.7 = (s32[15]{0:T(128)S(1)}, s32[15]{0:T(128)}, u32[]{:S(2)}) copy-start(s32[15]{0:T(128)} %zb.3) | copy-start | bytes 184
  0.0 14.2 %copy-start.6 = (s32[15]{0:T(128)S(1)}, s32[15]{0:T(128)}, u32[]{:S(2)}) copy-start(s32[15]{0:T(128)} %xb.3) | copy-start | bytes 184
  0.0 18.2 %copy-start.1 = (f32[24,32,128]{2,1,0:T(8,128)S(1)}, f32[24,32,128]{2,1,0:T(8,128)}, u32[]{:S(2)}) copy-start(f32[24,32,128]{2,1,0:T(8,128)} %param.13) | copy-start | bytes 1179652
  0.0 18.2 %copy-start.2 = (f32[24,32,128]{2,1,0:T(8,128)S(1)}, f32[24,32,128]{2,1,0:T(8,128)}, u32[]{:S(2)}) copy-start(f32[24,32,128]{2,1,0:T(8,128)} %param.14) | copy-start | bytes 1179652
  0.0 18.2 %copy-start.3 = (f32[15,8,8,8]{0,3,2,1:T(8,128)S(1)}, f32[15,8,8,8]{0,3,2,1:T(8,128)}, u32[]{:S(2)}) copy-start(f32[15,8,8,8]{0,3,2,1:T(8,128)} %param.15) | copy-start | bytes 92164
  0.0 18.2 %copy-start.4 = (f32[15,8,8,8]{0,3,2,1:T(8,128)S(1)}, f32[15,8,8,8]{0,3,2,1:T(8,128)}, u32[]{:S(2)}) copy-start(f32[15,8,8,8]{0,3,2,1:T(8,128)} %param.16) | copy-start | bytes 92164
  0.1 18.2 %copy-start.5 = (f32[2,2]{1,0:T(2,128)S(1)}, f32[2,2]{1,0:T(2,128)}, u32[]{:S(2)}) copy-start(f32[2,2]{1,0:T(2,128)} %wavelet.1) | copy-start | bytes 52
  0.1 18.2 %copy-start.9 = (s32[2]{0:T(128)S(1)}, s32[2]{0:T(128)}, u32[]{:S(2)}) copy-start(s32[2]{0:T(128)} %sx.1) | copy-start | bytes 28
  0.1 18.2 %copy-start.10 = (s32[2]{0:T(128)S(1)}, s32[2]{0:T(128)}, u32[]{:S(2)}) copy-start(s32[2]{0:T(128)} %sz.1) | copy-start | bytes 28
  0.1 18.2 %copy-start.11 = (s32[2]{0:T(128)S(1)}, s32[2]{0:T(128)}, u32[]{:S(2)}) copy-start(s32[2]{0:T(128)} %sy.1) | copy-start | bytes 28
  1.3 8.7 %collective-permute-start = (f32[288,128]{1,0:T(8,128)S(1)}, f32[288,128]{1,0:T(8,128)S(1)}, u32[]{:S(2)}, u32[]{:S(2)}) collective-permute-start(f32[288,128]{1,0:T(8,128)S(1)} %get-tuple-element.22), channel_id=1, source_target_pairs={{1,2},{3,4},{5,6},{7,8},{9,10},{11,12},{13,14},{15,16},{17,18},{19... | collective-permute-start | bytes 442376 | tf_op jit(solution)/shard_map/ppermute | solution.py:468
  3.8 10.4 %collective-permute-start.1 = (f32[288,128]{1,0:T(8,128)S(1)}, f32[288,128]{1,0:T(8,128)S(1)}, u32[]{:S(2)}, u32[]{:S(2)}) collective-permute-start(f32[288,128]{1,0:T(8,128)S(1)} %get-tuple-element.23), channel_id=1, source_target_pairs={{0,1},{2,3},{4,5},{6,7},{8,9},{10,11},{12,13},{14,15},{16,17},{18,... | collective-permute-start | bytes 442376 | tf_op jit(solution)/shard_map/ppermute | solution.py:468
  14.2 4.2 %collective-permute-start.2 = (f32[320,128]{1,0:T(8,128)S(1)}, f32[320,128]{1,0:T(8,128)S(1)}, u32[]{:S(2)}, u32[]{:S(2)}) collective-permute-start(f32[320,128]{1,0:T(8,128)S(1)} %get-tuple-element.24), channel_id=1, source_target_pairs={{0,32},{1,33},{2,34},{3,35},{4,36},{5,37},{6,38},{7,39},{8,40},{9,... | collective-permute-start | bytes 491528 | tf_op jit(solution)/shard_map/ppermute | solution.py:464
  15.5 2.9 %collective-permute-start.3 = (f32[256,128]{1,0:T(8,128)S(1)}, f32[256,128]{1,0:T(8,128)S(1)}, u32[]{:S(2)}, u32[]{:S(2)}) collective-permute-start(f32[256,128]{1,0:T(8,128)S(1)} %get-tuple-element.25), channel_id=1, source_target_pairs={{0,64},{1,65},{2,66},{3,67},{4,68},{5,69},{6,70},{7,71},{8,72},{9,... | collective-permute-start | bytes 393224 | tf_op jit(solution)/shard_map/ppermute | solution.py:464
  16.2 2.2 %collective-permute-start.4 = (f32[192,128]{1,0:T(8,128)S(1)}, f32[192,128]{1,0:T(8,128)S(1)}, u32[]{:S(2)}, u32[]{:S(2)}) collective-permute-start(f32[192,128]{1,0:T(8,128)S(1)} %get-tuple-element.26), channel_id=1, source_target_pairs={{0,192},{1,193},{2,194},{3,195},{4,196},{5,197},{6,198},{7,199},{8... | collective-permute-start | bytes 294920 | tf_op jit(solution)/shard_map/ppermute | solution.py:464
  16.9 1.5 %collective-permute-start.5 = (f32[128,128]{1,0:T(8,128)S(1)}, f32[128,128]{1,0:T(8,128)S(1)}, u32[]{:S(2)}, u32[]{:S(2)}) collective-permute-start(f32[128,128]{1,0:T(8,128)S(1)} %get-tuple-element.27), channel_id=1, source_target_pairs={{0,256},{1,257},{2,258},{3,259},{4,260},{5,261},{6,262},{7,263},{8... | collective-permute-start | bytes 196616 | tf_op jit(solution)/shard_map/ppermute | solution.py:464
  17.6 11.1 %collective-permute-start.6 = (f32[64,128]{1,0:T(8,128)S(1)}, f32[64,128]{1,0:T(8,128)S(1)}, u32[]{:S(2)}, u32[]{:S(2)}) collective-permute-start(f32[64,128]{1,0:T(8,128)S(1)} %get-tuple-element.28), channel_id=1, source_target_pairs={{0,416},{1,417},{2,418},{3,419},{4,420},{5,421},{6,422},{7,423},{8... | collective-permute-start | bytes 98312 | tf_op jit(solution)/shard_map/ppermute | solution.py:464
  18.5 10.2 %collective-permute-start.7 = (f32[64,128]{1,0:T(8,128)S(1)}, f32[64,128]{1,0:T(8,128)S(1)}, u32[]{:S(2)}, u32[]{:S(2)}) collective-permute-start(f32[64,128]{1,0:T(8,128)S(1)} %get-tuple-element.30), channel_id=1, source_target_pairs={{32,288},{33,289},{34,290},{35,291},{36,292},{37,293},{38,294},{39... | collective-permute-start | bytes 98312 | tf_op jit(solution)/shard_map/ppermute | solution.py:464
  21.8 6.9 %collective-permute-start.8 = (f32[64,128]{1,0:T(8,128)S(1)}, f32[64,128]{1,0:T(8,128)S(1)}, u32[]{:S(2)}, u32[]{:S(2)}) collective-permute-start(f32[64,128]{1,0:T(8,128)S(1)} %get-tuple-element.31), channel_id=1, source_target_pairs={{32,96},{33,97},{34,98},{35,99},{36,100},{37,101},{38,102},{39,103... | collective-permute-start | bytes 98312 | tf_op jit(solution)/shard_map/ppermute | solution.py:464
  23.1 5.6 %collective-permute-start.9 = (f32[64,128]{1,0:T(8,128)S(1)}, f32[64,128]{1,0:T(8,128)S(1)}, u32[]{:S(2)}, u32[]{:S(2)}) collective-permute-start(f32[64,128]{1,0:T(8,128)S(1)} %get-tuple-element.32), channel_id=1, source_target_pairs={{32,224},{33,225},{34,226},{35,227},{36,228},{37,229},{38,230},{39... | collective-permute-start | bytes 98312 | tf_op jit(solution)/shard_map/ppermute | solution.py:464
  24.4 4.3 %collective-permute-start.10 = (f32[64,128]{1,0:T(8,128)S(1)}, f32[64,128]{1,0:T(8,128)S(1)}, u32[]{:S(2)}, u32[]{:S(2)}) collective-permute-start(f32[64,128]{1,0:T(8,128)S(1)} %get-tuple-element.33.refs_17_), channel_id=1, source_target_pairs={{32,160},{33,161},{34,162},{35,163},{36,164},{37,165},{38,166},{39... | collective-permute-start | bytes 98312 | tf_op jit(solution)/shard_map/ppermute | solution.py:464

commit v5 on v4

--- a/solution.py
+++ b/solution.py
@@ -10,11 +10,21 @@
 EDGE = 8
 SPAN = EDGE + 4
 DEPTH = 32
-PER_ROW = 10
-STRIPS = [(s, 1, i) for s in range(2) for i in range(SPAN)] + [
-    (s, 0, i) for s in range(2) for i in range(1, SPAN - 1)
-]
-ROWS = 64
+GRID = 24
+ROWS = 4 * SPAN
+
+
+def strips_of_a_piece():
+    found = []
+    for n, (s, i) in enumerate((s, i) for s in range(2) for i in range(SPAN)):
+        found.append((s, 1, i, n // 10 * SPAN, n % 10 * SPAN, 0, SPAN))
+    for n, (s, i) in enumerate((s, i) for s in range(2) for i in range(1, SPAN - 1)):
+        row, lane = (2 * SPAN, 48 + 10 * n) if n < 8 else (3 * SPAN, 10 * (n - 8))
+        found.append((s, 0, i, row, lane, 1, 10))
+    return found
+
+
+STRIPS = strips_of_a_piece()
 
 FIRST = (1, 2, 6, 8)
 NEXT = ((9, 3, 7, 5), (10, 4, 12), (14, 15), (11,))
@@ -59,84 +69,98 @@
     return (x0 < width) & (x0 + SPAN > 0)
 
 
-def from_sides(swap_a, swap_b, act):
-    even = lax.rem(lax.axis_index("gx"), 2) == 0
-
-    @pl.when(even)
-    def _():
-        act(swap_b, swap_a)
-
-    @pl.when(jnp.logical_not(even))
-    def _():
-        act(swap_a, swap_b)
-
-
-def edge_kernel(width, wave, stiff, buoy, swap_a, swap_b, sem):
+def swap_pairs(rows, slabs):
+    rounds = [[], [], []]
+    for row in range(rows):
+        for low in range(slabs - 1):
+            if row == 0 and low < 3:
+                rounds[(1, 0, 2)[low]].append((row, low))
+            else:
+                rounds[low % 2].append((row, low))
+    return rounds
+
+
+def from_sides(swaps, act):
+    slab, background = lax.axis_index("gx"), lax.axis_index("probe") == 0
+    apart = background & ((slab == 2) | (slab == 3))
+    turned = background & (slab < 2)
+    even = (lax.rem(slab, 2) == 0) != turned
+    for where, below, above in (
+        (even & jnp.logical_not(apart), 1, 0),
+        (jnp.logical_not(even | apart), 0, 1),
+        (background & (slab == 2), 0, 2),
+        (background & (slab == 3), 2, 1),
+    ):
+
+        @pl.when(where)
+        def _():
+            act(swaps[below], swaps[above])
+
+
+def edge_kernel(width, wave, stiff, buoy, swap_a, swap_b, swap_c, sem):
     def pack(low, high):
         pairs = []
         for out, outer, inner in ((low, 0, 0), (high, width - 1, width - 2)):
-            for s in range(2):
-                pairs.append((wave.at[s, 1, plane_rows(inner, 2)], out.at[plane_rows(2 * s, 2)]))
-                pairs.append((wave.at[s, 0, plane_rows(outer)], out.at[plane_rows(4 + s)]))
-            pairs.append((buoy.at[plane_rows(inner, 2)], out.at[plane_rows(6, 2)]))
-            pairs.append((stiff.at[plane_rows(outer)], out.at[plane_rows(8)]))
+            pairs.append((wave.at[:, 1, pl.ds(inner, 2)], out.at[pl.ds(0, 2), pl.ds(0, 2)]))
+            pairs.append((wave.at[:, 0, outer], out.at[pl.ds(0, 2), 2]))
+            pairs.append((buoy.at[pl.ds(inner, 2)], out.at[2, pl.ds(0, 2)]))
+            pairs.append((stiff.at[outer], out.at[2, 2]))
         wait_all(copy_all(pairs, sem))
 
-    from_sides(swap_a, swap_b, pack)
-
-
-def keep_sides(swap_a, swap_b, sides):
+    from_sides((swap_a, swap_b, swap_c), pack)
+
+
+def keep_sides(swaps, sides):
     def act(below, above):
         sides[0] = below[...]
         sides[1] = above[...]
 
-    from_sides(swap_a, swap_b, act)
-
-
-def split_kernel(width, xb, zb, yb, wave, swap_b, swap_a, *refs):
-    outs, sides = refs[:-1], refs[-1]
+    from_sides(swaps, act)
+
+
+def split_kernel(width, xb, zb, yb, wave, swap_b, swap_a, swap_c, *refs):
+    *outs, sides, near = refs
     packs = [(head, *rest) for head, rest in zip(FIRST, NEXT)] + [(row,) for row in DIRECT]
 
     @pl.when(lax.axis_index("probe") == 0)
     def _():
         first = lax.axis_index("gx") * width
-        keep_sides(swap_a, swap_b, sides)
-        lane = lax.broadcasted_iota(jnp.int32, (8, 128), 1)
-
+        keep_sides((swap_a, swap_b, swap_c), sides)
+        lane = lax.broadcasted_iota(jnp.int32, (16, 128), 1)
         starts = xb[...].reshape(1, -1) * EDGE - 2 - first
         each_bit = jnp.left_shift(1, lax.broadcasted_iota(jnp.int32, starts.shape, 1))
         bits = jnp.sum(jnp.where(met(starts, width), each_bit, 0))
 
-        def cut(g, out, spot_of):
-
+        def cut(g, out, n):
             @pl.when(jnp.bitwise_and(jnp.right_shift(bits, g), 1) == 1)
             def _():
                 x0, z0, y0 = window((xb, zb, yb), g, first)
-
-                def place(n, load):
-                    k, q = divmod(n, PER_ROW)
-                    for half in (0, SPAN - 8):
-                        spot = pl.ds(spot_of * ROWS + k * SPAN + half, 8)
-                        values = pltpu.roll(load(half), wrapped(SPAN * q - y0), 1)
-                        mine = (lane >= SPAN * q) & (lane < SPAN * (q + 1))
-                        out[spot, :] = jnp.where(mine, values, out[spot, :])
-
                 for i in range(SPAN):
                     p = x0 + i
-                    strips = [(n, s, t) for n, (s, t, j) in enumerate(STRIPS) if j == i]
 
                     @pl.when((p >= 0) & (p < width))
                     def _():
-                        for n, s, t in strips:
-                            place(n, lambda half: wave[s, t, pl.ds(p * DEPTH + z0 + half, 8), :])
+                        for s, t in ((0, 0), (0, 1), (1, 0), (1, 1)):
+                            for half in (0, SPAN - 8):
+                                near[s, t, i, pl.ds(half, 8), :] = wave[s, t, pl.ds(p * DEPTH + z0 + half, 8), :]
 
                     @pl.when(((p >= -2) & (p < 0)) | ((p >= width) & (p < width + 2)))
                     def _():
                         side = jnp.where(p < 0, 0, 1)
                         j = jnp.where(p < 0, p + 2, p - width)
-                        for n, s, t in strips:
-                            top = (2 * s + j if t else 4 + s) * DEPTH + z0
-                            place(n, lambda half: sides[side, pl.ds(top + half, 8), :])
+                        for s, t in ((0, 0), (0, 1), (1, 0), (1, 1)):
+                            top = (3 * s + (j if t else 2)) * DEPTH + z0
+                            for half in (0, SPAN - 8):
+                                near[s, t, i, pl.ds(half, 8), :] = sides[side, pl.ds(top + half, 8), :]
+
+                for row in range(0, ROWS, SPAN):
+                    packed = jnp.zeros((16, 128), jnp.float32)
+                    for s, t, i, _, start, y, count in (strip for strip in STRIPS if strip[3] == row):
+                        values = pltpu.roll(near[s, t, i], wrapped(start - y - y0), 1)
+                        packed = jnp.where((lane >= start) & (lane < start + count), values, packed)
+                    spot = n * ROWS + row
+                    out[pl.ds(spot, 8), :] = packed[:8]
+                    out[pl.ds(spot + 8, SPAN - 8), :] = packed[8:SPAN]
 
         for out, members in zip(outs, packs):
 
@@ -164,16 +188,16 @@
 def march_kernel(width, rows_of, *refs):
     @pl.when(rows_of(lax.axis_index("probe")))
     def _():
-        march(width, *refs[:14], *refs[-8:])
+        march(width, *refs[:15], *refs[-9:])
 
 
 def march(
-    width, xb, zb, yb, sx, sz, sy, wavelet, wave, stiff, buoy, swap_b, swap_a, pstiff, pbuoy, out, prep, fields,
-    sides, mid, later, weights, sem_out,
+    width, xb, zb, yb, sx, sz, sy, wavelet, wave, stiff, buoy, swap_b, swap_a, swap_c, pstiff, pbuoy, out, prep, fields,
+    sides, mid, later, weights, near, sem_out,
 ):
     first = lax.axis_index("gx") * width
     row = lax.axis_index("probe")
-    keep_sides(swap_a, swap_b, sides)
+    keep_sides((swap_a, swap_b, swap_c), sides)
     lane = lax.broadcasted_iota(jnp.int32, (DEPTH, 128), 1)
     depth = lax.broadcasted_iota(jnp.int32, (DEPTH, 128), 0)
     top, bottom = depth == 0, depth == DEPTH - 1
@@ -181,14 +205,14 @@
 
     def present(s, p):
         if isinstance(p, int) and p < 0:
-            return sides[0, plane_rows(2 * s + p + 2), :]
+            return sides[0, plane_rows(3 * s + p + 2), :]
         if isinstance(p, int) and p >= width:
-            return sides[1, plane_rows(2 * s + p - width), :]
+            return sides[1, plane_rows(3 * s + p - width), :]
         return wave[s, 1, plane_rows(p), :]
 
     def earlier(s, p):
         if isinstance(p, int) and (p < 0 or p >= width):
-            return sides[0 if p < 0 else 1, plane_rows(4 + s), :]
+            return sides[0 if p < 0 else 1, plane_rows(3 * s + 2), :]
         return wave[s, 0, plane_rows(p), :]
 
     def coefficients(p):
@@ -253,17 +277,16 @@
 
     lax.fori_loop(1, width - 1, step_one, 0, unroll=width - 2)
 
+    sources = [at(sx, s) - first for s in range(2)]
+
     def inject(ref, step, low, high, shift):
-        for s in range(2):
-            @pl.when(row == 0)
+        for s, x in enumerate(sources):
+
+            @pl.when((row == 0) & (x >= low) & (x < high))
             def _():
-                x = at(sx, s) - first
-
-                @pl.when((x >= low) & (x < high))
-                def _():
-                    hit = (lane == at(sy, s)) & (depth == at(sz, s))
-                    spot = plane_rows(x + shift)
-                    ref[s, spot, :] = ref[s, spot, :] + jnp.where(hit, at(wavelet.at[s], step), 0.0)
+                hit = (lane == at(sy, s)) & (depth == at(sz, s))
+                spot = plane_rows(x + shift)
+                ref[s, spot, :] = ref[s, spot, :] + jnp.where(hit, at(wavelet.at[s], step), 0.0)
 
     inject(mid, 0, -1, width + 1, 1)
     outs = copy_all([(mid.at[s, plane_rows(1, width)], out.at[s, 0]) for s in range(2)], sem_out)
@@ -293,11 +316,11 @@
     def _():
         strip = lax.broadcasted_iota(jnp.int32, (8, 128), 1)
         here = (strip < SPAN) & (strip + y0 >= 0) & (strip + y0 < 128)
-        prep[...] = jnp.zeros(prep.shape, jnp.float32)
+        near[...] = jnp.zeros(near.shape, jnp.float32)
 
         def bring(n, i, load):
             for half in (0, SPAN - 8):
-                prep[n, i, pl.ds(half, 8), :] = jnp.where(here, pltpu.roll(load(half), wrapped(-y0), 1), 0.0)
+                near[n, i, pl.ds(half, 8), :] = jnp.where(here, pltpu.roll(load(half), wrapped(-y0), 1), 0.0)
 
         for i in range(SPAN):
             p = x0 + i
@@ -307,8 +330,8 @@
                 bring(0, i, lambda half: buoy[pl.ds(p * DEPTH + z0 + half, 8), :])
                 bring(1, i, lambda half: stiff[pl.ds(p * DEPTH + z0 + half, 8), :])
                 for s in range(2):
-                    fields[i, s, 0] = mid[s, plane_rows(p + 1), :]
-                    fields[i, s, 1] = later[s, plane_rows(p), :]
+                    fields[i, s, 0, pl.ds(0, DEPTH), :] = mid[s, plane_rows(p + 1), :]
+                    fields[i, s, 1, pl.ds(0, DEPTH), :] = later[s, plane_rows(p), :]
 
             side = jnp.where(p < 0, 0, 1)
             j = jnp.where(p < 0, p + 2, p - width)
@@ -328,7 +351,24 @@
         for n, ref in ((2, pstiff), (3, pbuoy)):
             for i in range(EDGE):
                 column = jnp.sum(jnp.where(wide == g, ref[i], 0.0), axis=2, keepdims=True)
-                prep[n, 2 + i, pl.ds(dz, EDGE), :] = jnp.sum(jnp.where(diagonal, column, 0.0), axis=1)
+                near[n, 2 + i, pl.ds(dz, EDGE), :] = jnp.sum(jnp.where(diagonal, column, 0.0), axis=1)
+
+        none = jnp.zeros((16, 128), jnp.float32)
+
+        def faces(n, i):
+            c = near[n, i]
+            x = [0.5 * (c + near[n, i + d]) if 0 <= i + d < SPAN else none for d in (-1, 1)]
+            z, y = 0.5 * (c + pltpu.roll(c, 15, 0)), 0.5 * (c + pltpu.roll(c, 127, 1))
+            return [*x, pltpu.roll(z, 1, 0), z, pltpu.roll(y, 1, 1), y]
+
+        for i in range(SPAN):
+            k, sb = near[1, i], near[2, i]
+            forced, free = none, 2.0 + none
+            for n, (a, b) in enumerate(zip(faces(0, i), faces(3, i))):
+                given, own = sb * a + k * b, k * a
+                prep[n, i], prep[7 + n, i] = given, own
+                forced, free = forced - given, free - own
+            prep[6, i], prep[13, i] = forced, free
 
     wait_all(outs)
 
@@ -337,7 +377,7 @@
     count = len(FIRST) + len(DIRECT)
     longest = max(len(rest) for rest in NEXT)
     firsts, directs, nexts = refs[: len(FIRST)], refs[len(FIRST) : count], refs[count : count + longest]
-    prep, fields, _, out, piece, planes, sem = refs[count + longest :]
+    prep, fields, _, out, piece, planes, now, later, forced, sem = refs[count + longest :]
     row = lax.axis_index("probe")
     g = jnp.maximum(row - 1, 0)
     first = lax.axis_index("gx") * width
@@ -348,7 +388,7 @@
         def bring(where, source):
             @pl.when(where)
             def _():
-                piece[...] = source[pl.ds(0, ROWS), :]
+                piece[pl.ds(0, ROWS), :] = source[pl.ds(0, ROWS), :]
 
         for target, source in zip(FIRST + DIRECT, (*firsts, *directs)):
             bring(row == target, source)
@@ -359,74 +399,76 @@
                     where = where | (row == rest[n])
             bring(where, source)
 
+        planes[...] = fields[...]
         lane = lax.broadcasted_iota(jnp.int32, (16, 128), 1)
         depth = lax.broadcasted_iota(jnp.int32, (16, 128), 0)
         here = (lane < SPAN) & (depth < SPAN) & (lane + y0 >= 0) & (lane + y0 < 128)
-        c, k, sb, bb = (prep[n] for n in range(4))
-
-        def field(s, t):
-            got = []
+        inner = here & (lane >= 1) & (lane < SPAN - 1)
+        blank = jnp.zeros((8, 128), jnp.float32)
+        for ref in (now, later, forced):
+            for s in range(2):
+                for i in range(SPAN + 1):
+                    ref[s, pl.ds(i * GRID, 8), :] = blank
+
+        def strip(s, t, i):
+            found = [strip for strip in STRIPS if strip[:3] == (s, t, i)]
+            if not found:
+                return jnp.zeros((16, 128), jnp.float32)
+            _, _, _, row, start, y, _ = found[0]
+            values = piece[pl.ds(row, 16), :]
+            if start != y:
+                values = pltpu.roll(values, (y - start) % 128, 1)
+            x = x0 + i
+            ok = (first + x >= 0) & (first + x < extent) & (x >= -1 - t) & (x < width + 1 + t)
+            return jnp.where((here if t else inner) & ok, values, 0.0)
+
+        def cells(i, shift=0):
+            return pl.ds(i * GRID + 8 + shift, 16)
+
+        def around(ref, s, i):
+            v = ref[s, cells(i), :]
+            x = [ref[s, cells(i + d), :] if 0 <= i + d < SPAN else None for d in (-1, 1)]
+            z = [ref[s, cells(i, d), :] for d in (-1, 1)]
+            return [*x, *z, pltpu.roll(v, 1, 1), pltpu.roll(v, 127, 1), v]
+
+        def weighted(w, values):
+            terms = [a * b for a, b in zip(w, values) if b is not None]
+            return functools.reduce(jnp.add, terms)
+
+        for s in range(2):
             for i in range(SPAN):
-                if (s, t, i) not in STRIPS:
-                    got.append(jnp.zeros((16, 128), jnp.float32))
-                    continue
-                n, q = divmod(STRIPS.index((s, t, i)), PER_ROW)
-                values = piece[pl.ds(n * SPAN, 16), :]
-                if q:
-                    values = pltpu.roll(values, 128 - SPAN * q, 1)
-                x = x0 + i
-                ok = (first + x >= 0) & (first + x < extent) & (x >= -1 - t) & (x < width + 1 + t)
-                got.append(jnp.where(here & ok, values, 0.0))
-            return jnp.stack(got)
-
-        def up(v, axis):
-            return pltpu.roll(v, v.shape[axis] - 1, axis)
-
-        def faces(coef):
-            return 0.5 * (coef[1:] + coef[:-1]), 0.5 * (coef + up(coef, 1)), 0.5 * (coef + up(coef, 2))
-
-        def steps(v):
-            return v[1:] - v[:-1], up(v, 1) - v, up(v, 2) - v
-
-        def gather(coef, step):
-            fx, fz, fy = (a * b for a, b in zip(coef, step))
-            zero = jnp.zeros((1, 16, 128), jnp.float32)
-            total = jnp.concatenate([fx, zero], 0) - jnp.concatenate([zero, fx], 0)
-            total += fz - pltpu.roll(fz, 1, 1)
-            total += fy - pltpu.roll(fy, 1, 2)
-            return total
-
-        of_c = faces(c)
-        of_b = faces(bb)
+                now[s, cells(i), :] = strip(s, 1, i)
+        shots = []
         for s in range(2):
-            now = field(s, 1)
-            step = steps(now)
-            laplace = gather(of_c, step)
-            forcing = sb * laplace + k * gather(of_b, step)
             hit = here & (lane + y0 == at(sy, s)) & (depth + z0 == at(sz, s))
-            x, amplitude = at(sx, s), at(wavelet.at[s], 0)
-            source = []
-            for i in range(SPAN):
-                source.append(jnp.where(hit & (first + x0 + i == x), amplitude, 0.0))
-            then = steps(2.0 * now - field(s, 0) + k * laplace + jnp.stack(source))
-            second = sb * gather(of_c, then) + k * gather(of_b, then)
-            gains = (forcing, 2.0 * forcing + k * gather(of_c, steps(forcing)) + second)
-            for t in range(2):
-                moved = pltpu.roll(gains[t], wrapped(y0), 2)
-                for i in range(SPAN):
-                    planes[i, s, t, pl.ds(0, DEPTH), :] = fields[i, s, t]
-                    spot = pl.ds(z0, 16)
-                    planes[i, s, t, spot, :] = planes[i, s, t, spot, :] + moved[i]
-
-        def each_plane(act):
-            for i in range(SPAN):
+            shots.append((at(sx, s) - first - x0, jnp.where(hit, at(wavelet.at[s], 0), 0.0)))
+        for i in range(SPAN):
+            of_forcing, of_step = ([prep[n + m, i] for n in range(7)] for m in (0, 7))
+            for s, (x, source) in enumerate(shots):
+                values = around(now, s, i)
+                forced[s, cells(i), :] = weighted(of_forcing, values)
+                after = weighted(of_step, values) - strip(s, 0, i)
+                later[s, cells(i), :] = after + jnp.where(x == i, source, 0.0)
+
+        def each_plane(act, low=0, high=SPAN):
+            for i in range(low, high):
 
                 @pl.when((x0 + i >= 0) & (x0 + i < width))
                 def _():
                     target = out.at[:, :, plane_rows(x0 + i)]
                     act(pltpu.make_async_copy(planes.at[i, :, :, pl.ds(0, DEPTH)], target, sem.at[i]))
 
-        each_plane(lambda copy: copy.start())
+        part = SPAN // 3
+        for low in range(0, SPAN, part):
+            for i in range(low, low + part):
+                of_forcing, of_step = ([prep[n + m, i] for n in range(7)] for m in (0, 7))
+                for s in range(2):
+                    gain = forced[s, cells(i), :]
+                    more = weighted(of_step, around(forced, s, i)) + weighted(of_forcing, around(later, s, i))
+                    for t, value in enumerate((gain, more)):
+                        spot = pl.ds(z0, 16)
+                        planes[i, s, t, spot, :] = fields[i, s, t, spot, :] + pltpu.roll(value, wrapped(y0), 1)
+            each_plane(lambda copy: copy.start(), low, low + part)
         each_plane(lambda copy: copy.wait())
 
 
@@ -463,45 +505,48 @@
         every = [(a * slabs + s, b * slabs + s) for a, b in pairs for s in range(slabs)]
         return lax.ppermute(value, ("probe", "gx"), every)
 
-    def swap(value, start):
-        pairs = [(s, s + 1) for s in range(start, slabs - 1, 2)]
-        return lax.ppermute(value, "gx", pairs + [(b, a) for a, b in pairs])
-
-    edge = vmem(9 * DEPTH, 128)
-    edge_a, edge_b = call(
-        functools.partial(edge_kernel, width), "edges", [edge, edge], [pltpu.HBM] * 3, [dma(12)]
-    )(wave, stiff, buoy)
-    swap_a, swap_b = swap(edge_a, 0), swap(edge_b, 1)
+    def swap(value, pairs):
+        both = [(row, a, b) for row, low in pairs for a, b in ((low, low + 1), (low + 1, low))]
+        return lax.ppermute(value, ("probe", "gx"), [(row * slabs + a, row * slabs + b) for row, a, b in both])
+
+    edge = vmem(3, 3, DEPTH, 128)
+    edge_a, edge_b, edge_c = call(
+        functools.partial(edge_kernel, width), "edges", [edge] * 3, [pltpu.HBM] * 3, [dma(8)]
+    )(wavefields[0], stiffness, buoyancy)
+    edge_a, edge_b, edge_c = (edges.reshape(-1, 128) for edges in (edge_a, edge_b, edge_c))
+    rounds = swap_pairs(lax.axis_size("probe"), slabs)
+    swaps = [swap(*each) for each in zip((edge_a, edge_b, edge_c), rounds)]
 
     counts = [1 + len(rest) for rest in NEXT] + [1] * len(DIRECT)
     packs = call(
         functools.partial(split_kernel, width),
         "split",
         [vmem(n * ROWS, 128) for n in counts],
-        [pltpu.VMEM] * 6,
-        [vmem(2, 9 * DEPTH, 128)],
-    )(*blocks, wave, swap_b, swap_a)
+        [pltpu.VMEM] * 7,
+        [vmem(2, 9 * DEPTH, 128), vmem(2, 2, SPAN, 16, 128)],
+    )(*blocks, wave, swaps[1], swaps[0], swaps[2])
     got = [along_rows(p, [(0, row)]) for p, row in zip(packs, FIRST + DIRECT)]
 
     def march_on(name, rows_of, before=()):
-        marched = [hbm(2, 2, rows, 128), vmem(4, SPAN, 16, 128), vmem(SPAN, 2, 2, DEPTH, 128)]
-        operands = (*blocks, *sources, wave, stiff, buoy, swap_b, swap_a, *perts, *before)
+        marched = [hbm(2, 2, rows, 128), vmem(14, SPAN, 16, 128), vmem(SPAN, 2, 2, DEPTH + 8, 128)]
+        operands = (*blocks, *sources, wave, stiff, buoy, swaps[1], swaps[0], swaps[2], *perts, *before)
         return call(
             functools.partial(march_kernel, width, rows_of),
             name,
             marched,
-            [pltpu.VMEM] * 14 + [pltpu.HBM, pltpu.VMEM, pltpu.VMEM, pltpu.VMEM][: len(before)],
+            [pltpu.VMEM] * 15 + [pltpu.HBM, pltpu.VMEM, pltpu.VMEM, pltpu.VMEM][: len(before)],
             [
                 vmem(2, 9 * DEPTH, 128),
                 vmem(2, (width + 2) * DEPTH, 128),
                 vmem(2, rows, 128),
                 vmem(7, rows, 128),
+                vmem(4, SPAN, 16, 128),
                 dma(8),
             ],
-            input_output_aliases={14: 0, 15: 1, 16: 2} if before else {},
+            input_output_aliases={15: 0, 16: 1, 17: 2} if before else {},
         )(*operands)
 
-    late = lambda row: functools.reduce(jnp.logical_or, [row == r for r in FIRST[1:]])
+    late = lambda row: functools.reduce(jnp.logical_or, [row == r for r in FIRST])
     marched = march_on("march_first", late)
 
     longest = max(len(rest) for rest in NEXT)
@@ -519,7 +564,12 @@
         "born",
         hbm(2, 2, rows, 128),
         [pltpu.VMEM] * (len(operands) - 1) + [pltpu.HBM],
-        [vmem(ROWS, 128), vmem(SPAN, 2, 2, DEPTH + 8, 128), dma(SPAN)],
+        [
+            vmem(ROWS + 8, 128),
+            vmem(SPAN, 2, 2, DEPTH + 8, 128),
+            *[vmem(2, SPAN * GRID + 8, 128)] * 3,
+            dma(SPAN),
+        ],
         input_output_aliases={len(operands) - 1: 0},
     )(*operands)
     return result.reshape(wavefields.shape)

time: 31.7 us -> 31.1 us (0.981)
  the two profiles are of different devices: /device:TPU:361 before, /device:TPU:52 now
where the time goes in v5:
time: 31.1 us; the launch traced here: 30.8 us
  starting transfers between devices  12.8 us (41%)
  waiting for transfers between devices  9.91 us (32%)
  Pallas kernels  7.65 us (25%)
  between operations  0.35 us (1%)
    pallas_call x6, Pallas kernels, call(): made(*map(pltpu.with_memory_space_constraint, args, spaces))  7.65 us
    ppermute x9, starting transfers between devices, along_rows(): return lax.ppermute(value, ('probe', 'gx'), every)  6.61 us
    ppermute x3, starting transfers between devices, swap(): lax.ppermute(value, ('probe', 'gx'), [(row * slabs + a, row * slabs + b)...  6.19 us
    ppermute x3, waiting for transfers between devices, swap(): lax.ppermute(value, ('probe', 'gx'), [(row * slabs + a, row * slabs + b)...  5.23 us
    ppermute x9, waiting for transfers between devices, along_rows(): return lax.ppermute(value, ('probe', 'gx'), every)  4.68 us
  transfers between devices with their start and end apart: 12, of which 3 were waited for; matrix products, arithmetic and copies ran while one was open for 0% of the time, Pallas kernels for 12%

profile of v5, /device:TPU:52, one launch (start us, length us, event | category | flops | bytes accessed | tf_op | source)
XLA Modules:
  0.0 30.8 jit_solution(15534823687864951765)
XLA Ops:
  0.0 1.1 %edges.1 = (f32[3,3,32,128]{3,2,1,0:T(8,128)S(1)}, f32[3,3,32,128]{3,2,1,0:T(8,128)S(1)}, f32[3,3,32,128]{3,2,1,0:T(8,128)S(1)}) custom-call(f32[2,2,24,32,128]{4,3,2,1,0:T(8,128)} %bitcast.10, f32[24,32,128]{2,1,0:T(8,128)} %stiff.1, f32[24,32,128]{2,1,0:T(8,128)} %buoy.1), custom_call_target="tpu_custom_call" | custom-call | tf_op jit(solution)/shard_map/edges/pallas_call | solution.py:502
  1.2 0.0 copy-start.1
  1.2 0.0 copy-start.2
  1.2 0.0 copy-start.4
  1.2 0.0 copy-start.5
  1.2 0.0 copy-start.11
  1.2 3.3 %collective-permute-start.1 = (f32[288,128]{1,0:T(8,128)S(1)}, f32[288,128]{1,0:T(8,128)S(1)}, u32[]{:S(2)}, u32[]{:S(2)}) collective-permute-start(f32[288,128]{1,0:T(8,128)S(1)} %bitcast.24), channel_id=1, source_target_pairs={{1,2},{2,1},{4,5},{5,4},{6,7},{7,6},{8,9},{9,8},{10,11},{11,10},{1... | collective-permute-start | bytes 442376 | tf_op jit(solution)/shard_map/ppermute | solution.py:510
  4.6 2.2 %collective-permute-start = (f32[288,128]{1,0:T(8,128)S(1)}, f32[288,128]{1,0:T(8,128)S(1)}, u32[]{:S(2)}, u32[]{:S(2)}) collective-permute-start(f32[288,128]{1,0:T(8,128)S(1)} %bitcast.23), channel_id=1, source_target_pairs={{0,1},{1,0},{3,4},{4,3},{5,6},{6,5},{7,8},{8,7},{9,10},{10,9},{11,... | collective-permute-start | bytes 442376 | tf_op jit(solution)/shard_map/ppermute | solution.py:510
  6.8 0.7 %collective-permute-start.2 = (f32[288,128]{1,0:T(8,128)S(1)}, f32[288,128]{1,0:T(8,128)S(1)}, u32[]{:S(2)}, u32[]{:S(2)}) collective-permute-start(f32[288,128]{1,0:T(8,128)S(1)} %bitcast.22), channel_id=1, source_target_pairs={{2,3},{3,2}} | collective-permute-start | bytes 442376 | tf_op jit(solution)/shard_map/ppermute | solution.py:510
  7.5 1.4 %collective-permute-done.1.swap_a.refs_11_ = f32[288,128]{1,0:T(8,128)S(1)} collective-permute-done((f32[288,128]{1,0:T(8,128)S(1)}, f32[288,128]{1,0:T(8,128)S(1)}, u32[]{:S(2)}, u32[]{:S(2)}) %collective-permute-start.1) | collective-permute-done | bytes 147488 | tf_op jit(solution)/shard_map/ppermute | solution.py:510
  8.9 3.8 %collective-permute-done.swap_b.refs_10_ = f32[288,128]{1,0:T(8,128)S(1)} collective-permute-done((f32[288,128]{1,0:T(8,128)S(1)}, f32[288,128]{1,0:T(8,128)S(1)}, u32[]{:S(2)}, u32[]{:S(2)}) %collective-permute-start) | collective-permute-done | bytes 147488 | tf_op jit(solution)/shard_map/ppermute | solution.py:510
  12.7 0.7 %collective-permute-start.3 = (f32[240,128]{1,0:T(8,128)S(1)}, f32[240,128]{1,0:T(8,128)S(1)}, u32[]{:S(2)}, u32[]{:S(2)}) collective-permute-start(f32[240,128]{1,0:T(8,128)S(1)} %get-tuple-element.26), channel_id=1, source_target_pairs={{0,32},{1,33},{2,34},{3,35},{4,36},{5,37},{6,38},{7,39},{8,40},{9,... | collective-permute-start | bytes 368648 | tf_op jit(solution)/shard_map/ppermute | solution.py:506
  13.4 0.7 %collective-permute-start.4 = (f32[192,128]{1,0:T(8,128)S(1)}, f32[192,128]{1,0:T(8,128)S(1)}, u32[]{:S(2)}, u32[]{:S(2)}) collective-permute-start(f32[192,128]{1,0:T(8,128)S(1)} %get-tuple-element.27), channel_id=1, source_target_pairs={{0,64},{1,65},{2,66},{3,67},{4,68},{5,69},{6,70},{7,71},{8,72},{9,... | collective-permute-start | bytes 294920 | tf_op jit(solution)/shard_map/ppermute | solution.py:506
  14.1 0.7 %collective-permute-start.5 = (f32[144,128]{1,0:T(8,128)S(1)}, f32[144,128]{1,0:T(8,128)S(1)}, u32[]{:S(2)}, u32[]{:S(2)}) collective-permute-start(f32[144,128]{1,0:T(8,128)S(1)} %get-tuple-element.28), channel_id=1, source_target_pairs={{0,192},{1,193},{2,194},{3,195},{4,196},{5,197},{6,198},{7,199},{8... | collective-permute-start | bytes 221192 | tf_op jit(solution)/shard_map/ppermute | solution.py:506
  14.8 0.7 %collective-permute-start.6 = (f32[96,128]{1,0:T(8,128)S(1)}, f32[96,128]{1,0:T(8,128)S(1)}, u32[]{:S(2)}, u32[]{:S(2)}) collective-permute-start(f32[96,128]{1,0:T(8,128)S(1)} %get-tuple-element.29), channel_id=1, source_target_pairs={{0,256},{1,257},{2,258},{3,259},{4,260},{5,261},{6,262},{7,263},{8... | collective-permute-start | bytes 147464 | tf_op jit(solution)/shard_map/ppermute | solution.py:506
  15.4 0.7 %collective-permute-start.7 = (f32[48,128]{1,0:T(8,128)S(1)}, f32[48,128]{1,0:T(8,128)S(1)}, u32[]{:S(2)}, u32[]{:S(2)}) collective-permute-start(f32[48,128]{1,0:T(8,128)S(1)} %get-tuple-element.30), channel_id=1, source_target_pairs={{0,416},{1,417},{2,418},{3,419},{4,420},{5,421},{6,422},{7,423},{8... | collective-permute-start | bytes 73736 | tf_op jit(solution)/shard_map/ppermute | solution.py:506
  16.2 0.1 march_first.1
  16.4 0.7 %collective-permute-start.8 = (f32[48,128]{1,0:T(8,128)S(1)}, f32[48,128]{1,0:T(8,128)S(1)}, u32[]{:S(2)}, u32[]{:S(2)}) collective-permute-start(f32[48,128]{1,0:T(8,128)S(1)} %get-tuple-element.32), channel_id=1, source_target_pairs={{32,288},{33,289},{34,290},{35,291},{36,292},{37,293},{38,294},{39... | collective-permute-start | bytes 73736 | tf_op jit(solution)/shard_map/ppermute | solution.py:506
  17.0 0.7 %collective-permute-start.9 = (f32[48,128]{1,0:T(8,128)S(1)}, f32[48,128]{1,0:T(8,128)S(1)}, u32[]{:S(2)}, u32[]{:S(2)}) collective-permute-start(f32[48,128]{1,0:T(8,128)S(1)} %get-tuple-element.33), channel_id=1, source_target_pairs={{32,96},{33,97},{34,98},{35,99},{36,100},{37,101},{38,102},{39,103... | collective-permute-start | bytes 73736 | tf_op jit(solution)/shard_map/ppermute | solution.py:506
  17.7 1.3 %collective-permute-start.10 = (f32[48,128]{1,0:T(8,128)S(1)}, f32[48,128]{1,0:T(8,128)S(1)}, u32[]{:S(2)}, u32[]{:S(2)}) collective-permute-start(f32[48,128]{1,0:T(8,128)S(1)} %get-tuple-element.34), channel_id=1, source_target_pairs={{32,224},{33,225},{34,226},{35,227},{36,228},{37,229},{38,230},{39... | collective-permute-start | bytes 73736 | tf_op jit(solution)/shard_map/ppermute | solution.py:506
  19.0 0.7 %collective-permute-start.11 = (f32[48,128]{1,0:T(8,128)S(1)}, f32[48,128]{1,0:T(8,128)S(1)}, u32[]{:S(2)}, u32[]{:S(2)}) collective-permute-start(f32[48,128]{1,0:T(8,128)S(1)} %get-tuple-element.35.refs_18_), channel_id=1, source_target_pairs={{32,160},{33,161},{34,162},{35,163},{36,164},{37,165},{38,166},{39... | collective-permute-start | bytes 73736 | tf_op jit(solution)/shard_map/ppermute | solution.py:506
  19.7 3.4 %march_rest.1 = (f32[2,2,768,128]{3,2,1,0:T(8,128)}, f32[14,12,16,128]{3,2,1,0:T(8,128)S(1)}, f32[12,2,2,40,128]{4,3,2,1,0:T(8,128)S(1)}) custom-call(s32[15]{0:T(128)S(1)} %copy-done.6, s32[15]{0:T(128)S(1)} %copy-done.7, s32[15]{0:T(128)S(1)} %copy-done.8, s32[2]{0:T(128)S(1)} %copy-done.9, ...), custom_call_target="tpu_custom_call", output_to_operand_aliasing={{0}: (15, {}), {1}: (16, {}), {2}: (17, {})} | custom-call | tf_op jit(solution)/shard_map/march_rest/pallas_call | solution.py:502
  23.2 4.7 %collective-permute-done.10.refs_7_ = f32[48,128]{1,0:T(8,128)S(1)} collective-permute-done((f32[48,128]{1,0:T(8,128)S(1)}, f32[48,128]{1,0:T(8,128)S(1)}, u32[]{:S(2)}, u32[]{:S(2)}) %collective-permute-start.10) | collective-permute-done | bytes 24608 | tf_op jit(solution)/shard_map/ppermute | solution.py:506
  27.8 3.0 %born.1 = f32[2,2,768,128]{3,2,1,0:T(8,128)} custom-call(s32[15]{0:T(128)S(1)} %copy-done.6, s32[15]{0:T(128)S(1)} %copy-done.7, s32[15]{0:T(128)S(1)} %copy-done.8, s32[2]{0:T(128)S(1)} %copy-done.9, s32[2]{0:T(128)S(1)} %copy-done.10, s32[2]{0:T(128)S(1)} %copy-done.11, f32[2,2]{1,0:T(2,128)S(1)} %copy-done.5, ...), custom_call_target="tpu_custom_call", output_to_operand_aliasing={{}: (18, {})} | custom-call | tf_op jit(solution)/shard_map/born/pallas_call | solution.py:502
  (30 shorter events, 0.1 us)
Async XLA Ops:
  0.0 12.7 %copy-start = (f32[1,2,2,24,32,128]{5,4,3,2,1,0:T(8,128)S(1)}, f32[1,2,2,24,32,128]{5,4,3,2,1,0:T(8,128)}, u32[]{:S(2)}) copy-start(f32[1,2,2,24,32,128]{5,4,3,2,1,0:T(8,128)} %param.12) | copy-start | bytes 4718596
  0.0 12.7 %copy-start.8 = (s32[15]{0:T(128)S(1)}, s32[15]{0:T(128)}, u32[]{:S(2)}) copy-start(s32[15]{0:T(128)} %yb.3) | copy-start | bytes 184
  0.0 12.7 %copy-start.7 = (s32[15]{0:T(128)S(1)}, s32[15]{0:T(128)}, u32[]{:S(2)}) copy-start(s32[15]{0:T(128)} %zb.3) | copy-start | bytes 184
  0.0 12.7 %copy-start.6 = (s32[15]{0:T(128)S(1)}, s32[15]{0:T(128)}, u32[]{:S(2)}) copy-start(s32[15]{0:T(128)} %xb.3) | copy-start | bytes 184
  1.2 15.0 %copy-start.1 = (f32[24,32,128]{2,1,0:T(8,128)S(1)}, f32[24,32,128]{2,1,0:T(8,128)}, u32[]{:S(2)}) copy-start(f32[24,32,128]{2,1,0:T(8,128)} %stiff.1) | copy-start | bytes 1179652
  1.2 15.0 %copy-start.2 = (f32[24,32,128]{2,1,0:T(8,128)S(1)}, f32[24,32,128]{2,1,0:T(8,128)}, u32[]{:S(2)}) copy-start(f32[24,32,128]{2,1,0:T(8,128)} %buoy.1) | copy-start | bytes 1179652
  1.2 15.0 %copy-start.3 = (f32[15,8,8,8]{0,3,2,1:T(8,128)S(1)}, f32[15,8,8,8]{0,3,2,1:T(8,128)}, u32[]{:S(2)}) copy-start(f32[15,8,8,8]{0,3,2,1:T(8,128)} %param.15) | copy-start | bytes 92164
  1.2 15.0 %copy-start.4 = (f32[15,8,8,8]{0,3,2,1:T(8,128)S(1)}, f32[15,8,8,8]{0,3,2,1:T(8,128)}, u32[]{:S(2)}) copy-start(f32[15,8,8,8]{0,3,2,1:T(8,128)} %param.16) | copy-start | bytes 92164
  1.2 15.0 %copy-start.5 = (f32[2,2]{1,0:T(2,128)S(1)}, f32[2,2]{1,0:T(2,128)}, u32[]{:S(2)}) copy-start(f32[2,2]{1,0:T(2,128)} %wavelet.1) | copy-start | bytes 52
  1.2 15.0 %copy-start.9 = (s32[2]{0:T(128)S(1)}, s32[2]{0:T(128)}, u32[]{:S(2)}) copy-start(s32[2]{0:T(128)} %sx.1) | copy-start | bytes 28
  1.2 15.0 %copy-start.10 = (s32[2]{0:T(128)S(1)}, s32[2]{0:T(128)}, u32[]{:S(2)}) copy-start(s32[2]{0:T(128)} %sz.1) | copy-start | bytes 28
  1.2 14.9 %copy-start.11 = (s32[2]{0:T(128)S(1)}, s32[2]{0:T(128)}, u32[]{:S(2)}) copy-start(s32[2]{0:T(128)} %sy.1) | copy-start | bytes 28
  1.2 7.6 %collective-permute-start.1 = (f32[288,128]{1,0:T(8,128)S(1)}, f32[288,128]{1,0:T(8,128)S(1)}, u32[]{:S(2)}, u32[]{:S(2)}) collective-permute-start(f32[288,128]{1,0:T(8,128)S(1)} %bitcast.24), channel_id=1, source_target_pairs={{1,2},{2,1},{4,5},{5,4},{6,7},{7,6},{8,9},{9,8},{10,11},{11,10},{1... | collective-permute-start | bytes 442376 | tf_op jit(solution)/shard_map/ppermute | solution.py:510
  4.6 8.1 %collective-permute-start = (f32[288,128]{1,0:T(8,128)S(1)}, f32[288,128]{1,0:T(8,128)S(1)}, u32[]{:S(2)}, u32[]{:S(2)}) collective-permute-start(f32[288,128]{1,0:T(8,128)S(1)} %bitcast.23), channel_id=1, source_target_pairs={{0,1},{1,0},{3,4},{4,3},{5,6},{6,5},{7,8},{8,7},{9,10},{10,9},{11,... | collective-permute-start | bytes 442376 | tf_op jit(solution)/shard_map/ppermute | solution.py:510
  6.8 5.9 %collective-permute-start.2 = (f32[288,128]{1,0:T(8,128)S(1)}, f32[288,128]{1,0:T(8,128)S(1)}, u32[]{:S(2)}, u32[]{:S(2)}) collective-permute-start(f32[288,128]{1,0:T(8,128)S(1)} %bitcast.22), channel_id=1, source_target_pairs={{2,3},{3,2}} | collective-permute-start | bytes 442376 | tf_op jit(solution)/shard_map/ppermute | solution.py:510
  12.7 3.6 %collective-permute-start.3 = (f32[240,128]{1,0:T(8,128)S(1)}, f32[240,128]{1,0:T(8,128)S(1)}, u32[]{:S(2)}, u32[]{:S(2)}) collective-permute-start(f32[240,128]{1,0:T(8,128)S(1)} %get-tuple-element.26), channel_id=1, source_target_pairs={{0,32},{1,33},{2,34},{3,35},{4,36},{5,37},{6,38},{7,39},{8,40},{9,... | collective-permute-start | bytes 368648 | tf_op jit(solution)/shard_map/ppermute | solution.py:506
  13.4 2.9 %collective-permute-start.4 = (f32[192,128]{1,0:T(8,128)S(1)}, f32[192,128]{1,0:T(8,128)S(1)}, u32[]{:S(2)}, u32[]{:S(2)}) collective-permute-start(f32[192,128]{1,0:T(8,128)S(1)} %get-tuple-element.27), channel_id=1, source_target_pairs={{0,64},{1,65},{2,66},{3,67},{4,68},{5,69},{6,70},{7,71},{8,72},{9,... | collective-permute-start | bytes 294920 | tf_op jit(solution)/shard_map/ppermute | solution.py:506
  14.1 2.2 %collective-permute-start.5 = (f32[144,128]{1,0:T(8,128)S(1)}, f32[144,128]{1,0:T(8,128)S(1)}, u32[]{:S(2)}, u32[]{:S(2)}) collective-permute-start(f32[144,128]{1,0:T(8,128)S(1)} %get-tuple-element.28), channel_id=1, source_target_pairs={{0,192},{1,193},{2,194},{3,195},{4,196},{5,197},{6,198},{7,199},{8... | collective-permute-start | bytes 221192 | tf_op jit(solution)/shard_map/ppermute | solution.py:506
  14.8 1.5 %collective-permute-start.6 = (f32[96,128]{1,0:T(8,128)S(1)}, f32[96,128]{1,0:T(8,128)S(1)}, u32[]{:S(2)}, u32[]{:S(2)}) collective-permute-start(f32[96,128]{1,0:T(8,128)S(1)} %get-tuple-element.29), channel_id=1, source_target_pairs={{0,256},{1,257},{2,258},{3,259},{4,260},{5,261},{6,262},{7,263},{8... | collective-permute-start | bytes 147464 | tf_op jit(solution)/shard_map/ppermute | solution.py:506
  15.4 7.7 %collective-permute-start.7 = (f32[48,128]{1,0:T(8,128)S(1)}, f32[48,128]{1,0:T(8,128)S(1)}, u32[]{:S(2)}, u32[]{:S(2)}) collective-permute-start(f32[48,128]{1,0:T(8,128)S(1)} %get-tuple-element.30), channel_id=1, source_target_pairs={{0,416},{1,417},{2,418},{3,419},{4,420},{5,421},{6,422},{7,423},{8... | collective-permute-start | bytes 73736 | tf_op jit(solution)/shard_map/ppermute | solution.py:506
  16.4 6.8 %collective-permute-start.8 = (f32[48,128]{1,0:T(8,128)S(1)}, f32[48,128]{1,0:T(8,128)S(1)}, u32[]{:S(2)}, u32[]{:S(2)}) collective-permute-start(f32[48,128]{1,0:T(8,128)S(1)} %get-tuple-element.32), channel_id=1, source_target_pairs={{32,288},{33,289},{34,290},{35,291},{36,292},{37,293},{38,294},{39... | collective-permute-start | bytes 73736 | tf_op jit(solution)/shard_map/ppermute | solution.py:506
  17.0 6.1 %collective-permute-start.9 = (f32[48,128]{1,0:T(8,128)S(1)}, f32[48,128]{1,0:T(8,128)S(1)}, u32[]{:S(2)}, u32[]{:S(2)}) collective-permute-start(f32[48,128]{1,0:T(8,128)S(1)} %get-tuple-element.33), channel_id=1, source_target_pairs={{32,96},{33,97},{34,98},{35,99},{36,100},{37,101},{38,102},{39,103... | collective-permute-start | bytes 73736 | tf_op jit(solution)/shard_map/ppermute | solution.py:506
  17.7 10.1 %collective-permute-start.10 = (f32[48,128]{1,0:T(8,128)S(1)}, f32[48,128]{1,0:T(8,128)S(1)}, u32[]{:S(2)}, u32[]{:S(2)}) collective-permute-start(f32[48,128]{1,0:T(8,128)S(1)} %get-tuple-element.34), channel_id=1, source_target_pairs={{32,224},{33,225},{34,226},{35,227},{36,228},{37,229},{38,230},{39... | collective-permute-start | bytes 73736 | tf_op jit(solution)/shard_map/ppermute | solution.py:506
  19.0 8.8 %collective-permute-start.11 = (f32[48,128]{1,0:T(8,128)S(1)}, f32[48,128]{1,0:T(8,128)S(1)}, u32[]{:S(2)}, u32[]{:S(2)}) collective-permute-start(f32[48,128]{1,0:T(8,128)S(1)} %get-tuple-element.35.refs_18_), channel_id=1, source_target_pairs={{32,160},{33,161},{34,162},{35,163},{36,164},{37,165},{38,166},{39... | collective-permute-start | bytes 73736 | tf_op jit(solution)/shard_map/ppermute | solution.py:506

commit v6 on v5

--- a/solution.py
+++ b/solution.py
@@ -377,7 +377,7 @@
     count = len(FIRST) + len(DIRECT)
     longest = max(len(rest) for rest in NEXT)
     firsts, directs, nexts = refs[: len(FIRST)], refs[len(FIRST) : count], refs[count : count + longest]
-    prep, fields, _, out, piece, planes, now, later, forced, sem = refs[count + longest :]
+    prep, fields, _, out, piece, planes, now, before, later, forced, sem = refs[count + longest :]
     row = lax.axis_index("probe")
     g = jnp.maximum(row - 1, 0)
     first = lax.axis_index("gx") * width
@@ -404,11 +404,13 @@
         depth = lax.broadcasted_iota(jnp.int32, (16, 128), 0)
         here = (lane < SPAN) & (depth < SPAN) & (lane + y0 >= 0) & (lane + y0 < 128)
         inner = here & (lane >= 1) & (lane < SPAN - 1)
-        blank = jnp.zeros((8, 128), jnp.float32)
+        blank, whole = jnp.zeros((8, 128), jnp.float32), jnp.zeros((GRID, 128), jnp.float32)
         for ref in (now, later, forced):
             for s in range(2):
-                for i in range(SPAN + 1):
+                for i in range(SPAN + 3):
                     ref[s, pl.ds(i * GRID, 8), :] = blank
+                for i in (0, SPAN + 1):
+                    ref[s, pl.ds(i * GRID, GRID), :] = whole
 
         def strip(s, t, i):
             found = [strip for strip in STRIPS if strip[:3] == (s, t, i)]
@@ -423,32 +425,37 @@
             return jnp.where((here if t else inner) & ok, values, 0.0)
 
         def cells(i, shift=0):
-            return pl.ds(i * GRID + 8 + shift, 16)
+            start = (i + 1) * GRID
+            return pl.ds((start if isinstance(i, int) else pl.multiple_of(start, 8)) + 8 + shift, 16)
 
         def around(ref, s, i):
             v = ref[s, cells(i), :]
-            x = [ref[s, cells(i + d), :] if 0 <= i + d < SPAN else None for d in (-1, 1)]
+            x = [ref[s, cells(i + d), :] for d in (-1, 1)]
             z = [ref[s, cells(i, d), :] for d in (-1, 1)]
             return [*x, *z, pltpu.roll(v, 1, 1), pltpu.roll(v, 127, 1), v]
 
         def weighted(w, values):
-            terms = [a * b for a, b in zip(w, values) if b is not None]
-            return functools.reduce(jnp.add, terms)
+            a, b, c, d, e, f, g = (x * y for x, y in zip(w, values))
+            return ((a + b) + (c + d)) + ((e + f) + g)
 
         for s in range(2):
             for i in range(SPAN):
                 now[s, cells(i), :] = strip(s, 1, i)
+                before[s, i] = strip(s, 0, i)
         shots = []
         for s in range(2):
             hit = here & (lane + y0 == at(sy, s)) & (depth + z0 == at(sz, s))
             shots.append((at(sx, s) - first - x0, jnp.where(hit, at(wavelet.at[s], 0), 0.0)))
-        for i in range(SPAN):
+        def first_pass(i, carry):
             of_forcing, of_step = ([prep[n + m, i] for n in range(7)] for m in (0, 7))
             for s, (x, source) in enumerate(shots):
                 values = around(now, s, i)
                 forced[s, cells(i), :] = weighted(of_forcing, values)
-                after = weighted(of_step, values) - strip(s, 0, i)
+                after = weighted(of_step, values) - before[s, i]
                 later[s, cells(i), :] = after + jnp.where(x == i, source, 0.0)
+            return carry
+
+        lax.fori_loop(0, SPAN, first_pass, 0, unroll=3)
 
         def each_plane(act, low=0, high=SPAN):
             for i in range(low, high):
@@ -458,16 +465,19 @@
                     target = out.at[:, :, plane_rows(x0 + i)]
                     act(pltpu.make_async_copy(planes.at[i, :, :, pl.ds(0, DEPTH)], target, sem.at[i]))
 
+        def second_pass(i, carry):
+            of_forcing, of_step = ([prep[n + m, i] for n in range(7)] for m in (0, 7))
+            for s in range(2):
+                gain = forced[s, cells(i), :]
+                more = weighted(of_step, around(forced, s, i)) + weighted(of_forcing, around(later, s, i))
+                for t, value in enumerate((gain, more)):
+                    spot = pl.ds(z0, 16)
+                    planes[i, s, t, spot, :] = fields[i, s, t, spot, :] + pltpu.roll(value, wrapped(y0), 1)
+            return carry
+
         part = SPAN // 3
         for low in range(0, SPAN, part):
-            for i in range(low, low + part):
-                of_forcing, of_step = ([prep[n + m, i] for n in range(7)] for m in (0, 7))
-                for s in range(2):
-                    gain = forced[s, cells(i), :]
-                    more = weighted(of_step, around(forced, s, i)) + weighted(of_forcing, around(later, s, i))
-                    for t, value in enumerate((gain, more)):
-                        spot = pl.ds(z0, 16)
-                        planes[i, s, t, spot, :] = fields[i, s, t, spot, :] + pltpu.roll(value, wrapped(y0), 1)
+            lax.fori_loop(low, low + part, second_pass, 0, unroll=2)
             each_plane(lambda copy: copy.start(), low, low + part)
         each_plane(lambda copy: copy.wait())
 
@@ -567,7 +577,9 @@
         [
             vmem(ROWS + 8, 128),
             vmem(SPAN, 2, 2, DEPTH + 8, 128),
-            *[vmem(2, SPAN * GRID + 8, 128)] * 3,
+            vmem(2, (SPAN + 2) * GRID + 8, 128),
+            vmem(2, SPAN, 16, 128),
+            *[vmem(2, (SPAN + 2) * GRID + 8, 128)] * 2,
             dma(SPAN),
         ],
         input_output_aliases={len(operands) - 1: 0},

time: 31.1 us -> 32.1 us (1.032)
  the two profiles are of different devices: /device:TPU:52 before, /device:TPU:59 now
where the time goes in v6:
time: 32.1 us; the launch traced here: 31.8 us
  starting transfers between devices  14 us (44%)
  waiting for transfers between devices  10 us (31%)
  Pallas kernels  7.36 us (23%)
  between operations  0.35 us (1%)
    ppermute x9, waiting for transfers between devices, along_rows(): return lax.ppermute(value, ('probe', 'gx'), every)  7.76 us
    ppermute x3, starting transfers between devices, swap(): lax.ppermute(value, ('probe', 'gx'), [(row * slabs + a, row * slabs + b)...  7.44 us
    pallas_call x6, Pallas kernels, call(): made(*map(pltpu.with_memory_space_constraint, args, spaces))  7.36 us
    ppermute x9, starting transfers between devices, along_rows(): return lax.ppermute(value, ('probe', 'gx'), every)  6.61 us
    ppermute x3, waiting for transfers between devices, swap(): lax.ppermute(value, ('probe', 'gx'), [(row * slabs + a, row * slabs + b)...  2.25 us
  transfers between devices with their start and end apart: 12, of which 2 were waited for; matrix products, arithmetic and copies ran while one was open for 0% of the time, Pallas kernels for 11%

profile of v6, /device:TPU:59, one launch (start us, length us, event | category | flops | bytes accessed | tf_op | source)
XLA Modules:
  0.0 31.8 jit_solution(10742646740809597026)
XLA Ops:
  0.0 1.1 %edges.1 = (f32[3,3,32,128]{3,2,1,0:T(8,128)S(1)}, f32[3,3,32,128]{3,2,1,0:T(8,128)S(1)}, f32[3,3,32,128]{3,2,1,0:T(8,128)S(1)}) custom-call(f32[2,2,24,32,128]{4,3,2,1,0:T(8,128)} %bitcast.10, f32[24,32,128]{2,1,0:T(8,128)} %stiff.1, f32[24,32,128]{2,1,0:T(8,128)} %buoy.1), custom_call_target="tpu_custom_call" | custom-call | tf_op jit(solution)/shard_map/edges/pallas_call | solution.py:512
  1.2 0.0 copy-start.1
  1.2 0.0 copy-start.2
  1.2 0.0 copy-start.3
  1.2 0.0 copy-start.4
  1.2 0.0 copy-start.5
  1.2 0.0 copy-start.9
  1.3 2.5 %collective-permute-start.1 = (f32[288,128]{1,0:T(8,128)S(1)}, f32[288,128]{1,0:T(8,128)S(1)}, u32[]{:S(2)}, u32[]{:S(2)}) collective-permute-start(f32[288,128]{1,0:T(8,128)S(1)} %bitcast.24), channel_id=1, source_target_pairs={{1,2},{2,1},{4,5},{5,4},{6,7},{7,6},{8,9},{9,8},{10,11},{11,10},{1... | collective-permute-start | bytes 442376 | tf_op jit(solution)/shard_map/ppermute | solution.py:520
  3.8 4.3 %collective-permute-start = (f32[288,128]{1,0:T(8,128)S(1)}, f32[288,128]{1,0:T(8,128)S(1)}, u32[]{:S(2)}, u32[]{:S(2)}) collective-permute-start(f32[288,128]{1,0:T(8,128)S(1)} %bitcast.23), channel_id=1, source_target_pairs={{0,1},{1,0},{3,4},{4,3},{5,6},{6,5},{7,8},{8,7},{9,10},{10,9},{11,... | collective-permute-start | bytes 442376 | tf_op jit(solution)/shard_map/ppermute | solution.py:520
  8.0 0.7 %collective-permute-start.2 = (f32[288,128]{1,0:T(8,128)S(1)}, f32[288,128]{1,0:T(8,128)S(1)}, u32[]{:S(2)}, u32[]{:S(2)}) collective-permute-start(f32[288,128]{1,0:T(8,128)S(1)} %bitcast.22), channel_id=1, source_target_pairs={{2,3},{3,2}} | collective-permute-start | bytes 442376 | tf_op jit(solution)/shard_map/ppermute | solution.py:520
  8.7 2.2 %collective-permute-done.swap_b.refs_10_ = f32[288,128]{1,0:T(8,128)S(1)} collective-permute-done((f32[288,128]{1,0:T(8,128)S(1)}, f32[288,128]{1,0:T(8,128)S(1)}, u32[]{:S(2)}, u32[]{:S(2)}) %collective-permute-start) | collective-permute-done | bytes 147488 | tf_op jit(solution)/shard_map/ppermute | solution.py:520
  11.0 0.7 %collective-permute-start.3 = (f32[240,128]{1,0:T(8,128)S(1)}, f32[240,128]{1,0:T(8,128)S(1)}, u32[]{:S(2)}, u32[]{:S(2)}) collective-permute-start(f32[240,128]{1,0:T(8,128)S(1)} %get-tuple-element.26), channel_id=1, source_target_pairs={{0,32},{1,33},{2,34},{3,35},{4,36},{5,37},{6,38},{7,39},{8,40},{9,... | collective-permute-start | bytes 368648 | tf_op jit(solution)/shard_map/ppermute | solution.py:516
  11.7 0.7 %collective-permute-start.4 = (f32[192,128]{1,0:T(8,128)S(1)}, f32[192,128]{1,0:T(8,128)S(1)}, u32[]{:S(2)}, u32[]{:S(2)}) collective-permute-start(f32[192,128]{1,0:T(8,128)S(1)} %get-tuple-element.27), channel_id=1, source_target_pairs={{0,64},{1,65},{2,66},{3,67},{4,68},{5,69},{6,70},{7,71},{8,72},{9,... | collective-permute-start | bytes 294920 | tf_op jit(solution)/shard_map/ppermute | solution.py:516
  12.4 0.7 %collective-permute-start.5 = (f32[144,128]{1,0:T(8,128)S(1)}, f32[144,128]{1,0:T(8,128)S(1)}, u32[]{:S(2)}, u32[]{:S(2)}) collective-permute-start(f32[144,128]{1,0:T(8,128)S(1)} %get-tuple-element.28), channel_id=1, source_target_pairs={{0,192},{1,193},{2,194},{3,195},{4,196},{5,197},{6,198},{7,199},{8... | collective-permute-start | bytes 221192 | tf_op jit(solution)/shard_map/ppermute | solution.py:516
  13.1 0.7 %collective-permute-start.6 = (f32[96,128]{1,0:T(8,128)S(1)}, f32[96,128]{1,0:T(8,128)S(1)}, u32[]{:S(2)}, u32[]{:S(2)}) collective-permute-start(f32[96,128]{1,0:T(8,128)S(1)} %get-tuple-element.29), channel_id=1, source_target_pairs={{0,256},{1,257},{2,258},{3,259},{4,260},{5,261},{6,262},{7,263},{8... | collective-permute-start | bytes 147464 | tf_op jit(solution)/shard_map/ppermute | solution.py:516
  13.7 0.7 %collective-permute-start.7 = (f32[48,128]{1,0:T(8,128)S(1)}, f32[48,128]{1,0:T(8,128)S(1)}, u32[]{:S(2)}, u32[]{:S(2)}) collective-permute-start(f32[48,128]{1,0:T(8,128)S(1)} %get-tuple-element.30), channel_id=1, source_target_pairs={{0,416},{1,417},{2,418},{3,419},{4,420},{5,421},{6,422},{7,423},{8... | collective-permute-start | bytes 73736 | tf_op jit(solution)/shard_map/ppermute | solution.py:516
  14.5 0.1 march_first.1
  14.7 1.3 %collective-permute-start.8 = (f32[48,128]{1,0:T(8,128)S(1)}, f32[48,128]{1,0:T(8,128)S(1)}, u32[]{:S(2)}, u32[]{:S(2)}) collective-permute-start(f32[48,128]{1,0:T(8,128)S(1)} %get-tuple-element.32), channel_id=1, source_target_pairs={{32,288},{33,289},{34,290},{35,291},{36,292},{37,293},{38,294},{39... | collective-permute-start | bytes 73736 | tf_op jit(solution)/shard_map/ppermute | solution.py:516
  16.0 0.7 %collective-permute-start.9 = (f32[48,128]{1,0:T(8,128)S(1)}, f32[48,128]{1,0:T(8,128)S(1)}, u32[]{:S(2)}, u32[]{:S(2)}) collective-permute-start(f32[48,128]{1,0:T(8,128)S(1)} %get-tuple-element.33), channel_id=1, source_target_pairs={{32,96},{33,97},{34,98},{35,99},{36,100},{37,101},{38,102},{39,103... | collective-permute-start | bytes 73736 | tf_op jit(solution)/shard_map/ppermute | solution.py:516
  16.6 0.7 %collective-permute-start.10 = (f32[48,128]{1,0:T(8,128)S(1)}, f32[48,128]{1,0:T(8,128)S(1)}, u32[]{:S(2)}, u32[]{:S(2)}) collective-permute-start(f32[48,128]{1,0:T(8,128)S(1)} %get-tuple-element.34), channel_id=1, source_target_pairs={{32,224},{33,225},{34,226},{35,227},{36,228},{37,229},{38,230},{39... | collective-permute-start | bytes 73736 | tf_op jit(solution)/shard_map/ppermute | solution.py:516
  17.3 0.7 %collective-permute-start.11 = (f32[48,128]{1,0:T(8,128)S(1)}, f32[48,128]{1,0:T(8,128)S(1)}, u32[]{:S(2)}, u32[]{:S(2)}) collective-permute-start(f32[48,128]{1,0:T(8,128)S(1)} %get-tuple-element.35.refs_18_), channel_id=1, source_target_pairs={{32,160},{33,161},{34,162},{35,163},{36,164},{37,165},{38,166},{39... | collective-permute-start | bytes 73736 | tf_op jit(solution)/shard_map/ppermute | solution.py:516
  18.0 3.4 %march_rest.1 = (f32[2,2,768,128]{3,2,1,0:T(8,128)}, f32[14,12,16,128]{3,2,1,0:T(8,128)S(1)}, f32[12,2,2,40,128]{4,3,2,1,0:T(8,128)S(1)}) custom-call(s32[15]{0:T(128)S(1)} %copy-done.6, s32[15]{0:T(128)S(1)} %copy-done.7, s32[15]{0:T(128)S(1)} %copy-done.8, s32[2]{0:T(128)S(1)} %copy-done.9, ...), custom_call_target="tpu_custom_call", output_to_operand_aliasing={{0}: (15, {}), {1}: (16, {}), {2}: (17, {})} | custom-call | tf_op jit(solution)/shard_map/march_rest/pallas_call | solution.py:512
  21.4 7.7 %collective-permute-done.8.refs_5_ = f32[48,128]{1,0:T(8,128)S(1)} collective-permute-done((f32[48,128]{1,0:T(8,128)S(1)}, f32[48,128]{1,0:T(8,128)S(1)}, u32[]{:S(2)}, u32[]{:S(2)}) %collective-permute-start.8) | collective-permute-done | bytes 24608 | tf_op jit(solution)/shard_map/ppermute | solution.py:516
  29.1 2.7 %born.1 = f32[2,2,768,128]{3,2,1,0:T(8,128)} custom-call(s32[15]{0:T(128)S(1)} %copy-done.6, s32[15]{0:T(128)S(1)} %copy-done.7, s32[15]{0:T(128)S(1)} %copy-done.8, s32[2]{0:T(128)S(1)} %copy-done.9, s32[2]{0:T(128)S(1)} %copy-done.10, s32[2]{0:T(128)S(1)} %copy-done.11, f32[2,2]{1,0:T(2,128)S(1)} %copy-done.5, ...), custom_call_target="tpu_custom_call", output_to_operand_aliasing={{}: (18, {})} | custom-call | tf_op jit(solution)/shard_map/born/pallas_call | solution.py:512
  (30 shorter events, 0.1 us)
Async XLA Ops:
  0.0 11.0 %copy-start = (f32[1,2,2,24,32,128]{5,4,3,2,1,0:T(8,128)S(1)}, f32[1,2,2,24,32,128]{5,4,3,2,1,0:T(8,128)}, u32[]{:S(2)}) copy-start(f32[1,2,2,24,32,128]{5,4,3,2,1,0:T(8,128)} %param.12) | copy-start | bytes 4718596
  0.0 11.0 %copy-start.8 = (s32[15]{0:T(128)S(1)}, s32[15]{0:T(128)}, u32[]{:S(2)}) copy-start(s32[15]{0:T(128)} %yb.3) | copy-start | bytes 184
  0.0 11.0 %copy-start.7 = (s32[15]{0:T(128)S(1)}, s32[15]{0:T(128)}, u32[]{:S(2)}) copy-start(s32[15]{0:T(128)} %zb.3) | copy-start | bytes 184
  0.0 11.0 %copy-start.6 = (s32[15]{0:T(128)S(1)}, s32[15]{0:T(128)}, u32[]{:S(2)}) copy-start(s32[15]{0:T(128)} %xb.3) | copy-start | bytes 184
  1.2 13.2 %copy-start.1 = (f32[24,32,128]{2,1,0:T(8,128)S(1)}, f32[24,32,128]{2,1,0:T(8,128)}, u32[]{:S(2)}) copy-start(f32[24,32,128]{2,1,0:T(8,128)} %stiff.1) | copy-start | bytes 1179652
  1.2 13.2 %copy-start.2 = (f32[24,32,128]{2,1,0:T(8,128)S(1)}, f32[24,32,128]{2,1,0:T(8,128)}, u32[]{:S(2)}) copy-start(f32[24,32,128]{2,1,0:T(8,128)} %buoy.1) | copy-start | bytes 1179652
  1.2 13.2 %copy-start.3 = (f32[15,8,8,8]{0,3,2,1:T(8,128)S(1)}, f32[15,8,8,8]{0,3,2,1:T(8,128)}, u32[]{:S(2)}) copy-start(f32[15,8,8,8]{0,3,2,1:T(8,128)} %param.15) | copy-start | bytes 92164
  1.2 13.2 %copy-start.4 = (f32[15,8,8,8]{0,3,2,1:T(8,128)S(1)}, f32[15,8,8,8]{0,3,2,1:T(8,128)}, u32[]{:S(2)}) copy-start(f32[15,8,8,8]{0,3,2,1:T(8,128)} %param.16) | copy-start | bytes 92164
  1.2 13.2 %copy-start.5 = (f32[2,2]{1,0:T(2,128)S(1)}, f32[2,2]{1,0:T(2,128)}, u32[]{:S(2)}) copy-start(f32[2,2]{1,0:T(2,128)} %wavelet.1) | copy-start | bytes 52
  1.2 13.2 %copy-start.9 = (s32[2]{0:T(128)S(1)}, s32[2]{0:T(128)}, u32[]{:S(2)}) copy-start(s32[2]{0:T(128)} %sx.1) | copy-start | bytes 28
  1.2 13.2 %copy-start.10 = (s32[2]{0:T(128)S(1)}, s32[2]{0:T(128)}, u32[]{:S(2)}) copy-start(s32[2]{0:T(128)} %sz.1) | copy-start | bytes 28
  1.2 13.2 %copy-start.11 = (s32[2]{0:T(128)S(1)}, s32[2]{0:T(128)}, u32[]{:S(2)}) copy-start(s32[2]{0:T(128)} %sy.1) | copy-start | bytes 28
  1.3 7.5 %collective-permute-start.1 = (f32[288,128]{1,0:T(8,128)S(1)}, f32[288,128]{1,0:T(8,128)S(1)}, u32[]{:S(2)}, u32[]{:S(2)}) collective-permute-start(f32[288,128]{1,0:T(8,128)S(1)} %bitcast.24), channel_id=1, source_target_pairs={{1,2},{2,1},{4,5},{5,4},{6,7},{7,6},{8,9},{9,8},{10,11},{11,10},{1... | collective-permute-start | bytes 442376 | tf_op jit(solution)/shard_map/ppermute | solution.py:520
  3.8 7.2 %collective-permute-start = (f32[288,128]{1,0:T(8,128)S(1)}, f32[288,128]{1,0:T(8,128)S(1)}, u32[]{:S(2)}, u32[]{:S(2)}) collective-permute-start(f32[288,128]{1,0:T(8,128)S(1)} %bitcast.23), channel_id=1, source_target_pairs={{0,1},{1,0},{3,4},{4,3},{5,6},{6,5},{7,8},{8,7},{9,10},{10,9},{11,... | collective-permute-start | bytes 442376 | tf_op jit(solution)/shard_map/ppermute | solution.py:520
  8.0 2.9 %collective-permute-start.2 = (f32[288,128]{1,0:T(8,128)S(1)}, f32[288,128]{1,0:T(8,128)S(1)}, u32[]{:S(2)}, u32[]{:S(2)}) collective-permute-start(f32[288,128]{1,0:T(8,128)S(1)} %bitcast.22), channel_id=1, source_target_pairs={{2,3},{3,2}} | collective-permute-start | bytes 442376 | tf_op jit(solution)/shard_map/ppermute | solution.py:520
  11.0 3.6 %collective-permute-start.3 = (f32[240,128]{1,0:T(8,128)S(1)}, f32[240,128]{1,0:T(8,128)S(1)}, u32[]{:S(2)}, u32[]{:S(2)}) collective-permute-start(f32[240,128]{1,0:T(8,128)S(1)} %get-tuple-element.26), channel_id=1, source_target_pairs={{0,32},{1,33},{2,34},{3,35},{4,36},{5,37},{6,38},{7,39},{8,40},{9,... | collective-permute-start | bytes 368648 | tf_op jit(solution)/shard_map/ppermute | solution.py:516
  11.7 2.9 %collective-permute-start.4 = (f32[192,128]{1,0:T(8,128)S(1)}, f32[192,128]{1,0:T(8,128)S(1)}, u32[]{:S(2)}, u32[]{:S(2)}) collective-permute-start(f32[192,128]{1,0:T(8,128)S(1)} %get-tuple-element.27), channel_id=1, source_target_pairs={{0,64},{1,65},{2,66},{3,67},{4,68},{5,69},{6,70},{7,71},{8,72},{9,... | collective-permute-start | bytes 294920 | tf_op jit(solution)/shard_map/ppermute | solution.py:516
  12.4 2.2 %collective-permute-start.5 = (f32[144,128]{1,0:T(8,128)S(1)}, f32[144,128]{1,0:T(8,128)S(1)}, u32[]{:S(2)}, u32[]{:S(2)}) collective-permute-start(f32[144,128]{1,0:T(8,128)S(1)} %get-tuple-element.28), channel_id=1, source_target_pairs={{0,192},{1,193},{2,194},{3,195},{4,196},{5,197},{6,198},{7,199},{8... | collective-permute-start | bytes 221192 | tf_op jit(solution)/shard_map/ppermute | solution.py:516
  13.1 1.5 %collective-permute-start.6 = (f32[96,128]{1,0:T(8,128)S(1)}, f32[96,128]{1,0:T(8,128)S(1)}, u32[]{:S(2)}, u32[]{:S(2)}) collective-permute-start(f32[96,128]{1,0:T(8,128)S(1)} %get-tuple-element.29), channel_id=1, source_target_pairs={{0,256},{1,257},{2,258},{3,259},{4,260},{5,261},{6,262},{7,263},{8... | collective-permute-start | bytes 147464 | tf_op jit(solution)/shard_map/ppermute | solution.py:516
  13.7 7.6 %collective-permute-start.7 = (f32[48,128]{1,0:T(8,128)S(1)}, f32[48,128]{1,0:T(8,128)S(1)}, u32[]{:S(2)}, u32[]{:S(2)}) collective-permute-start(f32[48,128]{1,0:T(8,128)S(1)} %get-tuple-element.30), channel_id=1, source_target_pairs={{0,416},{1,417},{2,418},{3,419},{4,420},{5,421},{6,422},{7,423},{8... | collective-permute-start | bytes 73736 | tf_op jit(solution)/shard_map/ppermute | solution.py:516
  14.7 14.5 %collective-permute-start.8 = (f32[48,128]{1,0:T(8,128)S(1)}, f32[48,128]{1,0:T(8,128)S(1)}, u32[]{:S(2)}, u32[]{:S(2)}) collective-permute-start(f32[48,128]{1,0:T(8,128)S(1)} %get-tuple-element.32), channel_id=1, source_target_pairs={{32,288},{33,289},{34,290},{35,291},{36,292},{37,293},{38,294},{39... | collective-permute-start | bytes 73736 | tf_op jit(solution)/shard_map/ppermute | solution.py:516
  16.0 13.2 %collective-permute-start.9 = (f32[48,128]{1,0:T(8,128)S(1)}, f32[48,128]{1,0:T(8,128)S(1)}, u32[]{:S(2)}, u32[]{:S(2)}) collective-permute-start(f32[48,128]{1,0:T(8,128)S(1)} %get-tuple-element.33), channel_id=1, source_target_pairs={{32,96},{33,97},{34,98},{35,99},{36,100},{37,101},{38,102},{39,103... | collective-permute-start | bytes 73736 | tf_op jit(solution)/shard_map/ppermute | solution.py:516
  16.6 12.5 %collective-permute-start.10 = (f32[48,128]{1,0:T(8,128)S(1)}, f32[48,128]{1,0:T(8,128)S(1)}, u32[]{:S(2)}, u32[]{:S(2)}) collective-permute-start(f32[48,128]{1,0:T(8,128)S(1)} %get-tuple-element.34), channel_id=1, source_target_pairs={{32,224},{33,225},{34,226},{35,227},{36,228},{37,229},{38,230},{39... | collective-permute-start | bytes 73736 | tf_op jit(solution)/shard_map/ppermute | solution.py:516
  17.3 11.8 %collective-permute-start.11 = (f32[48,128]{1,0:T(8,128)S(1)}, f32[48,128]{1,0:T(8,128)S(1)}, u32[]{:S(2)}, u32[]{:S(2)}) collective-permute-start(f32[48,128]{1,0:T(8,128)S(1)} %get-tuple-element.35.refs_18_), channel_id=1, source_target_pairs={{32,160},{33,161},{34,162},{35,163},{36,164},{37,165},{38,166},{39... | collective-permute-start | bytes 73736 | tf_op jit(solution)/shard_map/ppermute | solution.py:516
